TPU v7x, 32 devices: a whole 2x2x4 slice. The times are simulated.
32 devices in a mesh: patch: 2 (over x), epoch: 8 (over z, y), tile: 2 (over core).
Axes of the slice: x: 2, y: 2, z: 4, core: 2. Of those that a mesh axis runs over, the one named last changes fastest.
Arguments:
- template: float32 [1024, 1024], P(('patch', 'tile'), 'epoch'), parts along dimension 0, may hold values from -6 to 6
- science: float32 [16, 512, 1024], P(('patch', 'epoch'), 'tile'), parts along dimension 0, may hold values from -6 to 6, as said below
- flags: int32 [16, 512, 1024], P(('patch', 'epoch'), 'tile'), parts along dimension 0, may hold values 0 or 1
- stamp_rows: int32 [16, 32], P(('patch', 'epoch'), 'tile'), parts along dimension 0, may hold values from 0 to 224
- stamp_cols: int32 [16, 32], P(('patch', 'epoch'), 'tile'), parts along dimension 0, may hold values from 0 to 992
Outputs:
- detection: float32 [16, 512, 1024], P(('patch', 'epoch'), 'tile'), parts along dimension 0
- coefficients: float32 [24], P('patch'), parts along dimension 0
There are 2 independent parts, one for each index of `patch`. A program takes and returns all parts, laid end to end along the dimension named above; each array names one. Nothing has to cross between parts.
Inputs may be any that keep to these rules, and one draw needn't show every extreme that they name: `stamp_rows`: stamps lie inside their tile. `stamp_cols`: stamps lie inside the image. `science`: each exposure is the template matched by some kernel, plus noise.
All inputs are finite; a program needn't handle non-finite values. No bound on the sum of `flags` on one device may be relied on, other than what follows from the above.
Results may differ from a plain program's by a relative error of at most 0.0003.
Values sent between devices are 32-bit elements; how exact they have to be, the bound alone decides.
No kernel may reach another device: no remote copies, remote signals or barrier semaphores. Data moves between devices by JAX's collectives and lax.ppermute only.
A program may use at most 128 MiB of HBM per device.

v0:
```python
import jax
import jax.numpy as jnp
from jax import lax
from jax.sharding import PartitionSpec as P

STAMP = 32


def extended_2(block, sides, width):
    for axis, dim in sides:
        count = lax.axis_size(axis)
        forward = [(i, i + 1) for i in range(count - 1)]
        backward = [(target, source) for source, target in forward]
        low = lax.ppermute(
            lax.slice_in_dim(block, block.shape[dim] - width, None, axis=dim), axis, forward
        )
        high = lax.ppermute(lax.slice_in_dim(block, 0, width, axis=dim), axis, backward)
        block = jnp.concatenate([low, block, high], axis=dim)
    return block


def basis_profiles():
    offsets = jnp.arange(15, dtype=jnp.float32) - 7.0
    row_list = []
    col_list = []
    for sigma in (1.0, 2.0, 3.5):
        gauss = jnp.exp(-offsets * offsets / (2.0 * sigma * sigma))
        gauss = gauss / jnp.sum(gauss)
        for power_r, power_c in ((0, 0), (1, 0), (0, 1), (1, 1)):
            row_list.append(gauss * (offsets / 7.0) if power_r else gauss)
            col_list.append(gauss * (offsets / 7.0) if power_c else gauss)
    return (jnp.stack(row_list), jnp.stack(col_list))


def psf_profile():
    offsets = jnp.arange(15, dtype=jnp.float32) - 7.0
    gauss = jnp.exp(-offsets * offsets / 4.5)
    return (gauss / jnp.sum(gauss))[None, :]


def conv_rows(extended, profile):
    count = extended.shape[0] - 14
    total = jnp.zeros((profile.shape[0], count, extended.shape[1]), jnp.float32)
    for shift in range(15):
        total = total + profile[:, shift, None, None] * extended[None, shift : shift + count, :]
    return total


def conv_cols(extended, profile):
    count = extended.shape[2] - 14
    total = jnp.zeros((profile.shape[0], extended.shape[1], count), jnp.float32)
    for shift in range(15):
        total = total + profile[:, shift, None, None] * extended[:, :, shift : shift + count]
    return total


def local(template, science, flags, stamp_rows, stamp_cols):
    row_prof, col_prof = basis_profiles()
    full_rows = lax.all_gather(template, "epoch", axis=1, tiled=True)
    taller = extended_2(full_rows, (("tile", 0),), 7)
    widened = jnp.pad(taller, ((0, 0), (7, 7)))
    images = conv_cols(conv_rows(widened, row_prof), col_prof)
    own_science = science[0]
    rows_here = own_science.shape[0]
    cols_here = own_science.shape[1]
    pos_r = jnp.arange(rows_here)
    pos_c = jnp.arange(cols_here)
    top = stamp_rows[0]
    left = stamp_cols[0]
    row_ind = ((pos_r[None, :] >= top[:, None]) & (pos_r[None, :] < top[:, None] + STAMP)).astype(
        jnp.float32
    )
    col_ind = ((pos_c[None, :] >= left[:, None]) & (pos_c[None, :] < left[:, None] + STAMP)).astype(
        jnp.float32
    )
    weight = jnp.dot(row_ind.T, col_ind, precision=lax.Precision.HIGHEST)
    good = jnp.where(flags[0] == 0, weight, 0.0)
    normal_part = jnp.einsum(
        "kpq,lpq->kl", images * good[None], images, precision=lax.Precision.HIGHEST
    )
    rhs_part = jnp.einsum("kpq,pq->k", images, good * own_science, precision=lax.Precision.HIGHEST)
    normal, rhs = lax.psum((normal_part, rhs_part), ("epoch", "tile"))
    basis_count = normal.shape[0]
    system = normal + 0.05 * jnp.trace(normal) / basis_count * jnp.eye(
        basis_count, dtype=jnp.float32
    )
    factor = jnp.linalg.cholesky(system)
    middle = lax.linalg.triangular_solve(factor, rhs[:, None], left_side=True, lower=True)
    solved = lax.linalg.triangular_solve(
        factor, middle, left_side=True, lower=True, transpose_a=True
    )
    coefficients = solved[:, 0]
    model = jnp.einsum("k,kpq->pq", coefficients, images, precision=lax.Precision.HIGHEST)
    difference = own_science - model
    taller_diff = extended_2(difference, (("tile", 0),), 7)
    psf = psf_profile()
    detection = conv_cols(conv_rows(jnp.pad(taller_diff, ((0, 0), (7, 7))), psf), psf)
    return (detection, coefficients)


def solution(mesh):
    return jax.shard_map(
        local,
        mesh=mesh,
        in_specs=(
            P(("patch", "tile"), "epoch"),
            P(("patch", "epoch"), "tile", None),
            P(("patch", "epoch"), "tile", None),
            P(("patch", "epoch"), "tile"),
            P(("patch", "epoch"), "tile"),
        ),
        out_specs=(P(("patch", "epoch"), "tile", None), P("patch")),
        check_vma=False,
    )
```

profile of v0, /device:TPU:0, one launch (start us, length us, event | category | flops | bytes accessed | tf_op | source)
XLA Modules:
  0.0 324.9 jit_solution(9410804981818719330)
XLA Ops:
  7.2 0.7 all-gather.2.cloned.1.call-update
  9.1 0.7 exponential_reduce_fusion
  11.2 0.7 exponential_divide_fusion
  13.4 1.7 convolution_select_fusion
  15.2 37.1 %all-gather.2.cloned.1.call-done = f32[256,1024]{1,0:T(8,128)} async-done(((f32[256,128]{1,0:T(8,128)}), f32[256,1024]{1,0:T(8,128)}) %all-gather.2.cloned.1.call-update) | async-done | bytes 1048592 | tf_op jit(solution)/shard_map/all_gather | solution.py:59
  52.3 0.8 fusion.74
  53.1 1.3 collective-permute-start
  54.4 1.3 collective-permute-start.1
  56.4 1.1 collective-permute-done.1
  57.5 1.6 select_maximum_fusion.2
  59.2 2.5 fusion.72
  61.6 20.9 %multiply_add_fusion = f32[12,256,1038]{2,0,1:T(8,128)} fusion(f32[256,1038]{1,0:T(8,128)} %get-tuple-element.18, f32[12]{0:T(128)S(1)} %get-tuple-element.54, f32[256,1038]{1,0:T(8,128)S(1)} %get-tuple-element.5, f32[12]{0:T(128)S(1)} %get-tuple-element.55, f32[256,1038]{1,0:T(8,128)S(1)} %get-tuple-element.6, f32[12]{0:T(128)S(1)} %get-tuple-element.56, ...), kind=kLoop, calls=%fused_computation.2 | loop fusion | flops 92473344 | bytes 28699344 | tf_op jit(solution)/shard_map/add | solution.py:45
  82.6 105.5 %fusion.2 = f32[12,256,1024]{2,0,1:T(8,128)} fusion(f32[12,256,1038]{2,0,1:T(8,128)} %multiply_add_fusion, f32[12]{0:T(128)S(1)} %get-tuple-element.39, f32[12]{0:T(128)S(1)} %get-tuple-element.40, f32[12]{0:T(128)S(1)} %get-tuple-element.41, f32[12]{0:T(128)S(1)} %get-tuple-element.42, f32[12]{0:T(128)S(1)} %get-tuple-element.43, ...), kind=kLoop, calls=%fused_computation.4 | loop fusion | flops 91226112 | bytes 201327312 | tf_op jit(solution)/shard_map/add | solution.py:53
  188.1 29.8 %fusion.33 = f32[12,12]{1,0:T(8,128)S(1)} fusion(f32[12,256,1024]{2,0,1:T(8,128)} %fusion.2, f32[256,1024]{1,0:T(8,128)S(1)} %convolution_select_fusion), kind=kOutput, calls=%fused_computation.71 | convolution fusion | flops 456130560 | bytes 13632064 | tf_op jit(solution)/shard_map/kpq,lpq->kl/dot_general | solution.py:78
  217.9 20.3 %convolution_bitcast_fusion.1 = f32[12]{0:T(128)S(1)} fusion(f32[12,256,1024]{2,0,1:T(8,128)S(1)} %copy-done, f32[256,1024,1]{1,0,2:T(8,128)S(1)} %fusion.50), kind=kOutput, calls=%fused_computation.73 | convolution fusion | flops 37748736 | bytes 13631536 | tf_op jit(solution)/shard_map/kpq,pq->k/dot_general | solution.py:81
  238.1 32.4 %all-reduce.2 = (f32[12,12]{1,0:T(8,128)S(1)}, f32[12]{0:T(128)S(1)}) all-reduce(f32[12,12]{1,0:T(8,128)S(1)} %fusion.33, f32[12]{0:T(128)S(1)} %convolution_bitcast_fusion.1), channel_id=1, replica_groups=mesh['patch'=2,'epoch'=8,'tile'=2] {'epoch','tile'}, use_global_device_ids=true, to_apply=%region_4.5 | all-reduce | flops 156 | bytes 1248 | tf_op jit(solution)/shard_map/psum | solution.py:82
  271.9 1.1 cholesky.17
  274.4 0.9 custom-call.8
  275.6 11.7 %fusion.69 = f32[1,256,1024]{2,0,1:T(1,128)S(1)} fusion(f32[12,256,1024]{2,0,1:T(8,128)} %fusion.2, f32[1,12]{1,0:T(1,128)S(1)} %fusion.59), kind=kOutput, calls=%fused_computation.171 | convolution fusion | flops 37748736 | bytes 13631536 | tf_op jit(solution)/shard_map/k,kpq->pq/dot_general | solution.py:93
  287.7 1.3 collective-permute-start.2
  289.0 1.3 collective-permute-start.3
  290.9 1.1 collective-permute-done.3
  292.5 11.5 %fusion.19 = f32[1,256,1038]{2,1,0:T(8,128)S(1)} fusion(f32[270,1038]{1,0:T(8,128)S(1)} %select_maximum_fusion, f32[]{:T(128)} %bitcast.60, f32[]{:T(128)} %bitcast.59, f32[]{:T(128)} %bitcast.58, f32[]{:T(128)} %bitcast.57, f32[]{:T(128)} %bitcast.56, f32[]{:T(128)} %bitcast.55, f32[]{:T(128)} %bitcast.54, f32[]{:T(128)} %bitcast.53, f32[]{:T(128)} %bitcast.52, ...), kind=kLoop, calls=%fused_computation.43 | loop fusion | flops 7706112 | bytes 17006652 | tf_op jit(solution)/shard_map/add | solution.py:45
  304.0 14.0 %fusion.36 = f32[1,256,1024]{2,1,0:T(8,128)} fusion(f32[1,256,1038]{2,1,0:T(8,128)S(1)} %fusion.19, f32[]{:T(128)} %bitcast.60, f32[]{:T(128)} %bitcast.59, f32[]{:T(128)} %bitcast.58, f32[]{:T(128)} %bitcast.57, f32[]{:T(128)} %bitcast.56, f32[]{:T(128)} %bitcast.55, f32[]{:T(128)} %bitcast.54, f32[]{:T(128)} %bitcast.53, f32[]{:T(128)} %bitcast.52, ...), kind=kLoop, calls=%fused_computation.75 | loop fusion | flops 7602176 | bytes 16777276 | tf_op jit(solution)/shard_map/add | solution.py:53
  (36 shorter events, 8.7 us)
Async XLA Ops:
  7.2 45.2 %all-gather.2.cloned.1.call-start = ((), (), s32[]{:S(2)}) async-start(), calls=%async_computation | async-start | bytes 1179648 | tf_op jit(solution)/shard_map/all_gather | solution.py:59
  12.1 3.0 copy-start.1
  53.1 3.3 %collective-permute-start = (f32[7,1024]{1,0:T(8,128)S(1)}, f32[7,1024]{1,0:T(8,128)S(1)}, u32[]{:S(2)}, u32[]{:S(2)}) collective-permute-start(f32[7,1024]{1,0:T(8,128)S(1)} %get-tuple-element.21), channel_id=1, source_target_pairs={{0,1},{2,3},{4,5},{6,7},{8,9},{10,11},{12,13},{14,15},{16,17},{18,... | collective-permute-start | bytes 86024 | tf_op jit(solution)/shard_map/ppermute | solution.py:14
  54.4 3.1 collective-permute-start.1
  188.1 29.8 %copy-start = (f32[12,256,1024]{2,0,1:T(8,128)S(1)}, f32[12,256,1024]{2,0,1:T(8,128)}, u32[]{:S(2)}) copy-start(f32[12,256,1024]{2,0,1:T(8,128)} %fusion.2) | copy-start | bytes 37748740
  275.6 11.7 %copy-start.3 = (f32[1,12]{1,0:T(1,128)}, f32[1,12]{1,0:T(1,128)S(1)}, u32[]{:S(2)}) copy-start(f32[1,12]{1,0:T(1,128)S(1)} %fusion.59) | copy-start | bytes 148
  275.6 11.7 %copy-start.2 = (f32[1,256,1024]{2,1,0:T(8,128)S(1)}, f32[1,256,1024]{2,1,0:T(8,128)}, u32[]{:S(2)}) copy-start(f32[1,256,1024]{2,1,0:T(8,128)} %param.6) | copy-start | bytes 3145732
  287.7 3.2 collective-permute-start.2
  289.0 3.1 collective-permute-start.3
Sparse Core Ops, SparseCore 0:
  10.0 42.2 all-gather.1
where the time goes:
time: 326 us; the launch traced here: 325 us
  other arithmetic  164 us (50%)
  matrix products  63.7 us (20%)
  waiting for transfers between devices  40.1 us (12%)
  blocking collectives  32.4 us (10%)
  between operations  14.9 us (5%)
  starting transfers between devices  5.19 us (2%)
  local copies, waits for them, and re-layouts  4.25 us (1%)
    add x2, other arithmetic, conv_cols(): total + profile[:, shift, None, None] * extended[:, :, shift:shift + count]  120 us
    all_gather x1, waiting for transfers between devices, local(): full_rows = lax.all_gather(template, 'epoch', axis=1, tiled=True)  37.1 us
    psum x1, blocking collectives, local(): normal, rhs = lax.psum((normal_part, rhs_part), ('epoch', 'tile'))  32.4 us
    add x2, other arithmetic, conv_rows(): total + profile[:, shift, None, None] * extended[None, shift:shift + coun...  32.4 us
    dot_general x1, matrix products, local(): jnp.einsum('kpq,lpq->kl', images * good[None], images, precision=lax.Prec...  29.8 us
    dot_general x1, matrix products, local(): jnp.einsum('kpq,pq->k', images, good * own_science, precision=lax.Precisi...  20.3 us
    dot_general x1, matrix products, local(): jnp.einsum('k,kpq->pq', coefficients, images, precision=lax.Precision.HIG...  11.7 us
  transfers between devices with their start and end apart: 5, of which 3 were waited for; matrix products, arithmetic and copies ran while one was open for 3% of the time, Pallas kernels for 0%

commit v1 on v0

v1 whole, which is shorter than its diff:
```python
import functools

import jax
import jax.numpy as jnp
import numpy as np
from jax import lax
from jax.experimental import pallas as pl
from jax.experimental.pallas import tpu as pltpu
from jax.sharding import PartitionSpec as P

STAMP = 32
HALF = 7
TAPS = 15
SIGMAS = (1.0, 2.0, 3.5)
NB = 12
LANES = 128
HALO = 16
WIN = LANES + 2 * HALO
PATCH_ROWS = 48
F32 = jnp.float32
BF16 = jnp.bfloat16
LIMIT = 56 * 1024 * 1024


def split_np(a):
    a = np.asarray(a, np.float32)
    hi = a.astype(BF16)
    lo = (a - hi.astype(np.float32)).astype(BF16)
    return hi, lo


def profiles():
    offsets = np.arange(TAPS, dtype=np.float64) - HALF
    rows = []
    for sigma in SIGMAS:
        gauss = np.exp(-offsets * offsets / (2.0 * sigma * sigma))
        gauss = gauss / gauss.sum()
        rows += [gauss, gauss * offsets / HALF]
    return np.stack(rows)


def psf_profile():
    offsets = np.arange(TAPS, dtype=np.float64) - HALF
    gauss = np.exp(-offsets * offsets / 4.5)
    return gauss / gauss.sum()


def band(profile, size):
    out = np.zeros((size, size))
    for shift in range(TAPS):
        out += profile[shift] * np.eye(size, k=shift - HALF)
    return out


def three_bands(size):
    psf = band(psf_profile(), size)
    return [psf @ band(p, size) for p in profiles()], psf


def pick(matrix, rows, cols):
    cols = np.asarray(cols)
    ok = (cols >= 0) & (cols < matrix.shape[1])
    out = matrix[np.asarray(rows)[:, None], np.clip(cols, 0, matrix.shape[1] - 1)[None, :]]
    return np.where(ok[None, :], out, 0.0)


def starts():
    return (0, LANES, 2 * LANES)


def row_tables():
    size = 3 * LANES
    ops, psf = three_bands(size)

    def stack(ms):
        out = []
        for start in starts():
            rows = np.arange(LANES) + start
            cols = np.arange(WIN) + start - HALO
            hi, lo = split_np(np.concatenate([pick(m, rows, cols) for m in ms], axis=0))
            out.append(np.concatenate([hi, hi, lo], axis=1))
        return np.stack(out)

    return stack(ops), stack([psf])


def column_tables():
    size = 3 * LANES
    ops, psf = three_bands(size)

    def one(matrix, start):
        lane = np.arange(LANES)
        cols = np.concatenate([start + lane, np.where(lane < 64, start + LANES + lane, start - LANES + lane)])
        return pick(matrix, np.arange(LANES) + start, cols).T

    model = []
    for start in starts():
        per = []
        for s in range(3):
            both = np.concatenate([one(ops[2 * s], start), one(ops[2 * s + 1], start)], axis=1)
            per.append(np.stack(split_np(both)))
        model.append(np.stack(per))
    return np.stack(model), np.stack([np.stack(split_np(one(psf, start))) for start in starts()])


def stamp_table():
    prof = profiles()
    out = np.zeros((256, 6, LANES))
    for q in range(4):
        for c in range(STAMP):
            for v in range(TAPS):
                out[q * 64 + c + v, :, q * STAMP + c] = prof[:, v]
    return np.stack(split_np(out.reshape(256, 6 * LANES)))


def pair_list():
    return [(k, l) for k in range(NB) for l in range(k, NB)] + [(k, NB) for k in range(NB)]


def place_tables():
    pairs = pair_list()
    first = np.zeros((2, 96, LANES), np.float32)
    left = np.zeros((16, 192), np.float32)
    for p, (k, l) in enumerate(pairs):
        first[0, p, l] = 1.0
        left[k, p] = 1.0
        if l < NB and l != k:
            first[1, p, k] = 1.0
            left[l, 96 + p] = 1.0
    return first, left


def dot(a, b):
    return jnp.dot(a, b, preferred_element_type=F32)


def split(x):
    hi = x.astype(BF16)
    lo = (x - hi.astype(F32)).astype(BF16)
    return hi, lo


def stack3(x):
    hi, lo = split(x)
    return jnp.concatenate([hi, lo, hi], axis=0)


def params(**kw):
    return pltpu.CompilerParams(vmem_limit_bytes=LIMIT, **kw)


VMEM = functools.partial(pl.BlockSpec, memory_space=pltpu.VMEM)
SMEM = functools.partial(pl.BlockSpec, memory_space=pltpu.SMEM)


def lane_index(shape):
    return lax.broadcasted_iota(jnp.int32, shape, len(shape) - 1)


def science_kernel(n_tile, info, tops, lefts, sci, edge, flags, lrow, wcol, d0, wp, sp, sb, fb, mid):
    tile = info[0]
    rows, cols = sci.shape
    nblk = cols // LANES
    nrow = rows // LANES
    for m in range(nblk):
        piece = slice(m * LANES, (m + 1) * LANES)
        e = edge[:, piece]
        sb[m, 0:HALO, :] = jnp.where(tile == 0, 0.0, e)
        sb[m, HALO : HALO + rows, :] = sci[:, piece]
        sb[m, HALO + rows :, :] = jnp.where(tile == n_tile - 1, 0.0, e)
        fb[m] = jnp.where(flags[:, piece] == 0, 1.0, 0.0)
    for b in range(nrow):
        v = variant(tile, b, n_tile, nrow)
        left = lrow[v]
        for m in range(0, nblk, 2):
            x = jnp.concatenate(
                [sb[m, b * LANES : b * LANES + WIN, :], sb[m + 1, b * LANES : b * LANES + WIN, :]], axis=1
            )
            y = dot(left, stack3(x))
            mid[m, b * LANES : (b + 1) * LANES, :] = y[:, :LANES]
            mid[m + 1, b * LANES : (b + 1) * LANES, :] = y[:, LANES:]
    lane = lane_index((rows, LANES))
    for m in range(nblk):
        v = 0 if m == 0 else (2 if m == nblk - 1 else 1)
        rim = jnp.where(lane < 64, mid[min(m + 1, nblk - 1)], mid[max(m - 1, 0)])
        hi, lo = split(jnp.concatenate([mid[m], rim], axis=1))
        d0[:, m * LANES : (m + 1) * LANES] = dot(hi, wcol[v, 0]) + dot(lo, wcol[v, 0]) + dot(hi, wcol[v, 1])
    lane = lane_index((STAMP, LANES))
    for g in range(tops.shape[1] // 4):
        w = jnp.zeros((STAMP, LANES), F32)
        s = jnp.zeros((STAMP, LANES), F32)
        for q in range(4):
            top = tops[0, g * 4 + q]
            left = lefts[0, g * 4 + q]
            blk = left // LANES
            off = left - blk * LANES
            nxt = jnp.minimum(blk + 1, nblk - 1)
            shift = lax.rem(q * STAMP - off + LANES, LANES)
            near = lane < q * STAMP - off + LANES
            here = (lane >= q * STAMP) & (lane < (q + 1) * STAMP)

            def window(ref, first):
                a = pltpu.roll(ref[blk, pl.ds(first, STAMP), :], shift, 1)
                b = pltpu.roll(ref[nxt, pl.ds(first, STAMP), :], shift, 1)
                return jnp.where(near, a, b)

            w = jnp.where(here, window(fb, top), w)
            s = jnp.where(here, window(sb, top + HALO), s)
        wp[g * STAMP : (g + 1) * STAMP, :] = w
        sp[g * STAMP : (g + 1) * STAMP, :] = w * s


def variant(tile, b, n_tile, nrow):
    v = jnp.int32(1)
    if b == 0:
        v = jnp.where(tile == 0, 0, v)
    if b == nrow - 1:
        v = jnp.where(tile == n_tile - 1, 2, v)
    return v


def assemble(info, n_tile, blocks, t):
    tile = info[0]
    rows = blocks[0].shape[0] - HALO
    for m in (0, len(blocks) + 1):
        t[m] = jnp.zeros(t.shape[1:], F32)
    for slot, block in enumerate(blocks):
        at = info[1 + slot] + 1
        e = block[rows:, :]
        t[at, 0:HALO, :] = jnp.where(tile == 0, 0.0, e)
        t[at, HALO : HALO + rows, :] = block[0:rows, :]
        t[at, HALO + rows :, :] = jnp.where(tile == n_tile - 1, 0.0, e)


def stamp_kernel(n_tile, nblk, info, tops, lefts, *refs):
    blocks = refs[:nblk]
    wp, sp, mcol, first, leftm, system, t, y, images, sums = refs[nblk:]
    assemble(info, n_tile, blocks, t)
    groups = tops.shape[1] // 4
    lane = lane_index((PATCH_ROWS, LANES))
    prof = profiles()
    xs = []
    for g in range(groups):
        halves = []
        for pair in range(2):
            parts = []
            for h in range(2):
                j = g * 4 + pair * 2 + h
                start = lefts[0, j] + (LANES - HALF)
                blk = start // LANES
                off = start - blk * LANES
                shift = lax.rem(64 * h - off + LANES, LANES)
                rows = pl.ds(tops[0, j] + (HALO - HALF), PATCH_ROWS)
                a = pltpu.roll(t[blk, rows, :], shift, 1)
                b = pltpu.roll(t[blk + 1, rows, :], shift, 1)
                parts.append(jnp.where(lane < 64 * h - off + LANES, a, b))
            halves.append(jnp.where(lane < 64, parts[0], parts[1]))
        xs.append(jnp.concatenate(halves, axis=1))
    hi, lo = split(jnp.concatenate(xs, axis=0))
    for p in range(6):
        piece = slice(p * LANES, (p + 1) * LANES)
        wh = mcol[0, :, piece]
        y[p] = dot(hi, wh) + dot(lo, wh) + dot(hi, mcol[1, :, piece])
    for s in range(3):
        gauss = prof[2 * s]
        for j in range(2):
            for g in range(groups):
                base = g * PATCH_ROWS

                def at(o):
                    return y[2 * s + j, base + HALF + o : base + HALF + o + STAMP, :]

                even = at(0) * np.float32(gauss[HALF])
                odd = None
                for d in range(1, HALF + 1):
                    up, down = at(d), at(-d)
                    even = even + (up + down) * np.float32(gauss[HALF + d])
                    term = (up - down) * np.float32(gauss[HALF + d] * d / HALF)
                    odd = term if odd is None else odd + term
                images[4 * s + 2 * j, g * STAMP : (g + 1) * STAMP, :] = even
                images[4 * s + 2 * j + 1, g * STAMP : (g + 1) * STAMP, :] = odd
    depth = groups * STAMP
    w = wp[...]
    weighted = None
    for p, (k, l) in enumerate(pair_list()):
        if l == NB:
            prod = sp[...] * images[k]
        else:
            if l == k:
                weighted = w * images[k]
            prod = weighted * images[l]
        sums[p * 8 : (p + 1) * 8, :] = jnp.sum(prod.reshape(depth // 8, 8, LANES), axis=0)
    used = len(pair_list())
    sums[used * 8 :, :] = jnp.zeros((96 * 8 - used * 8, LANES), F32)
    total = sums[pl.ds(0, 96, stride=8), :]
    for r in range(1, 8):
        total = total + sums[pl.ds(r, 96, stride=8), :]
    total = jnp.sum(total, axis=1, keepdims=True)
    spread = jnp.concatenate([total * first[0], total * first[1]], axis=0)
    system[...] = jnp.dot(leftm[...], spread, preferred_element_type=F32, precision=lax.Precision.HIGHEST)


def images_kernel(n_tile, nblk, info, *refs):
    blocks = refs[:nblk]
    lrow, wcol, out, t, rhi, rlo = refs[nblk:]
    m = pl.program_id(0)
    rows = rhi.shape[2]
    nrow = rows // LANES

    @pl.when(m == 0)
    def _():
        tile = info[0]
        assemble(info, n_tile, blocks, t)
        for b in range(nrow):
            left = lrow[variant(tile, b, n_tile, nrow)]
            for c in range(0, nblk, 2):
                x = jnp.concatenate(
                    [t[c + 1, b * LANES : b * LANES + WIN, :], t[c + 2, b * LANES : b * LANES + WIN, :]], axis=1
                )
                hi, lo = split(dot(left, stack3(x)))
                for p in range(6):
                    for h in range(2):
                        piece = (slice(p * LANES, (p + 1) * LANES), slice(h * LANES, (h + 1) * LANES))
                        rhi[c + h, p, b * LANES : (b + 1) * LANES, :] = hi[piece]
                        rlo[c + h, p, b * LANES : (b + 1) * LANES, :] = lo[piece]

    lane = lane_index((2 * rows, LANES))
    v = jnp.where(m == 0, 0, jnp.where(m == nblk - 1, 2, 1))
    after = jnp.minimum(m + 1, nblk - 1)
    before = jnp.maximum(m - 1, 0)
    for s in range(3):

        def window(ref):
            def get(i):
                return ref[i, 2 * s : 2 * s + 2].reshape(2 * rows, LANES)

            rim = jnp.where(lane < 64, get(after), get(before))
            return jnp.concatenate([get(m), rim], axis=1)

        hi, lo = window(rhi), window(rlo)
        q = dot(hi, wcol[v, s, 0]) + dot(lo, wcol[v, s, 0]) + dot(hi, wcol[v, s, 1])
        for i in range(2):
            for j in range(2):
                out[0, 4 * s + i + 2 * j] = q[i * rows : (i + 1) * rows, j * LANES : (j + 1) * LANES]


def final_kernel(system, d0, images, detection, coefficients, solved):
    @pl.when(pl.program_id(0) == 0)
    def _():
        a = system[...]
        row = lax.broadcasted_iota(jnp.int32, a.shape, 0)
        lane = lane_index(a.shape)
        diag = (row == lane) & (row < NB)
        trace = jnp.sum(jnp.sum(jnp.where(diag, a, 0.0), axis=1, keepdims=True), axis=0, keepdims=True)
        a = a + jnp.where(diag, 0.05 * trace / NB, 0.0)
        for k in range(NB):
            pivot = a[k : k + 1, :] / a[k : k + 1, k : k + 1]
            a = jnp.where(row == k, pivot, a - a[:, k : k + 1] * pivot)
        solved[...] = jnp.broadcast_to(a[:, NB : NB + 1], a.shape)
        for k in range(NB):
            coefficients[k] = solved[k, 0]

    total = d0[...]
    for k in range(NB):
        total = total - solved[k : k + 1, :] * images[0, k]
    detection[...] = total


def ring_order(count):
    return list(range(0, count, 2)) + list(range(count - 1, 0, -2))


def swap(x):
    return lax.ppermute(x, "tile", [(0, 1), (1, 0)])


def gather_ring(block, count):
    ring = ring_order(count)
    ahead = [(ring[i], ring[(i + 1) % count]) for i in range(count)]
    back = [(t, s) for s, t in ahead]
    out = [block]
    fwd = bwd = block
    for step in range(count // 2):
        fwd = lax.ppermute(fwd, "epoch", ahead)
        out.append(fwd)
        if step < count // 2 - 1:
            bwd = lax.ppermute(bwd, "epoch", back)
            out.append(bwd)
    return out


def ring_table(count):
    ring = ring_order(count)
    table = np.zeros((count, count), np.int32)
    for i, me in enumerate(ring):
        order = [me]
        for step in range(1, count // 2 + 1):
            order.append(ring[(i - step) % count])
            if step < count // 2:
                order.append(ring[(i + step) % count])
        table[me] = order
    return table


def all_sum(x, count):
    x = x + swap(x)
    if count & (count - 1):
        return lax.psum(x, "epoch")
    bit = 1
    while bit < count:
        x = x + lax.ppermute(x, "epoch", [(i, i ^ bit) for i in range(count)])
        bit *= 2
    return x


def local(template, science, flags, stamp_rows, stamp_cols):
    n_tile = lax.axis_size("tile")
    n_epoch = lax.axis_size("epoch")
    rows, width = template.shape
    science, flags = science[0], flags[0]
    cols = science.shape[1]
    nblk = cols // LANES
    groups = stamp_rows.shape[1] // 4
    tile = lax.axis_index("tile")

    def edge_of(x):
        return jnp.where(tile == 0, x[-HALO:], x[:HALO])

    edges = swap(jnp.concatenate([edge_of(template), edge_of(science)], axis=1))
    tall = jnp.concatenate([template, edges[:, :width]], axis=0)
    if width == LANES:
        blocks = gather_ring(tall, n_epoch)
        order = jnp.asarray(ring_table(n_epoch))[lax.axis_index("epoch")]
    else:
        whole = lax.all_gather(tall, "epoch", axis=1, tiled=True)
        blocks = [whole[:, m * LANES : (m + 1) * LANES] for m in range(nblk)]
        order = jnp.arange(nblk, dtype=jnp.int32)
    info = jnp.concatenate([tile[None].astype(jnp.int32), order])

    lrow6, lrow1 = row_tables()
    wcol6, wcol1 = column_tables()

    depth = groups * STAMP
    d0, wp, sp = pl.pallas_call(
        functools.partial(science_kernel, n_tile),
        out_shape=(
            jax.ShapeDtypeStruct((rows, cols), F32),
            jax.ShapeDtypeStruct((depth, LANES), F32),
            jax.ShapeDtypeStruct((depth, LANES), F32),
        ),
        in_specs=[SMEM()] * 3 + [VMEM()] * 5,
        out_specs=(VMEM(), VMEM(), VMEM()),
        scratch_shapes=[
            pltpu.VMEM((nblk, rows + 2 * HALO, LANES), F32),
            pltpu.VMEM((nblk, rows, LANES), F32),
            pltpu.VMEM((nblk, rows, LANES), F32),
        ],
        compiler_params=params(),
        cost_estimate=pl.CostEstimate(flops=2 * 10**9, bytes_accessed=4 * 2**20, transcendentals=0),
        name="science_filter",
    )(info, stamp_rows, stamp_cols, science, edges[:, width:], flags, jnp.asarray(lrow1), jnp.asarray(wcol1))

    first, leftm = place_tables()
    system = pl.pallas_call(
        functools.partial(stamp_kernel, n_tile, nblk),
        out_shape=jax.ShapeDtypeStruct((16, LANES), F32),
        in_specs=[SMEM()] * 3 + [VMEM()] * (nblk + 5),
        out_specs=VMEM(),
        scratch_shapes=[
            pltpu.VMEM((nblk + 2, rows + 2 * HALO, LANES), F32),
            pltpu.VMEM((6, groups * PATCH_ROWS, LANES), F32),
            pltpu.VMEM((NB, depth, LANES), F32),
            pltpu.VMEM((96 * 8, LANES), F32),
        ],
        compiler_params=params(),
        cost_estimate=pl.CostEstimate(flops=10**9, bytes_accessed=2 * 2**20, transcendentals=0),
        name="stamp_sums",
    )(info, stamp_rows, stamp_cols, *blocks, wp, sp, jnp.asarray(stamp_table()), jnp.asarray(first), jnp.asarray(leftm))

    images = pl.pallas_call(
        functools.partial(images_kernel, n_tile, nblk),
        out_shape=jax.ShapeDtypeStruct((nblk, NB, rows, LANES), F32),
        grid=(nblk,),
        in_specs=[SMEM()] + [VMEM()] * (nblk + 2),
        out_specs=pl.BlockSpec((1, NB, rows, LANES), lambda m: (m, 0, 0, 0)),
        scratch_shapes=[
            pltpu.VMEM((nblk + 2, rows + 2 * HALO, LANES), F32),
            pltpu.VMEM((nblk, 6, rows, LANES), BF16),
            pltpu.VMEM((nblk, 6, rows, LANES), BF16),
        ],
        compiler_params=params(),
        cost_estimate=pl.CostEstimate(flops=8 * 10**9, bytes_accessed=16 * 2**20, transcendentals=0),
        name="filtered_images",
    )(info, *blocks, jnp.asarray(lrow6), jnp.asarray(wcol6))

    system = all_sum(system, n_epoch)

    detection, coefficients = pl.pallas_call(
        final_kernel,
        out_shape=(
            jax.ShapeDtypeStruct((rows, cols), F32),
            jax.ShapeDtypeStruct((NB,), F32),
        ),
        grid=(nblk,),
        in_specs=[
            VMEM(),
            pl.BlockSpec((rows, LANES), lambda m: (0, m)),
            pl.BlockSpec((1, NB, rows, LANES), lambda m: (m, 0, 0, 0)),
        ],
        out_specs=(pl.BlockSpec((rows, LANES), lambda m: (0, m)), SMEM()),
        scratch_shapes=[pltpu.VMEM((16, LANES), F32)],
        compiler_params=params(),
        cost_estimate=pl.CostEstimate(flops=10**8, bytes_accessed=16 * 2**20, transcendentals=0),
        name="solve_subtract",
    )(system, d0, images)
    return (detection[None], coefficients)


def solution(mesh):
    return jax.shard_map(
        local,
        mesh=mesh,
        in_specs=(
            P(("patch", "tile"), "epoch"),
            P(("patch", "epoch"), "tile", None),
            P(("patch", "epoch"), "tile", None),
            P(("patch", "epoch"), "tile"),
            P(("patch", "epoch"), "tile"),
        ),
        out_specs=(P(("patch", "epoch"), "tile", None), P("patch")),
        check_vma=False,
    )
```

time: 326 us -> 69.1 us (0.21)
  other arithmetic: 164 us -> 4.5 us
  matrix products: 63.7 us -> 0 us
  blocking collectives: 32.4 us -> 0 us
  Pallas kernels: 0 us -> 31.5 us
  waiting for transfers between devices: 40.1 us -> 15.7 us
  between operations: 14.9 us -> 0.75 us
  starting transfers between devices: 5.19 us -> 14.3 us
    add x6 -> x4, other arithmetic: 153 us -> 1.31 us  [the longest x1 0.7 us: all_sum(): x = x + swap(x)]
    dot_general x4 -> x0, matrix products: 63.4 us -> none  [the longest x1 29.8 us: local(): jnp.einsum('kpq,lpq->kl', images * good[None], images, precision=lax.Prec...]
    all_gather x1 -> x0, waiting for transfers between devices: 37.1 us -> none  [local(): full_rows = lax.all_gather(template, 'epoch', axis=1, tiled=True)]
    psum x1 -> x0, blocking collectives: 32.4 us -> none  [local(): normal, rhs = lax.psum((normal_part, rhs_part), ('epoch', 'tile'))]
    pallas_call x0 -> x4, Pallas kernels: none -> 31.5 us  [the longest x1 13.5 us: local(): pl.pallas_call(functools.partial(images_kernel, n_tile, nblk), out_shape=...]
    ppermute x4 -> x12, waiting for transfers between devices: 2.28 us -> 15.7 us  [the longest x4 8.17 us: gather_ring(): fwd = lax.ppermute(fwd, 'epoch', ahead)]
    ppermute x4 -> x12, starting transfers between devices: 5.16 us -> 14.3 us  [the longest x4 8.39 us: gather_ring(): fwd = lax.ppermute(fwd, 'epoch', ahead)]
    another operation x5 -> x0, other arithmetic: 3.33 us -> none  [the longest x3 1.76 us: local(): factor = jnp.linalg.cholesky(system)]
  transfers between devices with their start and end apart: 5 -> 12, of which waited for: 3 -> 7; matrix products, arithmetic and copies ran while one was open for 3% -> 3% of each run, Pallas kernels for 0% -> 26%
where the time goes in v1:
time: 69.1 us; the launch traced here: 68.7 us
  Pallas kernels  31.5 us (46%)
  waiting for transfers between devices  15.7 us (23%)
  starting transfers between devices  14.3 us (21%)
  other arithmetic  4.5 us (7%)
  local copies, waits for them, and re-layouts  2.03 us (3%)
  between operations  0.75 us (1%)
    pallas_call x1, Pallas kernels, local(): pl.pallas_call(functools.partial(images_kernel, n_tile, nblk), out_shape=...  13.5 us
    pallas_call x1, Pallas kernels, local(): pl.pallas_call(final_kernel, out_shape=(jax.ShapeDtypeStruct((rows, cols)...  9.28 us
    ppermute x4, starting transfers between devices, gather_ring(): fwd = lax.ppermute(fwd, 'epoch', ahead)  8.39 us
    ppermute x4, waiting for transfers between devices, gather_ring(): fwd = lax.ppermute(fwd, 'epoch', ahead)  8.17 us
    ppermute x3, waiting for transfers between devices, all_sum(): x = x + lax.ppermute(x, 'epoch', [(i, i ^ bit) for i in range(count)])  5.2 us
    ppermute x3, starting transfers between devices, all_sum(): x = x + lax.ppermute(x, 'epoch', [(i, i ^ bit) for i in range(count)])  4.71 us
    pallas_call x1, Pallas kernels, local(): pl.pallas_call(functools.partial(science_kernel, n_tile), out_shape=(jax....  4.35 us
    pallas_call x1, Pallas kernels, local(): pl.pallas_call(functools.partial(stamp_kernel, n_tile, nblk), out_shape=j...  4.34 us
  transfers between devices with their start and end apart: 12, of which 7 were waited for; matrix products, arithmetic and copies ran while one was open for 3% of the time, Pallas kernels for 26%

profile of v1, /device:TPU:0, one launch (start us, length us, event | category | flops | bytes accessed | tf_op | source)
XLA Modules:
  0.0 68.7 jit_solution(1257516166863603203)
XLA Ops:
  0.6 0.7 %slice_select_fusion = f32[16,128]{1,0:T(8,128)S(1)} fusion(f32[256,128]{1,0:T(8,128)} %param.13, pred[]{:T(512)S(6)} %eq.4), kind=kLoop, calls=%fused_computation.3 | loop fusion | flops 2048 | bytes 24577 | tf_op jit(solution)/shard_map/jit(_where)/select_n | solution.py:427
  1.4 0.9 %select_bitcast_fusion = f32[16,1024]{1,0:T(8,128)S(1)} fusion(f32[1,256,1024]{2,1,0:T(8,128)} %param.14, pred[]{:T(512)S(6)} %eq.4), kind=kLoop, calls=%fused_computation.2 | loop fusion | flops 16384 | bytes 196609 | tf_op jit(solution)/shard_map/jit(_where)/select_n | solution.py:427
  2.8 0.9 %collective-permute-done = f32[16,1152]{1,0:T(8,128)S(1)} collective-permute-done((f32[16,1152]{1,0:T(8,128)S(1)}, f32[16,1152]{1,0:T(8,128)S(1)}, u32[]{:S(2)}, u32[]{:S(2)}) %collective-permute-start) | collective-permute-done | bytes 73760 | tf_op jit(solution)/shard_map/ppermute | solution.py:374
  3.7 0.9 %pad_maximum_fusion.refs_0_ = f32[272,128]{1,0:T(8,128)S(1)} fusion(f32[16,128]{1,0:T(8,128)S(1)} %slice.26, f32[256,128]{1,0:T(8,128)} %param.13), kind=kLoop, calls=%fused_computation | loop fusion | flops 34816 | bytes 278528 | tf_op jit(solution)/shard_map/concatenate | solution.py:430
  4.6 3.0 %collective-permute-start.1 = (f32[272,128]{1,0:T(8,128)S(1)}, f32[272,128]{1,0:T(8,128)S(1)}, u32[]{:S(2)}, u32[]{:S(2)}) collective-permute-start(f32[272,128]{1,0:T(8,128)S(1)} %pad_maximum_fusion.refs_0_), channel_id=1, source_target_pairs={{0,4},{4,8},{8,12},{12,14},{14,10},{10,6},{6,2},{2,0},{1,5},{5,9},... | collective-permute-start | bytes 417800 | tf_op jit(solution)/shard_map/ppermute | solution.py:384
  7.6 3.9 %collective-permute-done.1.refs_1_ = f32[272,128]{1,0:T(8,128)S(1)} collective-permute-done((f32[272,128]{1,0:T(8,128)S(1)}, f32[272,128]{1,0:T(8,128)S(1)}, u32[]{:S(2)}, u32[]{:S(2)}) %collective-permute-start.1) | collective-permute-done | bytes 139296 | tf_op jit(solution)/shard_map/ppermute | solution.py:384
  11.5 1.8 %collective-permute-start.3 = (f32[272,128]{1,0:T(8,128)S(1)}, f32[272,128]{1,0:T(8,128)S(1)}, u32[]{:S(2)}, u32[]{:S(2)}) collective-permute-start(f32[272,128]{1,0:T(8,128)S(1)} %collective-permute-done.1.refs_1_), channel_id=1, source_target_pairs={{0,4},{4,8},{8,12},{12,14},{14,10},{10,6},{6,2},{2,0},{1,5},{5,9},... | collective-permute-start | bytes 417800 | tf_op jit(solution)/shard_map/ppermute | solution.py:384
  13.6 3.2 %collective-permute-done.3.refs_3_ = f32[272,128]{1,0:T(8,128)S(1)} collective-permute-done((f32[272,128]{1,0:T(8,128)S(1)}, f32[272,128]{1,0:T(8,128)S(1)}, u32[]{:S(2)}, u32[]{:S(2)}) %collective-permute-start.3) | collective-permute-done | bytes 139296 | tf_op jit(solution)/shard_map/ppermute | solution.py:384
  16.8 1.6 %collective-permute-start.5 = (f32[272,128]{1,0:T(8,128)S(1)}, f32[272,128]{1,0:T(8,128)S(1)}, u32[]{:S(2)}, u32[]{:S(2)}) collective-permute-start(f32[272,128]{1,0:T(8,128)S(1)} %collective-permute-done.3.refs_3_), channel_id=1, source_target_pairs={{0,4},{4,8},{8,12},{12,14},{14,10},{10,6},{6,2},{2,0},{1,5},{5,9},... | collective-permute-start | bytes 417800 | tf_op jit(solution)/shard_map/ppermute | solution.py:384
  18.4 0.7 %dynamic-slice_bitcast_fusion = s32[8]{0:T(128)S(1)} fusion(s32[8,8]{1,0:T(8,128)} %constant.28.clone, s32[]{:T(128)S(6)} %select_n.22), kind=kLoop, calls=%fused_computation.5 | loop fusion | bytes 68 | tf_op jit(solution)/shard_map/squeeze | solution.py:433
  19.1 0.7 pad_add_fusion.info
  20.8 1.0 %collective-permute-done.5.refs_5_ = f32[272,128]{1,0:T(8,128)S(1)} collective-permute-done((f32[272,128]{1,0:T(8,128)S(1)}, f32[272,128]{1,0:T(8,128)S(1)}, u32[]{:S(2)}, u32[]{:S(2)}) %collective-permute-start.5) | collective-permute-done | bytes 139296 | tf_op jit(solution)/shard_map/ppermute | solution.py:384
  21.8 2.0 %collective-permute-start.7 = (f32[272,128]{1,0:T(8,128)S(1)}, f32[272,128]{1,0:T(8,128)S(1)}, u32[]{:S(2)}, u32[]{:S(2)}) collective-permute-start(f32[272,128]{1,0:T(8,128)S(1)} %collective-permute-done.5.refs_5_), channel_id=1, source_target_pairs={{0,4},{4,8},{8,12},{12,14},{14,10},{10,6},{6,2},{2,0},{1,5},{5,9},... | collective-permute-start | bytes 417800 | tf_op jit(solution)/shard_map/ppermute | solution.py:384
  23.8 4.3 %science_filter.1 = (f32[256,1024]{1,0:T(8,128)}, f32[128,128]{1,0:T(8,128)}, f32[128,128]{1,0:T(8,128)}) custom-call(s32[9]{0:T(128)} %pad_add_fusion.info, s32[1,16]{1,0:T(1,128)} %tops.3, s32[1,16]{1,0:T(1,128)} %lefts.3, f32[256,1024]{1,0:T(8,128)} %bitcast.8, f32[16,1024]{1,0:T(8,128)} %slice.27.edge, s32[256,1024]{1,0:T(8,128)} %bitcast.9, ...), custom_call_target="tpu_custom_call" | custom-call | flops 2000000000 | bytes 4194304 | tf_op jit(solution)/shard_map/science_filter/pallas_call | solution.py:444
  28.2 0.6 copy-done.6
  28.9 4.3 %stamp_sums.1 = f32[16,128]{1,0:T(8,128)} custom-call(s32[9]{0:T(128)} %pad_add_fusion.info, s32[1,16]{1,0:T(1,128)} %tops.3, s32[1,16]{1,0:T(1,128)} %lefts.3, f32[272,128]{1,0:T(8,128)} %copy-done, f32[272,128]{1,0:T(8,128)} %copy-done.1, f32[272,128]{1,0:T(8,128)} %copy-done.2, f32[272,128]{1,0:T(8,128)} %copy-done.3, f32[272,128]{1,0:T(8,128)} %copy-done.4, ...), custom_call_target="tpu_custom_call" | custom-call | flops 1000000000 | bytes 2097152 | tf_op jit(solution)/shard_map/stamp_sums/pallas_call | solution.py:464
  33.3 1.4 %collective-permute-done.8 = f32[16,128]{1,0:T(8,128)S(1)} collective-permute-done((f32[16,128]{1,0:T(8,128)}, f32[16,128]{1,0:T(8,128)S(1)}, u32[]{:S(2)}, u32[]{:S(2)}) %collective-permute-start.8) | collective-permute-done | bytes 8224 | tf_op jit(solution)/shard_map/ppermute | solution.py:374
  34.7 0.7 %add.16 = f32[16,128]{1,0:T(8,128)S(1)} add(f32[16,128]{1,0:T(8,128)} %stamp_sums.1, f32[16,128]{1,0:T(8,128)S(1)} %collective-permute-done.8) | non-fusion elementwise | flops 2048 | bytes 24576 | tf_op jit(solution)/shard_map/add | solution.py:406
  35.9 3.1 %collective-permute-done.9 = f32[16,128]{1,0:T(8,128)S(1)} collective-permute-done((f32[16,128]{1,0:T(8,128)S(1)}, f32[16,128]{1,0:T(8,128)S(1)}, u32[]{:S(2)}, u32[]{:S(2)}) %collective-permute-start.9) | collective-permute-done | bytes 8224 | tf_op jit(solution)/shard_map/ppermute | solution.py:411
  39.0 1.6 %collective-permute-start.10 = (f32[16,128]{1,0:T(8,128)S(1)}, f32[16,128]{1,0:T(8,128)S(1)}, u32[]{:S(2)}, u32[]{:S(2)}) collective-permute-start(f32[16,128]{1,0:T(8,128)S(1)} %add.17), channel_id=1, source_target_pairs={{0,4},{2,6},{4,0},{6,2},{8,12},{10,14},{12,8},{14,10},{1,5},{3,7},... | collective-permute-start | bytes 24584 | tf_op jit(solution)/shard_map/ppermute | solution.py:411
  40.6 2.1 %collective-permute-done.10 = f32[16,128]{1,0:T(8,128)S(1)} collective-permute-done((f32[16,128]{1,0:T(8,128)S(1)}, f32[16,128]{1,0:T(8,128)S(1)}, u32[]{:S(2)}, u32[]{:S(2)}) %collective-permute-start.10) | collective-permute-done | bytes 8224 | tf_op jit(solution)/shard_map/ppermute | solution.py:411
  42.7 2.6 %collective-permute-start.11 = (f32[16,128]{1,0:T(8,128)S(1)}, f32[16,128]{1,0:T(8,128)S(1)}, u32[]{:S(2)}, u32[]{:S(2)}) collective-permute-start(f32[16,128]{1,0:T(8,128)S(1)} %add.18), channel_id=1, source_target_pairs={{0,8},{2,10},{4,12},{6,14},{8,0},{10,2},{12,4},{14,6},{1,9},{3,11}... | collective-permute-start | bytes 24584 | tf_op jit(solution)/shard_map/ppermute | solution.py:411
  45.3 13.5 %filtered_images.1.images = f32[8,12,256,128]{3,2,1,0:T(8,128)} custom-call(s32[9]{0:T(128)} %pad_add_fusion.info, f32[272,128]{1,0:T(8,128)} %copy-done, f32[272,128]{1,0:T(8,128)} %copy-done.1, f32[272,128]{1,0:T(8,128)} %copy-done.2, f32[272,128]{1,0:T(8,128)} %copy-done.3, f32[272,128]{1,0:T(8,128)} %copy-done.4, f32[272,128]{1,0:T(8,128)} %copy-done.5, ...), custom_call_target="tpu_custom_call" | custom-call | flops 8000000000 | bytes 16777216 | tf_op jit(solution)/shard_map/filtered_images/pallas_call | solution.py:480
  59.4 9.3 %solve_subtract.1 = (f32[256,1024]{1,0:T(8,128)}, f32[12]{0:T(128)}) custom-call(f32[16,128]{1,0:T(8,128)} %add.19.system, f32[256,1024]{1,0:T(8,128)} %get-tuple-element.9.d0, f32[8,12,256,128]{3,2,1,0:T(8,128)} %filtered_images.1.images), custom_call_target="tpu_custom_call" | custom-call | flops 100000000 | bytes 16777216 | tf_op jit(solution)/shard_map/solve_subtract/pallas_call | solution.py:498
  (32 shorter events, 3.0 us)
Async XLA Ops:
  2.3 1.4 %collective-permute-start = (f32[16,1152]{1,0:T(8,128)S(1)}, f32[16,1152]{1,0:T(8,128)S(1)}, u32[]{:S(2)}, u32[]{:S(2)}) collective-permute-start(f32[16,1152]{1,0:T(8,128)S(1)} %pad_maximum_fusion.1), channel_id=1, source_target_pairs={{0,1},{1,0},{2,3},{3,2},{4,5},{5,4},{6,7},{7,6},{8,9},{9,8},{10,11... | collective-permute-start | bytes 221192 | tf_op jit(solution)/shard_map/ppermute | solution.py:374
  4.6 23.6 %copy-start = (f32[272,128]{1,0:T(8,128)}, f32[272,128]{1,0:T(8,128)S(1)}, u32[]{:S(2)}) copy-start(f32[272,128]{1,0:T(8,128)S(1)} %pad_maximum_fusion.refs_0_) | copy-start | bytes 417796
  4.6 6.9 %collective-permute-start.1 = (f32[272,128]{1,0:T(8,128)S(1)}, f32[272,128]{1,0:T(8,128)S(1)}, u32[]{:S(2)}, u32[]{:S(2)}) collective-permute-start(f32[272,128]{1,0:T(8,128)S(1)} %pad_maximum_fusion.refs_0_), channel_id=1, source_target_pairs={{0,4},{4,8},{8,12},{12,14},{14,10},{10,6},{6,2},{2,0},{1,5},{5,9},... | collective-permute-start | bytes 417800 | tf_op jit(solution)/shard_map/ppermute | solution.py:384
  7.6 5.7 %collective-permute-start.2 = (f32[272,128]{1,0:T(8,128)S(1)}, f32[272,128]{1,0:T(8,128)S(1)}, u32[]{:S(2)}, u32[]{:S(2)}) collective-permute-start(f32[272,128]{1,0:T(8,128)S(1)} %pad_maximum_fusion.refs_0_), channel_id=1, source_target_pairs={{4,0},{8,4},{12,8},{14,12},{10,14},{6,10},{2,6},{0,2},{5,1},{9,5},... | collective-permute-start | bytes 417800 | tf_op jit(solution)/shard_map/ppermute | solution.py:387
  11.5 16.6 %copy-start.1 = (f32[272,128]{1,0:T(8,128)}, f32[272,128]{1,0:T(8,128)S(1)}, u32[]{:S(2)}) copy-start(f32[272,128]{1,0:T(8,128)S(1)} %collective-permute-done.1.refs_1_) | copy-start | bytes 417796
  11.5 5.2 %collective-permute-start.3 = (f32[272,128]{1,0:T(8,128)S(1)}, f32[272,128]{1,0:T(8,128)S(1)}, u32[]{:S(2)}, u32[]{:S(2)}) collective-permute-start(f32[272,128]{1,0:T(8,128)S(1)} %collective-permute-done.1.refs_1_), channel_id=1, source_target_pairs={{0,4},{4,8},{8,12},{12,14},{14,10},{10,6},{6,2},{2,0},{1,5},{5,9},... | collective-permute-start | bytes 417800 | tf_op jit(solution)/shard_map/ppermute | solution.py:384
  13.3 14.8 %copy-start.2 = (f32[272,128]{1,0:T(8,128)}, f32[272,128]{1,0:T(8,128)S(1)}, u32[]{:S(2)}) copy-start(f32[272,128]{1,0:T(8,128)S(1)} %collective-permute-done.2.refs_2_) | copy-start | bytes 417796
  13.3 7.0 %collective-permute-start.4 = (f32[272,128]{1,0:T(8,128)S(1)}, f32[272,128]{1,0:T(8,128)S(1)}, u32[]{:S(2)}, u32[]{:S(2)}) collective-permute-start(f32[272,128]{1,0:T(8,128)S(1)} %collective-permute-done.2.refs_2_), channel_id=1, source_target_pairs={{4,0},{8,4},{12,8},{14,12},{10,14},{6,10},{2,6},{0,2},{5,1},{9,5},... | collective-permute-start | bytes 417800 | tf_op jit(solution)/shard_map/ppermute | solution.py:387
  16.8 11.4 %copy-start.3 = (f32[272,128]{1,0:T(8,128)}, f32[272,128]{1,0:T(8,128)S(1)}, u32[]{:S(2)}) copy-start(f32[272,128]{1,0:T(8,128)S(1)} %collective-permute-done.3.refs_3_) | copy-start | bytes 417796
  16.8 5.1 %collective-permute-start.5 = (f32[272,128]{1,0:T(8,128)S(1)}, f32[272,128]{1,0:T(8,128)S(1)}, u32[]{:S(2)}, u32[]{:S(2)}) collective-permute-start(f32[272,128]{1,0:T(8,128)S(1)} %collective-permute-done.3.refs_3_), channel_id=1, source_target_pairs={{0,4},{4,8},{8,12},{12,14},{14,10},{10,6},{6,2},{2,0},{1,5},{5,9},... | collective-permute-start | bytes 417800 | tf_op jit(solution)/shard_map/ppermute | solution.py:384
  20.4 7.8 %copy-start.4 = (f32[272,128]{1,0:T(8,128)}, f32[272,128]{1,0:T(8,128)S(1)}, u32[]{:S(2)}) copy-start(f32[272,128]{1,0:T(8,128)S(1)} %collective-permute-done.4.refs_4_) | copy-start | bytes 417796
  20.4 7.8 %collective-permute-start.6 = (f32[272,128]{1,0:T(8,128)S(1)}, f32[272,128]{1,0:T(8,128)S(1)}, u32[]{:S(2)}, u32[]{:S(2)}) collective-permute-start(f32[272,128]{1,0:T(8,128)S(1)} %collective-permute-done.4.refs_4_), channel_id=1, source_target_pairs={{4,0},{8,4},{12,8},{14,12},{10,14},{6,10},{2,6},{0,2},{5,1},{9,5},... | collective-permute-start | bytes 417800 | tf_op jit(solution)/shard_map/ppermute | solution.py:387
  21.8 6.4 %copy-start.5 = (f32[272,128]{1,0:T(8,128)}, f32[272,128]{1,0:T(8,128)S(1)}, u32[]{:S(2)}) copy-start(f32[272,128]{1,0:T(8,128)S(1)} %collective-permute-done.5.refs_5_) | copy-start | bytes 417796
  21.8 6.4 %collective-permute-start.7 = (f32[272,128]{1,0:T(8,128)S(1)}, f32[272,128]{1,0:T(8,128)S(1)}, u32[]{:S(2)}, u32[]{:S(2)}) collective-permute-start(f32[272,128]{1,0:T(8,128)S(1)} %collective-permute-done.5.refs_5_), channel_id=1, source_target_pairs={{0,4},{4,8},{8,12},{12,14},{14,10},{10,6},{6,2},{2,0},{1,5},{5,9},... | collective-permute-start | bytes 417800 | tf_op jit(solution)/shard_map/ppermute | solution.py:384
  28.2 0.7 copy-start.6
  28.2 0.7 %copy-start.7 = (f32[272,128]{1,0:T(8,128)}, f32[272,128]{1,0:T(8,128)S(1)}, u32[]{:S(2)}) copy-start(f32[272,128]{1,0:T(8,128)S(1)} %collective-permute-done.7.refs_7_) | copy-start | bytes 417796
  33.3 1.4 %collective-permute-start.8 = (f32[16,128]{1,0:T(8,128)}, f32[16,128]{1,0:T(8,128)S(1)}, u32[]{:S(2)}, u32[]{:S(2)}) collective-permute-start(f32[16,128]{1,0:T(8,128)} %stamp_sums.1), channel_id=1, source_target_pairs={{0,1},{1,0},{2,3},{3,2},{4,5},{5,4},{6,7},{7,6},{8,9},{9,8},{10,11... | collective-permute-start | bytes 24584 | tf_op jit(solution)/shard_map/ppermute | solution.py:374
  35.4 3.7 %collective-permute-start.9 = (f32[16,128]{1,0:T(8,128)S(1)}, f32[16,128]{1,0:T(8,128)S(1)}, u32[]{:S(2)}, u32[]{:S(2)}) collective-permute-start(f32[16,128]{1,0:T(8,128)S(1)} %add.16), channel_id=1, source_target_pairs={{0,2},{2,0},{4,6},{6,4},{8,10},{10,8},{12,14},{14,12},{1,3},{3,1},... | collective-permute-start | bytes 24584 | tf_op jit(solution)/shard_map/ppermute | solution.py:411
  39.0 3.7 %collective-permute-start.10 = (f32[16,128]{1,0:T(8,128)S(1)}, f32[16,128]{1,0:T(8,128)S(1)}, u32[]{:S(2)}, u32[]{:S(2)}) collective-permute-start(f32[16,128]{1,0:T(8,128)S(1)} %add.17), channel_id=1, source_target_pairs={{0,4},{2,6},{4,0},{6,2},{8,12},{10,14},{12,8},{14,10},{1,5},{3,7},... | collective-permute-start | bytes 24584 | tf_op jit(solution)/shard_map/ppermute | solution.py:411
  42.7 16.1 %collective-permute-start.11 = (f32[16,128]{1,0:T(8,128)S(1)}, f32[16,128]{1,0:T(8,128)S(1)}, u32[]{:S(2)}, u32[]{:S(2)}) collective-permute-start(f32[16,128]{1,0:T(8,128)S(1)} %add.18), channel_id=1, source_target_pairs={{0,8},{2,10},{4,12},{6,14},{8,0},{10,2},{12,4},{14,6},{1,9},{3,11}... | collective-permute-start | bytes 24584 | tf_op jit(solution)/shard_map/ppermute | solution.py:411

commit v2 on v1

--- a/solution.py
+++ b/solution.py
@@ -157,25 +157,44 @@
     return lax.broadcasted_iota(jnp.int32, shape, len(shape) - 1)
 
 
-def science_kernel(n_tile, info, tops, lefts, sci, edge, flags, lrow, wcol, d0, wp, sp, sb, fb, mid):
+def variant(tile, b, n_tile, nrow):
+    v = jnp.int32(1)
+    if b == 0:
+        v = jnp.where(tile == 0, 0, v)
+    if b == nrow - 1:
+        v = jnp.where(tile == n_tile - 1, 2, v)
+    return v
+
+
+def window_rows(tile, b, n_tile, nrow, own, edge):
+    size = nrow * LANES
+    low, high = b * LANES - HALO, (b + 1) * LANES + HALO
+    parts = []
+    if low < 0:
+        parts.append(jnp.where(tile == 0, 0.0, edge()))
+    parts.append(own(max(low, 0), min(high, size)))
+    if high > size:
+        parts.append(jnp.where(tile == n_tile - 1, 0.0, edge()))
+    return jnp.concatenate(parts, axis=0)
+
+
+def science_kernel(n_tile, info, sci, edge, lrow, wcol, after, *refs):
+    count = len(refs) // 2 - 1
+    d0, mid, sems = refs[count], refs[-2], refs[-1]
+    copies = [pltpu.make_async_copy(refs[i], refs[count + 1 + i], sems.at[i]) for i in range(count)]
+    for copy in copies:
+        copy.start()
     tile = info[0]
-    rows, cols = sci.shape
-    nblk = cols // LANES
+    nblk, rows = sci.shape[:2]
     nrow = rows // LANES
-    for m in range(nblk):
-        piece = slice(m * LANES, (m + 1) * LANES)
-        e = edge[:, piece]
-        sb[m, 0:HALO, :] = jnp.where(tile == 0, 0.0, e)
-        sb[m, HALO : HALO + rows, :] = sci[:, piece]
-        sb[m, HALO + rows :, :] = jnp.where(tile == n_tile - 1, 0.0, e)
-        fb[m] = jnp.where(flags[:, piece] == 0, 1.0, 0.0)
     for b in range(nrow):
-        v = variant(tile, b, n_tile, nrow)
-        left = lrow[v]
+        left = lrow[variant(tile, b, n_tile, nrow)]
         for m in range(0, nblk, 2):
-            x = jnp.concatenate(
-                [sb[m, b * LANES : b * LANES + WIN, :], sb[m + 1, b * LANES : b * LANES + WIN, :]], axis=1
-            )
+
+            def own(lo, hi):
+                return jnp.concatenate([sci[m, lo:hi, :], sci[m + 1, lo:hi, :]], axis=1)
+
+            x = window_rows(tile, b, n_tile, nrow, own, lambda: edge[:, m * LANES : (m + 2) * LANES])
             y = dot(left, stack3(x))
             mid[m, b * LANES : (b + 1) * LANES, :] = y[:, :LANES]
             mid[m + 1, b * LANES : (b + 1) * LANES, :] = y[:, LANES:]
@@ -185,13 +204,37 @@
         rim = jnp.where(lane < 64, mid[min(m + 1, nblk - 1)], mid[max(m - 1, 0)])
         hi, lo = split(jnp.concatenate([mid[m], rim], axis=1))
         d0[:, m * LANES : (m + 1) * LANES] = dot(hi, wcol[v, 0]) + dot(lo, wcol[v, 0]) + dot(hi, wcol[v, 1])
+    for copy in copies:
+        copy.wait()
+
+
+def load_kernel(n_tile, stamps, info, *refs):
+    sci, flags, lrow, *tables = refs[: len(refs) // 2 - 2]
+    wp, sp, sb, lout, *outs = refs[len(refs) // 2 - 2 : -3]
+    fb, sems, more = refs[-3:]
+    tile = info[0]
+    nblk, rows = sb.shape[:2]
+    nrow = rows // LANES
+    early = []
+    for m in range(nblk):
+        piece = slice(m * LANES, (m + 1) * LANES)
+        early.append(pltpu.make_async_copy(sci.at[:, piece], sb.at[m], sems.at[m]))
+        early.append(pltpu.make_async_copy(flags.at[:, piece], fb.at[m], sems.at[nblk + m]))
+    late = [
+        pltpu.make_async_copy(lrow.at[variant(tile, b, n_tile, nrow)], lout.at[b], more.at[b]) for b in range(nrow)
+    ]
+    late += [pltpu.make_async_copy(t, o, more.at[nrow + i]) for i, (t, o) in enumerate(zip(tables, outs))]
+    for copy in early + late:
+        copy.start()
+    for copy in early:
+        copy.wait()
     lane = lane_index((STAMP, LANES))
-    for g in range(tops.shape[1] // 4):
+    for g in range(stamps // 4):
         w = jnp.zeros((STAMP, LANES), F32)
         s = jnp.zeros((STAMP, LANES), F32)
         for q in range(4):
-            top = tops[0, g * 4 + q]
-            left = lefts[0, g * 4 + q]
+            top = info[1 + g * 4 + q]
+            left = info[1 + stamps + g * 4 + q]
             blk = left // LANES
             off = left - blk * LANES
             nxt = jnp.minimum(blk + 1, nblk - 1)
@@ -199,44 +242,37 @@
             near = lane < q * STAMP - off + LANES
             here = (lane >= q * STAMP) & (lane < (q + 1) * STAMP)
 
-            def window(ref, first):
-                a = pltpu.roll(ref[blk, pl.ds(first, STAMP), :], shift, 1)
-                b = pltpu.roll(ref[nxt, pl.ds(first, STAMP), :], shift, 1)
+            def window(ref):
+                a = pltpu.roll(ref[blk, pl.ds(top, STAMP), :], shift, 1)
+                b = pltpu.roll(ref[nxt, pl.ds(top, STAMP), :], shift, 1)
                 return jnp.where(near, a, b)
 
-            w = jnp.where(here, window(fb, top), w)
-            s = jnp.where(here, window(sb, top + HALO), s)
+            w = jnp.where(here & (window(fb) == 0), 1.0, w)
+            s = jnp.where(here, window(sb), s)
         wp[g * STAMP : (g + 1) * STAMP, :] = w
-        sp[g * STAMP : (g + 1) * STAMP, :] = w * s
-
-
-def variant(tile, b, n_tile, nrow):
-    v = jnp.int32(1)
-    if b == 0:
-        v = jnp.where(tile == 0, 0, v)
-    if b == nrow - 1:
-        v = jnp.where(tile == n_tile - 1, 2, v)
-    return v
-
-
-def assemble(info, n_tile, blocks, t):
+        sp[g * STAMP : (g + 1) * STAMP, :] = jnp.where(w > 0.0, s, 0.0)
+    for copy in late:
+        copy.wait()
+
+
+def assemble(info, first, n_tile, blocks, t):
     tile = info[0]
     rows = blocks[0].shape[0] - HALO
     for m in (0, len(blocks) + 1):
         t[m] = jnp.zeros(t.shape[1:], F32)
     for slot, block in enumerate(blocks):
-        at = info[1 + slot] + 1
+        at = info[first + slot] + 1
         e = block[rows:, :]
         t[at, 0:HALO, :] = jnp.where(tile == 0, 0.0, e)
         t[at, HALO : HALO + rows, :] = block[0:rows, :]
         t[at, HALO + rows :, :] = jnp.where(tile == n_tile - 1, 0.0, e)
 
 
-def stamp_kernel(n_tile, nblk, info, tops, lefts, *refs):
+def stamp_kernel(n_tile, nblk, stamps, info, *refs):
     blocks = refs[:nblk]
     wp, sp, mcol, first, leftm, system, t, y, images, sums = refs[nblk:]
-    assemble(info, n_tile, blocks, t)
-    groups = tops.shape[1] // 4
+    assemble(info, 1 + 2 * stamps, n_tile, blocks, t)
+    groups = stamps // 4
     lane = lane_index((PATCH_ROWS, LANES))
     prof = profiles()
     xs = []
@@ -246,11 +282,11 @@
             parts = []
             for h in range(2):
                 j = g * 4 + pair * 2 + h
-                start = lefts[0, j] + (LANES - HALF)
+                start = info[1 + stamps + j] + (LANES - HALF)
                 blk = start // LANES
                 off = start - blk * LANES
                 shift = lax.rem(64 * h - off + LANES, LANES)
-                rows = pl.ds(tops[0, j] + (HALO - HALF), PATCH_ROWS)
+                rows = pl.ds(info[1 + j] + (HALO - HALF), PATCH_ROWS)
                 a = pltpu.roll(t[blk, rows, :], shift, 1)
                 b = pltpu.roll(t[blk + 1, rows, :], shift, 1)
                 parts.append(jnp.where(lane < 64 * h - off + LANES, a, b))
@@ -300,51 +336,53 @@
     system[...] = jnp.dot(leftm[...], spread, preferred_element_type=F32, precision=lax.Precision.HIGHEST)
 
 
-def images_kernel(n_tile, nblk, info, *refs):
-    blocks = refs[:nblk]
-    lrow, wcol, out, t, rhi, rlo = refs[nblk:]
-    m = pl.program_id(0)
+def rows_kernel(n_tile, first, slots, info, lrow, after, *refs):
+    blocks = refs[: len(slots)]
+    rhi, rlo = refs[-2:]
+    tile = info[0]
     rows = rhi.shape[2]
     nrow = rows // LANES
-
-    @pl.when(m == 0)
-    def _():
-        tile = info[0]
-        assemble(info, n_tile, blocks, t)
-        for b in range(nrow):
-            left = lrow[variant(tile, b, n_tile, nrow)]
-            for c in range(0, nblk, 2):
-                x = jnp.concatenate(
-                    [t[c + 1, b * LANES : b * LANES + WIN, :], t[c + 2, b * LANES : b * LANES + WIN, :]], axis=1
-                )
-                hi, lo = split(dot(left, stack3(x)))
-                for p in range(6):
-                    for h in range(2):
-                        piece = (slice(p * LANES, (p + 1) * LANES), slice(h * LANES, (h + 1) * LANES))
-                        rhi[c + h, p, b * LANES : (b + 1) * LANES, :] = hi[piece]
-                        rlo[c + h, p, b * LANES : (b + 1) * LANES, :] = lo[piece]
-
+    for b in range(nrow):
+        left = lrow[b]
+        xs = [
+            window_rows(tile, b, n_tile, nrow, lambda lo, hi: block[lo:hi, :], lambda: block[rows:, :])
+            for block in blocks
+        ]
+        hi, lo = split(dot(left, stack3(jnp.concatenate(xs, axis=1) if len(xs) > 1 else xs[0])))
+        for h, slot in enumerate(slots):
+            at = info[first + slot]
+            for p in range(6):
+                piece = (slice(p * LANES, (p + 1) * LANES), slice(h * LANES, (h + 1) * LANES))
+                rhi[at, p, b * LANES : (b + 1) * LANES, :] = hi[piece]
+                rlo[at, p, b * LANES : (b + 1) * LANES, :] = lo[piece]
+
+
+def columns_kernel(nblk, first, places, info, rhi, rlo, wcol, *refs):
+    out = refs[-1]
+    rows = rhi.shape[2]
     lane = lane_index((2 * rows, LANES))
-    v = jnp.where(m == 0, 0, jnp.where(m == nblk - 1, 2, 1))
-    after = jnp.minimum(m + 1, nblk - 1)
-    before = jnp.maximum(m - 1, 0)
-    for s in range(3):
-
-        def window(ref):
-            def get(i):
-                return ref[i, 2 * s : 2 * s + 2].reshape(2 * rows, LANES)
-
-            rim = jnp.where(lane < 64, get(after), get(before))
-            return jnp.concatenate([get(m), rim], axis=1)
-
-        hi, lo = window(rhi), window(rlo)
-        q = dot(hi, wcol[v, s, 0]) + dot(lo, wcol[v, s, 0]) + dot(hi, wcol[v, s, 1])
-        for i in range(2):
-            for j in range(2):
-                out[0, 4 * s + i + 2 * j] = q[i * rows : (i + 1) * rows, j * LANES : (j + 1) * LANES]
-
-
-def final_kernel(system, d0, images, detection, coefficients, solved):
+    for place in places:
+        m = info[first + place]
+        v = jnp.where(m == 0, 0, jnp.where(m == nblk - 1, 2, 1))
+        after = jnp.minimum(m + 1, nblk - 1)
+        before = jnp.maximum(m - 1, 0)
+        for s in range(3):
+
+            def window(ref):
+                def get(i):
+                    return ref[i, 2 * s : 2 * s + 2].reshape(2 * rows, LANES)
+
+                rim = jnp.where(lane < 64, get(after), get(before))
+                return jnp.concatenate([get(m), rim], axis=1)
+
+            hi, lo = window(rhi), window(rlo)
+            q = dot(hi, wcol[v, s, 0]) + dot(lo, wcol[v, s, 0]) + dot(hi, wcol[v, s, 1])
+            for i in range(2):
+                for j in range(2):
+                    out[m, 4 * s + i + 2 * j] = q[i * rows : (i + 1) * rows, j * LANES : (j + 1) * LANES]
+
+
+def final_kernel(step, system, d0, images, detection, coefficients, solved):
     @pl.when(pl.program_id(0) == 0)
     def _():
         a = system[...]
@@ -360,10 +398,12 @@
         for k in range(NB):
             coefficients[k] = solved[k, 0]
 
-    total = d0[...]
-    for k in range(NB):
-        total = total - solved[k : k + 1, :] * images[0, k]
-    detection[...] = total
+    for h in range(step):
+        m = pl.program_id(0) * step + h
+        total = d0[:, h * LANES : (h + 1) * LANES]
+        for k in range(NB):
+            total = total - solved[k : k + 1, :] * images[m, k]
+        detection[:, h * LANES : (h + 1) * LANES] = total
 
 
 def ring_order(count):
@@ -402,15 +442,54 @@
     return table
 
 
-def all_sum(x, count):
+def all_sum(x, count, beside):
+    beside[0](x)
     x = x + swap(x)
     if count & (count - 1):
+        for f in beside[1:]:
+            f(x)
         return lax.psum(x, "epoch")
-    bit = 1
-    while bit < count:
-        x = x + lax.ppermute(x, "epoch", [(i, i ^ bit) for i in range(count)])
-        bit *= 2
+    steps = count.bit_length() - 1
+    for i in range(steps):
+        for f in beside[1 + i :: steps]:
+            f(x)
+        x = x + lax.ppermute(x, "epoch", [(j, j ^ (1 << i)) for j in range(count)])
     return x
+
+
+def place_table(last, nblk):
+    return np.stack([(x + 2 + np.arange(nblk)) % nblk for x in last]).astype(np.int32)
+
+
+def in_vmem(x):
+    return pltpu.with_memory_space_constraint(x, pltpu.VMEM)
+
+
+ANY = functools.partial(pl.BlockSpec, memory_space=pl.ANY)
+HBM = functools.partial(pl.BlockSpec, memory_space=pltpu.HBM)
+
+
+def call(kernel, name, out, ins, limit, flops, scratch=(), aliases=None, outside=(), hbm=()):
+    ins = [pltpu.with_memory_space_constraint(x, pltpu.HBM) if i in hbm else x for i, x in enumerate(ins)]
+
+    def spec(i, x):
+        if i in outside:
+            return ANY()
+        if i in hbm:
+            return HBM()
+        return SMEM() if x.ndim == 1 else VMEM()
+
+    return pl.pallas_call(
+        kernel,
+        out_shape=out,
+        in_specs=[spec(i, x) for i, x in enumerate(ins)],
+        out_specs=jax.tree.map(lambda _: VMEM(), out, is_leaf=lambda x: hasattr(x, "shape")),
+        scratch_shapes=scratch,
+        input_output_aliases=aliases or {},
+        compiler_params=pltpu.CompilerParams(vmem_limit_bytes=limit * 2**20),
+        cost_estimate=pl.CostEstimate(flops=flops, bytes_accessed=2**20, transcendentals=0),
+        name=name,
+    )(*ins)
 
 
 def local(template, science, flags, stamp_rows, stamp_cols):
@@ -420,99 +499,151 @@
     science, flags = science[0], flags[0]
     cols = science.shape[1]
     nblk = cols // LANES
-    groups = stamp_rows.shape[1] // 4
+    nrow = rows // LANES
+    stamps = stamp_rows.shape[1]
+    groups = stamps // 4
+    depth = groups * STAMP
     tile = lax.axis_index("tile")
 
     def edge_of(x):
         return jnp.where(tile == 0, x[-HALO:], x[:HALO])
 
-    edges = swap(jnp.concatenate([edge_of(template), edge_of(science)], axis=1))
-    tall = jnp.concatenate([template, edges[:, :width]], axis=0)
+    tall = jnp.concatenate([template, swap(edge_of(template))], axis=0)
+    _, later, stamp_rows, stamp_cols = lax.optimization_barrier((tall, science, stamp_rows, stamp_cols))
+    science_edge = swap(edge_of(later))
     if width == LANES:
         blocks = gather_ring(tall, n_epoch)
-        order = jnp.asarray(ring_table(n_epoch))[lax.axis_index("epoch")]
+        table = np.concatenate([ring_table(n_epoch), place_table(ring_table(n_epoch)[:, -1], nblk)], axis=1)
+        order = jnp.asarray(table)[lax.axis_index("epoch")]
     else:
         whole = lax.all_gather(tall, "epoch", axis=1, tiled=True)
         blocks = [whole[:, m * LANES : (m + 1) * LANES] for m in range(nblk)]
-        order = jnp.arange(nblk, dtype=jnp.int32)
-    info = jnp.concatenate([tile[None].astype(jnp.int32), order])
+        order = jnp.asarray(np.concatenate([np.arange(nblk), place_table(np.full(1, nblk - 1), nblk)[0]]).astype(np.int32))
+    info = jnp.concatenate([tile[None].astype(jnp.int32), stamp_rows[0], stamp_cols[0], order])
+    at_slots = 1 + 2 * stamps
+    at_places = at_slots + nblk
 
     lrow6, lrow1 = row_tables()
     wcol6, wcol1 = column_tables()
-
-    depth = groups * STAMP
-    d0, wp, sp = pl.pallas_call(
+    first, leftm = place_tables()
+    lrow6 = jnp.asarray(lrow6)
+    tables = [jnp.asarray(x) for x in (lrow1, wcol1)]
+    later_tables = [jnp.asarray(x) for x in (stamp_table(), wcol6, first, leftm)]
+
+    def like(xs):
+        return tuple(pltpu.VMEM(x.shape, x.dtype) for x in xs)
+
+    wp, sp, sci, lrow6, lrow1, wcol1 = map(in_vmem, call(
+        functools.partial(load_kernel, n_tile, stamps),
+        "load_and_cut",
+        (
+            pltpu.VMEM((depth, LANES), F32),
+            pltpu.VMEM((depth, LANES), F32),
+            pltpu.VMEM((nblk, rows, LANES), F32),
+            pltpu.VMEM((nrow,) + lrow6.shape[1:], BF16),
+        )
+        + like(tables),
+        [info, science, flags, lrow6] + tables,
+        8,
+        2 * 10**9,
+        [
+            pltpu.VMEM((nblk, rows, LANES), jnp.int32),
+            pltpu.SemaphoreType.DMA((2 * nblk,)),
+            pltpu.SemaphoreType.DMA((nrow + len(tables),)),
+        ],
+        hbm=range(1, 4 + len(tables)),
+    ))
+    d0, mcol, wcol6, first, leftm = map(in_vmem, call(
         functools.partial(science_kernel, n_tile),
-        out_shape=(
-            jax.ShapeDtypeStruct((rows, cols), F32),
-            jax.ShapeDtypeStruct((depth, LANES), F32),
-            jax.ShapeDtypeStruct((depth, LANES), F32),
-        ),
-        in_specs=[SMEM()] * 3 + [VMEM()] * 5,
-        out_specs=(VMEM(), VMEM(), VMEM()),
-        scratch_shapes=[
-            pltpu.VMEM((nblk, rows + 2 * HALO, LANES), F32),
-            pltpu.VMEM((nblk, rows, LANES), F32),
-            pltpu.VMEM((nblk, rows, LANES), F32),
-        ],
-        compiler_params=params(),
-        cost_estimate=pl.CostEstimate(flops=2 * 10**9, bytes_accessed=4 * 2**20, transcendentals=0),
-        name="science_filter",
-    )(info, stamp_rows, stamp_cols, science, edges[:, width:], flags, jnp.asarray(lrow1), jnp.asarray(wcol1))
-
-    first, leftm = place_tables()
-    system = pl.pallas_call(
-        functools.partial(stamp_kernel, n_tile, nblk),
-        out_shape=jax.ShapeDtypeStruct((16, LANES), F32),
-        in_specs=[SMEM()] * 3 + [VMEM()] * (nblk + 5),
-        out_specs=VMEM(),
-        scratch_shapes=[
+        "science_filter",
+        (pltpu.VMEM((rows, cols), F32),) + like(later_tables),
+        [info, sci, science_edge, lrow1, wcol1, blocks[1]] + later_tables,
+        12,
+        2 * 10**9,
+        [pltpu.VMEM((nblk, rows, LANES), F32), pltpu.SemaphoreType.DMA((len(later_tables),))],
+        outside=(5,),
+        hbm=range(6, 6 + len(later_tables)),
+    ))
+
+    def row_filters(slots, r):
+        ins = [info, lrow6, blocks[1] if slots[0] < nblk - 1 else d0] + [blocks[slot] for slot in slots] + [in_vmem(x) for x in r]
+        n = len(ins)
+        return call(
+            functools.partial(rows_kernel, n_tile, at_slots, slots),
+            "template_rows",
+            (pltpu.VMEM((nblk, 6, rows, LANES), BF16),) * 2,
+            ins,
+            12,
+            10**9,
+            aliases={n - 2: 0, n - 1: 1} if r else None,
+            outside=(2,),
+        )
+
+    def column_filters(places, r, q, after):
+        ins = [info] + [in_vmem(x) for x in r] + [wcol6, after] + [in_vmem(x) for x in q]
+        return call(
+            functools.partial(columns_kernel, nblk, at_places, places),
+            "template_columns",
+            pltpu.VMEM((nblk, NB, rows, LANES), F32),
+            ins,
+            12,
+            10**9 * len(places),
+            aliases={5: 0} if q else None,
+            outside=(4,),
+        )
+
+    r = ()
+    for slots in [(0,)] + [(i, i + 1) for i in range(1, nblk - 1, 2)]:
+        r = row_filters(slots, r)
+    state = dict(r=r, q=())
+
+    def more_columns(places):
+        def go(x):
+            state["q"] = (column_filters(places, state["r"], state["q"], x),)
+
+        return go
+
+    def last_rows(x):
+        state["r"] = row_filters((nblk - 1,), state["r"])
+
+    groups_of = [tuple(range(i, i + 2)) for i in range(0, nblk, 2)]
+    more_columns(groups_of[0])(blocks[-2])
+
+    system = call(
+        functools.partial(stamp_kernel, n_tile, nblk, stamps),
+        "stamp_sums",
+        pltpu.VMEM((16, LANES), F32),
+        [info, *blocks, wp, sp, mcol, first, leftm],
+        12,
+        10**9,
+        [
             pltpu.VMEM((nblk + 2, rows + 2 * HALO, LANES), F32),
             pltpu.VMEM((6, groups * PATCH_ROWS, LANES), F32),
             pltpu.VMEM((NB, depth, LANES), F32),
             pltpu.VMEM((96 * 8, LANES), F32),
         ],
-        compiler_params=params(),
-        cost_estimate=pl.CostEstimate(flops=10**9, bytes_accessed=2 * 2**20, transcendentals=0),
-        name="stamp_sums",
-    )(info, stamp_rows, stamp_cols, *blocks, wp, sp, jnp.asarray(stamp_table()), jnp.asarray(first), jnp.asarray(leftm))
-
-    images = pl.pallas_call(
-        functools.partial(images_kernel, n_tile, nblk),
-        out_shape=jax.ShapeDtypeStruct((nblk, NB, rows, LANES), F32),
-        grid=(nblk,),
-        in_specs=[SMEM()] + [VMEM()] * (nblk + 2),
-        out_specs=pl.BlockSpec((1, NB, rows, LANES), lambda m: (m, 0, 0, 0)),
-        scratch_shapes=[
-            pltpu.VMEM((nblk + 2, rows + 2 * HALO, LANES), F32),
-            pltpu.VMEM((nblk, 6, rows, LANES), BF16),
-            pltpu.VMEM((nblk, 6, rows, LANES), BF16),
-        ],
-        compiler_params=params(),
-        cost_estimate=pl.CostEstimate(flops=8 * 10**9, bytes_accessed=16 * 2**20, transcendentals=0),
-        name="filtered_images",
-    )(info, *blocks, jnp.asarray(lrow6), jnp.asarray(wcol6))
-
-    system = all_sum(system, n_epoch)
-
+    )
+    system = all_sum(system, n_epoch, [last_rows] + [more_columns(g) for g in groups_of[1:]])
+
+    step = 2
     detection, coefficients = pl.pallas_call(
-        final_kernel,
+        functools.partial(final_kernel, step),
         out_shape=(
             jax.ShapeDtypeStruct((rows, cols), F32),
             jax.ShapeDtypeStruct((NB,), F32),
         ),
-        grid=(nblk,),
+        grid=(nblk // step,),
         in_specs=[
             VMEM(),
-            pl.BlockSpec((rows, LANES), lambda m: (0, m)),
-            pl.BlockSpec((1, NB, rows, LANES), lambda m: (m, 0, 0, 0)),
+            pl.BlockSpec((rows, step * LANES), lambda m: (0, m)),
+            VMEM(),
         ],
-        out_specs=(pl.BlockSpec((rows, LANES), lambda m: (0, m)), SMEM()),
+        out_specs=(pl.BlockSpec((rows, step * LANES), lambda m: (0, m)), SMEM()),
         scratch_shapes=[pltpu.VMEM((16, LANES), F32)],
-        compiler_params=params(),
+        compiler_params=pltpu.CompilerParams(vmem_limit_bytes=8 * 2**20),
         cost_estimate=pl.CostEstimate(flops=10**8, bytes_accessed=16 * 2**20, transcendentals=0),
         name="solve_subtract",
-    )(system, d0, images)
+    )(system, d0, in_vmem(state["q"][0]))
     return (detection[None], coefficients)
 
 

time: 69.1 us -> 47.5 us (0.69)
  waiting for transfers between devices: 15.7 us -> 1.28 us
  Pallas kernels: 31.5 us -> 25.8 us
  other arithmetic: 4.5 us -> 2.36 us
  starting transfers between devices: 14.3 us -> 15.4 us
    ppermute x4, waiting for transfers between devices: 8.17 us -> 1.22 us  [gather_ring(): fwd = lax.ppermute(fwd, 'epoch', ahead)]
    pallas_call x4 -> x13, Pallas kernels: 31.5 us -> 25.8 us  [the longest x12 22.3 us: call(): pl.pallas_call(kernel, out_shape=out, in_specs=[spec(i, x) for i, x in en...]
    ppermute x3, waiting for transfers between devices: 5.2 us -> 0.03 us  [all_sum(): x = x + lax.ppermute(x, 'epoch', [(j, j ^ 1 << i) for j in range(count)])]
    ppermute x2 -> x3, waiting for transfers between devices: 2.29 us -> 0.03 us  [swap(): return lax.ppermute(x, 'tile', [(0, 1), (1, 0)])]
    ppermute x3, starting transfers between devices: 4.71 us -> 6.15 us  [all_sum(): x = x + lax.ppermute(x, 'epoch', [(j, j ^ 1 << i) for j in range(count)])]
    concatenate x3 -> x1, other arithmetic: 1.59 us -> 0.75 us  [local(): jnp.concatenate([tile[None].astype(jnp.int32), stamp_rows[0], stamp_cols[...]
    add x1, other arithmetic: 0.7 us -> 0.01 us  [all_sum(): x = x + swap(x)]
  transfers between devices with their start and end apart: 12 -> 13, of which waited for: 7 -> 3; matrix products, arithmetic and copies ran while one was open for 3% -> 7% of each run, Pallas kernels for 26% -> 42%
where the time goes in v2:
time: 47.5 us; the launch traced here: 47.2 us
  Pallas kernels  25.8 us (54%)
  starting transfers between devices  15.4 us (32%)
  other arithmetic  2.36 us (5%)
  local copies, waits for them, and re-layouts  1.61 us (3%)
  waiting for transfers between devices  1.28 us (3%)
  between operations  0.79 us (2%)
    pallas_call x12, Pallas kernels, call(): pl.pallas_call(kernel, out_shape=out, in_specs=[spec(i, x) for i, x in en...  22.3 us
    ppermute x4, starting transfers between devices, gather_ring(): fwd = lax.ppermute(fwd, 'epoch', ahead)  8.06 us
    ppermute x3, starting transfers between devices, all_sum(): x = x + lax.ppermute(x, 'epoch', [(j, j ^ 1 << i) for j in range(count)])  6.15 us
    pallas_call x1, Pallas kernels, local(): pl.pallas_call(functools.partial(final_kernel, step), out_shape=(jax.Shap...  3.42 us
    select_n x2, other arithmetic, edge_of(): return jnp.where(tile == 0, x[-HALO:], x[:HALO])  1.6 us
    ppermute x4, waiting for transfers between devices, gather_ring(): fwd = lax.ppermute(fwd, 'epoch', ahead)  1.22 us
  transfers between devices with their start and end apart: 13, of which 3 were waited for; matrix products, arithmetic and copies ran while one was open for 7% of the time, Pallas kernels for 42%

profile of v2, /device:TPU:0, one launch (start us, length us, event | category | flops | bytes accessed | tf_op | source)
XLA Modules:
  0.0 47.2 jit_solution(16652521418967391459)
XLA Ops:
  1.8 0.9 %constant_dynamic-update-slice_fusion.1 = f32[272,128]{1,0:T(8,128)S(1)} fusion(f32[256,128]{1,0:T(8,128)} %param.13), kind=kLoop, calls=%fused_computation.3 | loop fusion | bytes 262144
  3.4 2.6 %collective-permute-start.1 = (f32[272,128]{1,0:T(8,128)S(1)}, f32[272,128]{1,0:T(8,128)S(1)}, u32[]{:S(2)}, u32[]{:S(2)}) collective-permute-start(f32[272,128]{1,0:T(8,128)S(1)} %constant_dynamic-update-slice_fusion.refs_0_), channel_id=1, source_target_pairs={{0,4},{4,8},{8,12},{12,14},{14,10},{10,6},{6,2},{2,0},{1,5},{5,9},... | collective-permute-start | bytes 417800 | tf_op jit(solution)/shard_map/ppermute | solution.py:424
  6.1 0.9 %slice_select_fusion = f32[16,1024]{1,0:T(8,128)S(1)} fusion(f32[256,1024]{1,0:T(8,128)} %bitcast.8, pred[]{:T(512)S(6)} %eq.4), kind=kLoop, calls=%fused_computation | loop fusion | flops 16384 | bytes 196609 | tf_op jit(solution)/shard_map/jit(_where)/select_n | solution.py:509
  7.2 0.7 %pad_add_fusion.info = s32[49]{0:T(128)S(1)} fusion(s32[16]{0:T(128)S(1)} %dynamic-slice_bitcast_fusion, s32[16]{0:T(128)} %bitcast.10, s32[16]{0:T(128)} %bitcast.11, s32[1]{0:T(128)} %bitcast), kind=kLoop, calls=%fused_computation.4 | loop fusion | flops 147 | bytes 392 | tf_op jit(solution)/shard_map/concatenate | solution.py:522
  8.0 3.3 %load_and_cut.1 = (f32[128,128]{1,0:T(8,128)S(1)}, f32[128,128]{1,0:T(8,128)S(1)}, f32[8,256,128]{2,1,0:T(8,128)S(1)}, bf16[2,768,480]{2,1,0:T(8,128)(2,1)S(1)},...) custom-call(s32[49]{0:T(128)S(1)} %pad_add_fusion.info, f32[256,1024]{1,0:T(8,128)} %bitcast.9, ...), custom_call_target="tpu_custom_call" | custom-call | flops 2000000000 | bytes 1048576 | tf_op jit(solution)/shard_map/load_and_cut/pallas_call | solution.py:482
  11.3 1.9 %collective-permute-start.3 = (f32[272,128]{1,0:T(8,128)S(1)}, f32[272,128]{1,0:T(8,128)S(1)}, u32[]{:S(2)}, u32[]{:S(2)}) collective-permute-start(f32[272,128]{1,0:T(8,128)S(1)} %collective-permute-done.1.after.refs_1_.refs_0_), channel_id=1, source_target_pairs={{0,4},{4,8},{8,12},{12,14},{14,10},{10,6},{6,2},{2,0},{1,5},{5,9},... | collective-permute-start | bytes 417800 | tf_op jit(solution)/shard_map/ppermute | solution.py:424
  13.4 2.5 %science_filter.1 = (f32[256,1024]{1,0:T(8,128)S(1)}, bf16[2,256,768]{2,1,0:T(8,128)(2,1)S(1)}, bf16[3,3,2,256,256]{4,3,2,1,0:T(8,128)(2,1)S(1)}, f32[2,96,128]{2,1,0:T(8,128)S(1)}, f32[16,192]{1,0:T(8,128)S(1)}) custom-call(s32[49]{0:T(128)S(1)} %pad_add_fusion.info, f32[8,256,128]{2,1,0:T(8,128)S(1)} %get-tuple-element.32.sci, ...), custom_call_target="tpu_custom_call" | custom-call | flops 2000000000 | bytes 1048576 | tf_op jit(solution)/shard_map/science_filter/pallas_call | solution.py:482
  15.9 1.1 %template_rows.5 = (bf16[8,6,256,128]{3,2,1,0:T(8,128)(2,1)S(1)}, bf16[8,6,256,128]{3,2,1,0:T(8,128)(2,1)S(1)}) custom-call(s32[49]{0:T(128)S(1)} %pad_add_fusion.info, bf16[2,768,480]{2,1,0:T(8,128)(2,1)S(1)} %get-tuple-element.40.lrow, f32[272,128]{1,0:T(8,128)S(1)} %collective-permute-done.1.after.refs_1_.refs_0_, ...), custom_call_target="tpu_custom_call" | custom-call | flops 1000000000 | bytes 1048576 | tf_op jit(solution)/shard_map/template_rows/pallas_call | solution.py:482
  17.4 1.8 %collective-permute-start.5 = (f32[272,128]{1,0:T(8,128)S(1)}, f32[272,128]{1,0:T(8,128)S(1)}, u32[]{:S(2)}, u32[]{:S(2)}) collective-permute-start(f32[272,128]{1,0:T(8,128)S(1)} %collective-permute-done.3.refs_3_.refs_0_), channel_id=1, source_target_pairs={{0,4},{4,8},{8,12},{12,14},{14,10},{10,6},{6,2},{2,0},{1,5},{5,9},... | collective-permute-start | bytes 417800 | tf_op jit(solution)/shard_map/ppermute | solution.py:424
  19.5 1.2 %template_rows.6 = (bf16[8,6,256,128]{3,2,1,0:T(8,128)(2,1)S(1)}, bf16[8,6,256,128]{3,2,1,0:T(8,128)(2,1)S(1)}) custom-call(s32[49]{0:T(128)S(1)} %pad_add_fusion.info, bf16[2,768,480]{2,1,0:T(8,128)(2,1)S(1)} %get-tuple-element.40.lrow, f32[272,128]{1,0:T(8,128)S(1)} %collective-permute-done.1.after.refs_1_.refs_0_, ...), custom_call_target="tpu_custom_call", output_to_operand_aliasing={{0}: (5, {}), {1}: (6, {})} | custom-call | flops 1000000000 | bytes 1048576 | tf_op jit(solution)/shard_map/template_rows/pallas_call | solution.py:482
  20.7 1.2 %template_rows.7 = (bf16[8,6,256,128]{3,2,1,0:T(8,128)(2,1)S(1)}, bf16[8,6,256,128]{3,2,1,0:T(8,128)(2,1)S(1)}) custom-call(s32[49]{0:T(128)S(1)} %pad_add_fusion.info, bf16[2,768,480]{2,1,0:T(8,128)(2,1)S(1)} %get-tuple-element.40.lrow, f32[272,128]{1,0:T(8,128)S(1)} %collective-permute-done.1.after.refs_1_.refs_0_, ...), custom_call_target="tpu_custom_call", output_to_operand_aliasing={{0}: (5, {}), {1}: (6, {})} | custom-call | flops 1000000000 | bytes 1048576 | tf_op jit(solution)/shard_map/template_rows/pallas_call | solution.py:482
  21.9 0.8 %collective-permute-done.5.refs_5_.refs_0_ = f32[272,128]{1,0:T(8,128)S(1)} collective-permute-done((f32[272,128]{1,0:T(8,128)S(1)}, f32[272,128]{1,0:T(8,128)S(1)}, u32[]{:S(2)}, u32[]{:S(2)}) %collective-permute-start.5) | collective-permute-done | bytes 139296 | tf_op jit(solution)/shard_map/ppermute | solution.py:424
  22.7 1.8 %collective-permute-start.7 = (f32[272,128]{1,0:T(8,128)S(1)}, f32[272,128]{1,0:T(8,128)S(1)}, u32[]{:S(2)}, u32[]{:S(2)}) collective-permute-start(f32[272,128]{1,0:T(8,128)S(1)} %collective-permute-done.5.refs_5_.refs_0_), channel_id=1, source_target_pairs={{0,4},{4,8},{8,12},{12,14},{14,10},{10,6},{6,2},{2,0},{1,5},{5,9},... | collective-permute-start | bytes 417800 | tf_op jit(solution)/shard_map/ppermute | solution.py:424
  24.5 1.2 %template_rows.8 = (bf16[8,6,256,128]{3,2,1,0:T(8,128)(2,1)S(1)}, bf16[8,6,256,128]{3,2,1,0:T(8,128)(2,1)S(1)}) custom-call(s32[49]{0:T(128)S(1)} %pad_add_fusion.info, bf16[2,768,480]{2,1,0:T(8,128)(2,1)S(1)} %get-tuple-element.40.lrow, f32[272,128]{1,0:T(8,128)S(1)} %collective-permute-done.1.after.refs_1_.refs_0_, ...), custom_call_target="tpu_custom_call", output_to_operand_aliasing={{0}: (5, {}), {1}: (6, {})} | custom-call | flops 1000000000 | bytes 1048576 | tf_op jit(solution)/shard_map/template_rows/pallas_call | solution.py:482
  25.7 2.0 %template_columns.4.refs_1_ = f32[8,12,256,128]{3,2,1,0:T(8,128)S(1)} custom-call(s32[49]{0:T(128)S(1)} %pad_add_fusion.info, bf16[8,6,256,128]{3,2,1,0:T(8,128)(2,1)S(1)} %get-tuple-element.47.refs_1_.rhi, bf16[8,6,256,128]{3,2,1,0:T(8,128)(2,1)S(1)} %get-tuple-element.48.refs_2_.rlo, bf16[3,3,2,256,256]{4,3,2,1,0:T(8,128)(2,1)S(1)} %get-tuple-element.51.wcol, ...), custom_call_target="tpu_custom_call" | custom-call | flops 2000000000 | bytes 1048576 | tf_op jit(solution)/shard_map/template_columns/pallas_call | solution.py:482
  27.8 2.6 %stamp_sums.1 = f32[16,128]{1,0:T(8,128)S(1)} custom-call(s32[49]{0:T(128)S(1)} %pad_add_fusion.info, f32[272,128]{1,0:T(8,128)S(1)} %constant_dynamic-update-slice_fusion.refs_0_, f32[272,128]{1,0:T(8,128)S(1)} %collective-permute-done.1.after.refs_1_.refs_0_, f32[272,128]{1,0:T(8,128)S(1)} %collective-permute-done.2.refs_2_.refs_1_, ...), custom_call_target="tpu_custom_call" | custom-call | flops 1000000000 | bytes 1048576 | tf_op jit(solution)/shard_map/stamp_sums/pallas_call | solution.py:482
  30.4 1.2 %template_rows.9 = (bf16[8,6,256,128]{3,2,1,0:T(8,128)(2,1)S(1)}, bf16[8,6,256,128]{3,2,1,0:T(8,128)(2,1)S(1)}) custom-call(s32[49]{0:T(128)S(1)} %pad_add_fusion.info, bf16[2,768,480]{2,1,0:T(8,128)(2,1)S(1)} %get-tuple-element.40.lrow, f32[256,1024]{1,0:T(8,128)S(1)} %get-tuple-element.39.after.d0, ...), custom_call_target="tpu_custom_call", output_to_operand_aliasing={{0}: (4, {}), {1}: (5, {})} | custom-call | flops 1000000000 | bytes 1048576 | tf_op jit(solution)/shard_map/template_rows/pallas_call | solution.py:482
  31.6 1.8 %collective-permute-start.10 = (f32[16,128]{1,0:T(8,128)S(1)}, f32[16,128]{1,0:T(8,128)S(1)}, u32[]{:S(2)}, u32[]{:S(2)}) collective-permute-start(f32[16,128]{1,0:T(8,128)S(1)} %add.16.refs_0_), channel_id=1, source_target_pairs={{0,2},{2,0},{4,6},{6,4},{8,10},{10,8},{12,14},{14,12},{1,3},{3,1},... | collective-permute-start | bytes 24584 | tf_op jit(solution)/shard_map/ppermute | solution.py:456
  33.4 2.0 %template_columns.5.refs_1_ = f32[8,12,256,128]{3,2,1,0:T(8,128)S(1)} custom-call(s32[49]{0:T(128)S(1)} %pad_add_fusion.info, bf16[8,6,256,128]{3,2,1,0:T(8,128)(2,1)S(1)} %get-tuple-element.49.rhi, bf16[8,6,256,128]{3,2,1,0:T(8,128)(2,1)S(1)} %get-tuple-element.50.rlo, ...), custom_call_target="tpu_custom_call", output_to_operand_aliasing={{}: (5, {})} | custom-call | flops 2000000000 | bytes 1048576 | tf_op jit(solution)/shard_map/template_columns/pallas_call | solution.py:482
  35.4 1.7 %collective-permute-start.11 = (f32[16,128]{1,0:T(8,128)S(1)}, f32[16,128]{1,0:T(8,128)S(1)}, u32[]{:S(2)}, u32[]{:S(2)}) collective-permute-start(f32[16,128]{1,0:T(8,128)S(1)} %add.17.refs_0_), channel_id=1, source_target_pairs={{0,4},{2,6},{4,0},{6,2},{8,12},{10,14},{12,8},{14,10},{1,5},{3,7},... | collective-permute-start | bytes 24584 | tf_op jit(solution)/shard_map/ppermute | solution.py:456
  37.1 2.0 %template_columns.6.refs_1_ = f32[8,12,256,128]{3,2,1,0:T(8,128)S(1)} custom-call(s32[49]{0:T(128)S(1)} %pad_add_fusion.info, bf16[8,6,256,128]{3,2,1,0:T(8,128)(2,1)S(1)} %get-tuple-element.49.rhi, bf16[8,6,256,128]{3,2,1,0:T(8,128)(2,1)S(1)} %get-tuple-element.50.rlo, ...), custom_call_target="tpu_custom_call", output_to_operand_aliasing={{}: (5, {})} | custom-call | flops 2000000000 | bytes 1048576 | tf_op jit(solution)/shard_map/template_columns/pallas_call | solution.py:482
  39.1 2.7 %collective-permute-start.12 = (f32[16,128]{1,0:T(8,128)S(1)}, f32[16,128]{1,0:T(8,128)S(1)}, u32[]{:S(2)}, u32[]{:S(2)}) collective-permute-start(f32[16,128]{1,0:T(8,128)S(1)} %add.18.refs_0_), channel_id=1, source_target_pairs={{0,8},{2,10},{4,12},{6,14},{8,0},{10,2},{12,4},{14,6},{1,9},{3,11}... | collective-permute-start | bytes 24584 | tf_op jit(solution)/shard_map/ppermute | solution.py:456
  41.8 2.0 %template_columns.7.images = f32[8,12,256,128]{3,2,1,0:T(8,128)S(1)} custom-call(s32[49]{0:T(128)S(1)} %pad_add_fusion.info, bf16[8,6,256,128]{3,2,1,0:T(8,128)(2,1)S(1)} %get-tuple-element.49.rhi, bf16[8,6,256,128]{3,2,1,0:T(8,128)(2,1)S(1)} %get-tuple-element.50.rlo, ...), custom_call_target="tpu_custom_call", output_to_operand_aliasing={{}: (5, {})} | custom-call | flops 2000000000 | bytes 1048576 | tf_op jit(solution)/shard_map/template_columns/pallas_call | solution.py:482
  43.8 3.4 %solve_subtract.1 = (f32[256,1024]{1,0:T(8,128)}, f32[12]{0:T(128)}) custom-call(f32[16,128]{1,0:T(8,128)S(1)} %add.19.system, f32[256,1024]{1,0:T(8,128)S(1)} %get-tuple-element.39.after.d0, f32[8,12,256,128]{3,2,1,0:T(8,128)S(1)} %template_columns.7.images), custom_call_target="tpu_custom_call" | custom-call | flops 100000000 | bytes 16777216 | tf_op jit(solution)/shard_map/solve_subtract/pallas_call | solution.py:629
  (25 shorter events, 3.1 us)
Async XLA Ops:
  1.4 2.1 %collective-permute-start = (f32[16,128]{1,0:T(8,128)S(1)}, f32[16,128]{1,0:T(8,128)S(1)}, u32[]{:S(2)}, u32[]{:S(2)}) collective-permute-start(f32[16,128]{1,0:T(8,128)S(1)} %slice_select_fusion.1), channel_id=1, source_target_pairs={{0,1},{1,0},{2,3},{3,2},{4,5},{5,4},{6,7},{7,6},{8,9},{9,8},{10,11... | collective-permute-start | bytes 24584 | tf_op jit(solution)/shard_map/ppermute | solution.py:414
  3.4 7.8 %collective-permute-start.1 = (f32[272,128]{1,0:T(8,128)S(1)}, f32[272,128]{1,0:T(8,128)S(1)}, u32[]{:S(2)}, u32[]{:S(2)}) collective-permute-start(f32[272,128]{1,0:T(8,128)S(1)} %constant_dynamic-update-slice_fusion.refs_0_), channel_id=1, source_target_pairs={{0,4},{4,8},{8,12},{12,14},{14,10},{10,6},{6,2},{2,0},{1,5},{5,9},... | collective-permute-start | bytes 417800 | tf_op jit(solution)/shard_map/ppermute | solution.py:424
  6.1 7.1 %collective-permute-start.2 = (f32[272,128]{1,0:T(8,128)S(1)}, f32[272,128]{1,0:T(8,128)S(1)}, u32[]{:S(2)}, u32[]{:S(2)}) collective-permute-start(f32[272,128]{1,0:T(8,128)S(1)} %constant_dynamic-update-slice_fusion.refs_0_), channel_id=1, source_target_pairs={{4,0},{8,4},{12,8},{14,12},{10,14},{6,10},{2,6},{0,2},{5,1},{9,5},... | collective-permute-start | bytes 417800 | tf_op jit(solution)/shard_map/ppermute | solution.py:427
  6.9 6.4 %collective-permute-start.8 = (f32[16,1024]{1,0:T(8,128)S(1)}, f32[16,1024]{1,0:T(8,128)S(1)}, u32[]{:S(2)}, u32[]{:S(2)}) collective-permute-start(f32[16,1024]{1,0:T(8,128)S(1)} %slice_select_fusion), channel_id=1, source_target_pairs={{0,1},{1,0},{2,3},{3,2},{4,5},{5,4},{6,7},{7,6},{8,9},{9,8},{10,11... | collective-permute-start | bytes 196616 | tf_op jit(solution)/shard_map/ppermute | solution.py:414
  11.3 6.1 %collective-permute-start.3 = (f32[272,128]{1,0:T(8,128)S(1)}, f32[272,128]{1,0:T(8,128)S(1)}, u32[]{:S(2)}, u32[]{:S(2)}) collective-permute-start(f32[272,128]{1,0:T(8,128)S(1)} %collective-permute-done.1.after.refs_1_.refs_0_), channel_id=1, source_target_pairs={{0,4},{4,8},{8,12},{12,14},{14,10},{10,6},{6,2},{2,0},{1,5},{5,9},... | collective-permute-start | bytes 417800 | tf_op jit(solution)/shard_map/ppermute | solution.py:424
  13.2 6.1 %collective-permute-start.4 = (f32[272,128]{1,0:T(8,128)S(1)}, f32[272,128]{1,0:T(8,128)S(1)}, u32[]{:S(2)}, u32[]{:S(2)}) collective-permute-start(f32[272,128]{1,0:T(8,128)S(1)} %collective-permute-done.2.refs_2_.refs_1_), channel_id=1, source_target_pairs={{4,0},{8,4},{12,8},{14,12},{10,14},{6,10},{2,6},{0,2},{5,1},{9,5},... | collective-permute-start | bytes 417800 | tf_op jit(solution)/shard_map/ppermute | solution.py:427
  17.4 5.3 %collective-permute-start.5 = (f32[272,128]{1,0:T(8,128)S(1)}, f32[272,128]{1,0:T(8,128)S(1)}, u32[]{:S(2)}, u32[]{:S(2)}) collective-permute-start(f32[272,128]{1,0:T(8,128)S(1)} %collective-permute-done.3.refs_3_.refs_0_), channel_id=1, source_target_pairs={{0,4},{4,8},{8,12},{12,14},{14,10},{10,6},{6,2},{2,0},{1,5},{5,9},... | collective-permute-start | bytes 417800 | tf_op jit(solution)/shard_map/ppermute | solution.py:424
  19.2 5.3 %collective-permute-start.6 = (f32[272,128]{1,0:T(8,128)S(1)}, f32[272,128]{1,0:T(8,128)S(1)}, u32[]{:S(2)}, u32[]{:S(2)}) collective-permute-start(f32[272,128]{1,0:T(8,128)S(1)} %collective-permute-done.4.refs_4_.refs_1_), channel_id=1, source_target_pairs={{4,0},{8,4},{12,8},{14,12},{10,14},{6,10},{2,6},{0,2},{5,1},{9,5},... | collective-permute-start | bytes 417800 | tf_op jit(solution)/shard_map/ppermute | solution.py:427
  22.7 5.1 %collective-permute-start.7 = (f32[272,128]{1,0:T(8,128)S(1)}, f32[272,128]{1,0:T(8,128)S(1)}, u32[]{:S(2)}, u32[]{:S(2)}) collective-permute-start(f32[272,128]{1,0:T(8,128)S(1)} %collective-permute-done.5.refs_5_.refs_0_), channel_id=1, source_target_pairs={{0,4},{4,8},{8,12},{12,14},{14,10},{10,6},{6,2},{2,0},{1,5},{5,9},... | collective-permute-start | bytes 417800 | tf_op jit(solution)/shard_map/ppermute | solution.py:424
  30.4 1.2 %collective-permute-start.9 = (f32[16,128]{1,0:T(8,128)S(1)}, f32[16,128]{1,0:T(8,128)S(1)}, u32[]{:S(2)}, u32[]{:S(2)}) collective-permute-start(f32[16,128]{1,0:T(8,128)S(1)} %stamp_sums.1), channel_id=1, source_target_pairs={{0,1},{1,0},{2,3},{3,2},{4,5},{5,4},{6,7},{7,6},{8,9},{9,8},{10,11... | collective-permute-start | bytes 24584 | tf_op jit(solution)/shard_map/ppermute | solution.py:414
  31.6 3.8 %collective-permute-start.10 = (f32[16,128]{1,0:T(8,128)S(1)}, f32[16,128]{1,0:T(8,128)S(1)}, u32[]{:S(2)}, u32[]{:S(2)}) collective-permute-start(f32[16,128]{1,0:T(8,128)S(1)} %add.16.refs_0_), channel_id=1, source_target_pairs={{0,2},{2,0},{4,6},{6,4},{8,10},{10,8},{12,14},{14,12},{1,3},{3,1},... | collective-permute-start | bytes 24584 | tf_op jit(solution)/shard_map/ppermute | solution.py:456
  35.4 3.7 %collective-permute-start.11 = (f32[16,128]{1,0:T(8,128)S(1)}, f32[16,128]{1,0:T(8,128)S(1)}, u32[]{:S(2)}, u32[]{:S(2)}) collective-permute-start(f32[16,128]{1,0:T(8,128)S(1)} %add.17.refs_0_), channel_id=1, source_target_pairs={{0,4},{2,6},{4,0},{6,2},{8,12},{10,14},{12,8},{14,10},{1,5},{3,7},... | collective-permute-start | bytes 24584 | tf_op jit(solution)/shard_map/ppermute | solution.py:456
  39.1 4.6 %collective-permute-start.12 = (f32[16,128]{1,0:T(8,128)S(1)}, f32[16,128]{1,0:T(8,128)S(1)}, u32[]{:S(2)}, u32[]{:S(2)}) collective-permute-start(f32[16,128]{1,0:T(8,128)S(1)} %add.18.refs_0_), channel_id=1, source_target_pairs={{0,8},{2,10},{4,12},{6,14},{8,0},{10,2},{12,4},{14,6},{1,9},{3,11}... | collective-permute-start | bytes 24584 | tf_op jit(solution)/shard_map/ppermute | solution.py:456

commit v3 on v2

v3 whole, which is shorter than its diff:
```python
import functools

import jax
import jax.numpy as jnp
import numpy as np
from jax import lax
from jax.experimental import pallas as pl
from jax.experimental.pallas import tpu as pltpu
from jax.sharding import PartitionSpec as P

STAMP = 32
HALF = 7
TAPS = 15
SIGMAS = (1.0, 2.0, 3.5)
NB = 12
LANES = 128
HALO = 16
WIN = LANES + 2 * HALO
PATCH_ROWS = 48
F32 = jnp.float32
BF16 = jnp.bfloat16
LIMIT = 56 * 1024 * 1024


def split_np(a):
    a = np.asarray(a, np.float32)
    hi = a.astype(BF16)
    lo = (a - hi.astype(np.float32)).astype(BF16)
    return hi, lo


def profiles():
    offsets = np.arange(TAPS, dtype=np.float64) - HALF
    rows = []
    for sigma in SIGMAS:
        gauss = np.exp(-offsets * offsets / (2.0 * sigma * sigma))
        gauss = gauss / gauss.sum()
        rows += [gauss, gauss * offsets / HALF]
    return np.stack(rows)


def psf_profile():
    offsets = np.arange(TAPS, dtype=np.float64) - HALF
    gauss = np.exp(-offsets * offsets / 4.5)
    return gauss / gauss.sum()


def band(profile, size):
    out = np.zeros((size, size))
    for shift in range(TAPS):
        out += profile[shift] * np.eye(size, k=shift - HALF)
    return out


def three_bands(size):
    psf = band(psf_profile(), size)
    return [psf @ band(p, size) for p in profiles()], psf


def pick(matrix, rows, cols):
    cols = np.asarray(cols)
    ok = (cols >= 0) & (cols < matrix.shape[1])
    out = matrix[np.asarray(rows)[:, None], np.clip(cols, 0, matrix.shape[1] - 1)[None, :]]
    return np.where(ok[None, :], out, 0.0)


def starts():
    return (0, LANES, 2 * LANES)


def row_tables():
    size = 3 * LANES
    ops, psf = three_bands(size)

    def stack(ms):
        out = []
        for start in starts():
            rows = np.arange(LANES) + start
            cols = np.arange(WIN) + start - HALO
            hi, lo = split_np(np.concatenate([pick(m, rows, cols) for m in ms], axis=0))
            out.append(np.concatenate([hi, hi, lo], axis=1))
        return np.stack(out)

    return stack(ops), stack([psf])


def column_tables():
    size = 3 * LANES
    ops, psf = three_bands(size)
    lane = np.arange(LANES)

    def own(matrix, start):
        return split_np(pick(matrix, lane + start, lane + start).T)

    def rim(matrix, start):
        side = np.where(lane < 64, start + LANES + lane, start - LANES + lane)
        return split_np(pick(matrix, lane + start, side).T)

    def model(matrix, start):
        hi, lo = own(matrix, start)
        rhi, rlo = rim(matrix, start)
        packed = np.zeros_like(rhi)
        for at in list(range(2 * HALF)) + list(range(LANES - 2 * HALF, LANES)):
            packed[at] = rhi[at]
            packed[(at + 64) % LANES] = rlo[at]
            packed[(at + 96) % LANES] = rhi[at]
        return np.stack([np.concatenate([hi, hi]), np.concatenate([lo, packed])])

    def science(start):
        return np.stack([np.concatenate(p) for p in zip(own(psf, start), rim(psf, start))])

    models = [
        [np.concatenate([model(ops[2 * s], start), model(ops[2 * s + 1], start)], axis=2) for s in range(3)]
        for start in starts()
    ]
    return np.array(models), np.stack([science(start) for start in starts()])


def stamp_table():
    prof = profiles()
    out = np.zeros((256, 6, LANES))
    for q in range(4):
        for c in range(STAMP):
            for v in range(TAPS):
                out[q * 64 + c + v, :, q * STAMP + c] = prof[:, v]
    return np.stack(split_np(out.reshape(256, 6 * LANES)))


def dot(a, b):
    return jnp.dot(a, b, preferred_element_type=F32)


def split(x):
    hi = x.astype(BF16)
    lo = (x - hi.astype(F32)).astype(BF16)
    return hi, lo


def stack3(x):
    hi, lo = split(x)
    return jnp.concatenate([hi, lo, hi], axis=0)


def params(**kw):
    return pltpu.CompilerParams(vmem_limit_bytes=LIMIT, **kw)


VMEM = functools.partial(pl.BlockSpec, memory_space=pltpu.VMEM)
SMEM = functools.partial(pl.BlockSpec, memory_space=pltpu.SMEM)


def row_index(shape):
    return lax.broadcasted_iota(jnp.int32, shape, len(shape) - 2)


def lane_index(shape):
    return lax.broadcasted_iota(jnp.int32, shape, len(shape) - 1)


def ring_place(step, count):
    me = lax.axis_index("epoch")
    at = jnp.where(lax.rem(me, 2) == 0, me // 2, count - 1 - me // 2)
    at = lax.rem(at + step + count, count)
    return jnp.where(at < count // 2, 2 * at, 2 * (count - 1 - at) + 1)


def slot_block(slot, nblk, ring):
    if not ring:
        return jnp.int32(slot)
    step = (slot + 1) // 2
    return ring_place(step if slot % 2 == 0 else -step, nblk)


def place_block(place, nblk, ring):
    return lax.rem(slot_block(nblk - 1, nblk, ring) + 2 + place, nblk)


def variant(tile, b, n_tile, nrow):
    v = jnp.int32(1)
    if b == 0:
        v = jnp.where(tile == 0, 0, v)
    if b == nrow - 1:
        v = jnp.where(tile == n_tile - 1, 2, v)
    return v


def window_rows(tile, b, n_tile, nrow, own, edge):
    size = nrow * LANES
    low, high = b * LANES - HALO, (b + 1) * LANES + HALO
    parts = []
    if low < 0:
        parts.append(jnp.where(tile == 0, 0.0, edge()))
    parts.append(own(max(low, 0), min(high, size)))
    if high > size:
        parts.append(jnp.where(tile == n_tile - 1, 0.0, edge()))
    return jnp.concatenate(parts, axis=0)


def science_kernel(n_tile, sci, edge, lrow, wcol, after, *refs):
    count = len(refs) // 2 - 1
    d0, mid, sems = refs[count], refs[-2], refs[-1]
    copies = [pltpu.make_async_copy(refs[i], refs[count + 1 + i], sems.at[i]) for i in range(count)]
    for copy in copies:
        copy.start()
    tile = lax.axis_index("tile")
    nblk, rows = sci.shape[:2]
    nrow = rows // LANES
    for b in range(nrow):
        left = lrow[variant(tile, b, n_tile, nrow)]
        for m in range(0, nblk, 2):

            def own(lo, hi):
                return jnp.concatenate([sci[m, lo:hi, :], sci[m + 1, lo:hi, :]], axis=1)

            x = window_rows(tile, b, n_tile, nrow, own, lambda: edge[:, m * LANES : (m + 2) * LANES])
            y = dot(left, stack3(x))
            mid[m, b * LANES : (b + 1) * LANES, :] = y[:, :LANES]
            mid[m + 1, b * LANES : (b + 1) * LANES, :] = y[:, LANES:]
    lane = lane_index((rows, LANES))
    for m in range(nblk):
        v = 0 if m == 0 else (2 if m == nblk - 1 else 1)
        rim = jnp.where(lane < 64, mid[min(m + 1, nblk - 1)], mid[max(m - 1, 0)])
        hi, lo = split(jnp.concatenate([mid[m], rim], axis=1))
        d0[:, m * LANES : (m + 1) * LANES] = dot(hi, wcol[v, 0]) + dot(lo, wcol[v, 0]) + dot(hi, wcol[v, 1])
    for copy in copies:
        copy.wait()


def load_kernel(n_tile, *refs):
    half = len(refs) // 2
    after, sci, flags, lrow, *tables = refs[:half]
    sb, fb, lout, *outs = refs[half:-1]
    sems = refs[-1]
    tile = lax.axis_index("tile")
    nblk, rows = sb.shape[:2]
    nrow = rows // LANES
    pairs = []
    for m in range(nblk):
        piece = slice(m * LANES, (m + 1) * LANES)
        pairs += [(sci.at[:, piece], sb.at[m]), (flags.at[:, piece], fb.at[m])]
    pairs += [(lrow.at[variant(tile, b, n_tile, nrow)], lout.at[b]) for b in range(nrow)]
    pairs += list(zip(tables, outs))
    copies = [pltpu.make_async_copy(a, b, sems.at[i]) for i, (a, b) in enumerate(pairs)]
    for copy in copies:
        copy.start()
    for copy in copies:
        copy.wait()


def cut_kernel(info, sb, fb, after, wp, sp):
    stamps = info.shape[0] // 2
    nblk = sb.shape[0]
    lane = lane_index((STAMP, LANES))
    for g in range(stamps // 4):
        w = jnp.zeros((STAMP, LANES), F32)
        s = jnp.zeros((STAMP, LANES), F32)
        for q in range(4):
            top = info[g * 4 + q]
            left = info[stamps + g * 4 + q]
            blk = left // LANES
            off = left - blk * LANES
            nxt = jnp.minimum(blk + 1, nblk - 1)
            shift = lax.rem(q * STAMP - off + LANES, LANES)
            near = lane < q * STAMP - off + LANES
            here = (lane >= q * STAMP) & (lane < (q + 1) * STAMP)

            def window(ref):
                a = pltpu.roll(ref[blk, pl.ds(top, STAMP), :], shift, 1)
                b = pltpu.roll(ref[nxt, pl.ds(top, STAMP), :], shift, 1)
                return jnp.where(near, a, b)

            w = jnp.where(here & (window(fb) == 0), 1.0, w)
            s = jnp.where(here, window(sb), s)
        wp[g * STAMP : (g + 1) * STAMP, :] = w
        sp[g * STAMP : (g + 1) * STAMP, :] = jnp.where(w > 0.0, s, 0.0)


def put_block(n_tile, block, at, t):
    tile = lax.axis_index("tile")
    rows = block.shape[0] - HALO
    e = block[rows:, :]
    t[at + 1, 0:HALO, :] = jnp.where(tile == 0, 0.0, e)
    t[at + 1, HALO : HALO + rows, :] = block[0:rows, :]
    t[at + 1, HALO + rows :, :] = jnp.where(tile == n_tile - 1, 0.0, e)


def stamp_kernel(n_tile, nblk, ring, info, last, t_in, wp, sp, mcol, after, system, t, y, images):
    stamps = info.shape[0] // 2
    put_block(n_tile, last, slot_block(nblk - 1, nblk, ring), t)
    groups = stamps // 4
    lane = lane_index((PATCH_ROWS, LANES))
    prof = profiles()
    xs = []
    for g in range(groups):
        halves = []
        for pair in range(2):
            parts = []
            for h in range(2):
                j = g * 4 + pair * 2 + h
                start = info[stamps + j] + (LANES - HALF)
                blk = start // LANES
                off = start - blk * LANES
                shift = lax.rem(64 * h - off + LANES, LANES)
                rows = pl.ds(info[j] + (HALO - HALF), PATCH_ROWS)
                a = pltpu.roll(t[blk, rows, :], shift, 1)
                b = pltpu.roll(t[blk + 1, rows, :], shift, 1)
                parts.append(jnp.where(lane < 64 * h - off + LANES, a, b))
            halves.append(jnp.where(lane < 64, parts[0], parts[1]))
        xs.append(jnp.concatenate(halves, axis=1))
    hi, lo = split(jnp.concatenate(xs, axis=0))
    both = jnp.concatenate([hi, lo], axis=0)
    depth = groups * PATCH_ROWS
    for p in range(0, 6, 2):
        piece = slice(p * LANES, (p + 2) * LANES)
        main = dot(both, mcol[0, :, piece])
        total = main[:depth] + main[depth:] + dot(hi, mcol[1, :, piece])
        y[p] = total[:, :LANES]
        y[p + 1] = total[:, LANES:]
    for s in range(3):
        gauss = prof[2 * s]
        for j in range(2):
            for g in range(groups):
                base = g * PATCH_ROWS

                def at(o):
                    return y[2 * s + j, base + HALF + o : base + HALF + o + STAMP, :]

                even = at(0) * np.float32(gauss[HALF])
                odd = None
                for d in range(1, HALF + 1):
                    up, down = at(d), at(-d)
                    even = even + (up + down) * np.float32(gauss[HALF + d])
                    term = (up - down) * np.float32(gauss[HALF + d] * d / HALF)
                    odd = term if odd is None else odd + term
                images[4 * s + 2 * j, g * STAMP : (g + 1) * STAMP, :] = even
                images[4 * s + 2 * j + 1, g * STAMP : (g + 1) * STAMP, :] = odd
    depth = groups * STAMP
    row = row_index((8, LANES))
    lane = lane_index((8, LANES))
    zero = jnp.zeros((8, LANES), F32)
    tiles = [[zero, zero] for _ in range(NB + 1)]

    def collect(k, l, x):
        tiles[l][k // 8] = jnp.where(row == k % 8, x, tiles[l][k // 8])

    w = wp[...]
    for k in range(NB):
        weighted = w * images[k]
        for l in range(k, NB + 1):
            prod = weighted * images[l] if l < NB else sp[...] * images[k]
            x = jnp.sum(prod.reshape(depth // 8, 8, LANES), axis=0)
            for d in (4, 2, 1):
                x = x + pltpu.roll(x, d, 0)
            collect(k, l, x)
            if k < l < NB:
                collect(l, k, x)
    for h in range(2):
        out = zero
        for l in range(NB + 1):
            out = jnp.where(lane == l, jnp.sum(tiles[l][h], axis=1, keepdims=True), out)
        system[h * 8 : (h + 1) * 8, :] = out


def rows_kernel(n_tile, slots, ring, store, lrow, after, *refs):
    blocks = refs[: len(slots)]
    rhi, rlo = refs[-3:-1] if store else refs[-2:]
    tile = lax.axis_index("tile")
    nblk, _, rows = rhi.shape[:3]
    nrow = rows // LANES
    places = [slot_block(slot, nblk, ring) for slot in slots]
    if store:
        t = refs[-1]
        if slots[0] == 0:
            t[0] = jnp.zeros(t.shape[1:], F32)
            t[nblk + 1] = jnp.zeros(t.shape[1:], F32)
        for block, at in zip(blocks, places):
            put_block(n_tile, block, at, t)
    for b in range(nrow):
        xs = [
            window_rows(tile, b, n_tile, nrow, lambda lo, hi: block[lo:hi, :], lambda: block[rows:, :])
            for block in blocks
        ]
        hi, lo = split(dot(lrow[b], stack3(jnp.concatenate(xs, axis=1) if len(xs) > 1 else xs[0])))
        for h, at in enumerate(places):
            for p in range(6):
                piece = (slice(p * LANES, (p + 1) * LANES), slice(h * LANES, (h + 1) * LANES))
                rhi[at, p, b * LANES : (b + 1) * LANES, :] = hi[piece]
                rlo[at, p, b * LANES : (b + 1) * LANES, :] = lo[piece]


def columns_kernel(nblk, places, ring, rhi, rlo, wcol, after, *refs):
    out = refs[-1]
    rows = rhi.shape[2]
    lane = lane_index((2 * rows, LANES))
    reach = 2 * HALF
    in_low = (lane >= 96 - reach) & (lane < 96 + reach)
    in_high = (lane >= 64 - reach) & (lane < 64 + reach)
    for place in places:
        m = place_block(place, nblk, ring)
        v = jnp.where(m == 0, 0, jnp.where(m == nblk - 1, 2, 1))
        after = jnp.minimum(m + 1, nblk - 1)
        before = jnp.maximum(m - 1, 0)
        for s in range(3):

            def get(ref, i):
                return ref[i, 2 * s : 2 * s + 2].reshape(2 * rows, LANES)

            def rim(ref):
                return jnp.where(lane < 64, get(ref, after), get(ref, before))

            high, low, own = rim(rhi), rim(rlo), get(rhi, m)
            packed = jnp.where(in_low, pltpu.roll(low, 96, 1), jnp.where(in_high, pltpu.roll(high, 64, 1), high))
            q = dot(jnp.concatenate([own, get(rlo, m)], axis=1), wcol[v, s, 0])
            q = q + dot(jnp.concatenate([own, packed], axis=1), wcol[v, s, 1])
            for i in range(2):
                for j in range(2):
                    out[m, 4 * s + i + 2 * j] = q[i * rows : (i + 1) * rows, j * LANES : (j + 1) * LANES]


def final_kernel(system, d0, images, detection, coefficients, solved, out, scalars, sems):
    a = system[...]
    row = row_index(a.shape)
    col = [jnp.broadcast_to(a[:, j : j + 1], a.shape) for j in range(NB + 1)]
    trace = col[0][0:1, :]
    for k in range(1, NB):
        trace = trace + col[k][k : k + 1, :]
    ridge = trace * (0.05 / NB)
    for k in range(NB):
        col[k] = jnp.where(row == k, col[k] + ridge, col[k])
    result = jnp.zeros(a.shape, F32)
    for k in range(NB):
        factor = jnp.where(row == k, 0.0, col[k] * (1.0 / col[k][k : k + 1, :]))
        for j in range(k + 1, NB + 1):
            col[j] = col[j] - factor * col[j][k : k + 1, :]
    for k in range(NB):
        result = jnp.where(row == k, col[NB] / col[k], result)
    solved[...] = result
    for k in range(NB):
        scalars[k] = solved[k, 0]
    nblk, _, rows = images.shape[:3]
    parts = sems.shape[0] - 1
    size = rows // parts
    copies = [pltpu.make_async_copy(scalars, coefficients, sems.at[parts])]
    copies[0].start()
    for c in range(parts):
        piece = slice(c * size, (c + 1) * size)
        for m in range(nblk):
            total = d0[piece, m * LANES : (m + 1) * LANES]
            for k in range(NB):
                total = total - solved[k : k + 1, :] * images[m, k, piece, :]
            out[piece, m * LANES : (m + 1) * LANES] = total
        copies.append(pltpu.make_async_copy(out.at[piece], detection.at[piece], sems.at[c]))
        copies[-1].start()
    for copy in copies:
        copy.wait()


def ring_order(count):
    return list(range(0, count, 2)) + list(range(count - 1, 0, -2))


def swap(x):
    return lax.ppermute(x, "tile", [(0, 1), (1, 0)])


def gather_ring(block, count):
    ring = ring_order(count)
    ahead = [(ring[i], ring[(i + 1) % count]) for i in range(count)]
    back = [(t, s) for s, t in ahead]
    out = [block]
    fwd = bwd = block
    for step in range(count // 2):
        if step < count // 2 - 1:
            bwd = lax.ppermute(bwd, "epoch", back)
        fwd = lax.ppermute(fwd, "epoch", ahead)
        out += [fwd, bwd]
    return out[:count]


def all_sum(x, count, beside):
    beside[0](x)
    x = x + swap(x)
    if count & (count - 1):
        for f in beside[1:]:
            f(x)
        return lax.psum(x, "epoch")
    steps = count.bit_length() - 1
    for i in range(steps):
        for f in beside[1 + i :: steps]:
            f(x)
        x = x + lax.ppermute(x, "epoch", [(j, j ^ (1 << i)) for j in range(count)])
    return x


def in_vmem(x):
    return pltpu.with_memory_space_constraint(x, pltpu.VMEM)


ANY = functools.partial(pl.BlockSpec, memory_space=pl.ANY)
HBM = functools.partial(pl.BlockSpec, memory_space=pltpu.HBM)


def call(kernel, name, out, ins, limit, flops, scratch=(), aliases=None, outside=(), hbm=()):
    ins = [pltpu.with_memory_space_constraint(x, pltpu.HBM) if i in hbm else x for i, x in enumerate(ins)]

    def spec(i, x):
        if i in outside:
            return ANY()
        if i in hbm:
            return HBM()
        return SMEM() if x.ndim == 1 else VMEM()

    return pl.pallas_call(
        kernel,
        out_shape=out,
        in_specs=[spec(i, x) for i, x in enumerate(ins)],
        out_specs=jax.tree.map(lambda _: VMEM(), out, is_leaf=lambda x: hasattr(x, "shape")),
        scratch_shapes=scratch,
        input_output_aliases=aliases or {},
        compiler_params=pltpu.CompilerParams(vmem_limit_bytes=limit * 2**20),
        cost_estimate=pl.CostEstimate(flops=flops, bytes_accessed=2**20, transcendentals=0),
        name=name,
    )(*ins)


def local(template, science, flags, stamp_rows, stamp_cols):
    n_tile = lax.axis_size("tile")
    n_epoch = lax.axis_size("epoch")
    rows, width = template.shape
    science, flags = science[0], flags[0]
    cols = science.shape[1]
    nblk = cols // LANES
    nrow = rows // LANES
    stamps = stamp_rows.shape[1]
    groups = stamps // 4
    depth = groups * STAMP
    ring = width == LANES
    tile = lax.axis_index("tile")

    def edge_of(x):
        return jnp.where(tile == 0, x[-HALO:], x[:HALO])

    other = swap(template)
    tall = lax.optimization_barrier(jnp.pad(template, ((0, HALO), (0, 0))))
    tall = lax.dynamic_update_slice(tall, jnp.where(tile == 0, other[:HALO], other[-HALO:]), (rows, 0))
    _, later, stamp_rows, stamp_cols = lax.optimization_barrier((tall, science, stamp_rows, stamp_cols))
    science_edge = swap(edge_of(later))
    if ring:
        blocks = gather_ring(tall, n_epoch)
    else:
        whole = lax.all_gather(tall, "epoch", axis=1, tiled=True)
        blocks = [whole[:, m * LANES : (m + 1) * LANES] for m in range(nblk)]
    info = jnp.concatenate([stamp_rows[0], stamp_cols[0]])

    lrow6, lrow1 = (jnp.asarray(x) for x in row_tables())
    wcol6, wcol1 = (jnp.asarray(x) for x in column_tables())
    tables = [lrow1, wcol1]
    later_tables = [wcol6, jnp.asarray(stamp_table())]

    def like(xs):
        return tuple(pltpu.VMEM(x.shape, x.dtype) for x in xs)

    sci, bad, lrow6, lrow1, wcol1 = map(in_vmem, call(
        functools.partial(load_kernel, n_tile),
        "load",
        (
            pltpu.VMEM((nblk, rows, LANES), F32),
            pltpu.VMEM((nblk, rows, LANES), jnp.int32),
            pltpu.VMEM((nrow,) + lrow6.shape[1:], BF16),
        )
        + like(tables),
        [tall, science, flags, lrow6] + tables,
        2,
        2 * 10**9,
        [pltpu.SemaphoreType.DMA((2 * nblk + nrow + len(tables),))],
        outside=(0,),
        hbm=range(1, 4 + len(tables)),
    ))
    d0, wcol6, mcol = map(in_vmem, call(
        functools.partial(science_kernel, n_tile),
        "science_filter",
        (pltpu.VMEM((rows, cols), F32),) + like(later_tables),
        [sci, science_edge, lrow1, wcol1, blocks[1]] + later_tables,
        12,
        2 * 10**9,
        [pltpu.VMEM((nblk, rows, LANES), F32), pltpu.SemaphoreType.DMA((len(later_tables),))],
        outside=(4,),
        hbm=range(5, 5 + len(later_tables)),
    ))
    wp, sp = map(in_vmem, call(
        cut_kernel,
        "stamp_pixels",
        (pltpu.VMEM((depth, LANES), F32),) * 2,
        [info, sci, bad, blocks[3]],
        4,
        10**9,
        outside=(3,),
    ))

    def row_filters(slots, r, store):
        ins = [lrow6, blocks[1] if store else d0] + [blocks[slot] for slot in slots]
        n = len(ins)
        out = (pltpu.VMEM((nblk, 6, rows, LANES), BF16),) * 2
        if store:
            out += (pltpu.VMEM((nblk + 2, rows + 2 * HALO, LANES), F32),)
        return call(
            functools.partial(rows_kernel, n_tile, slots, ring, store),
            "template_rows",
            out,
            ins + [in_vmem(x) for x in r],
            12,
            10**9,
            aliases={n + i: i for i in range(len(r))},
            outside=(1,),
        )

    def column_filters(places, r, q, after):
        ins = [in_vmem(x) for x in r] + [wcol6, after] + [in_vmem(x) for x in q]
        return call(
            functools.partial(columns_kernel, nblk, places, ring),
            "template_columns",
            pltpu.VMEM((nblk, NB, rows, LANES), F32),
            ins,
            12,
            5 * 10**7 * len(places),
            aliases={4: 0} if q else None,
            outside=(3,),
        )

    r = ()
    for slots in [(0,)] + [(i, i + 1) for i in range(1, nblk - 1, 2)]:
        r = row_filters(slots, r, True)
    padded = r[2]
    state = dict(r=r[:2], q=())

    def more_columns(places):
        def go(x):
            state["q"] = (column_filters(places, state["r"], state["q"], x),)

        return go

    def last_rows(x):
        state["r"] = row_filters((nblk - 1,), state["r"], False)

    more_columns(range(nblk - 4))(blocks[-2])

    system, _ = call(
        functools.partial(stamp_kernel, n_tile, nblk, ring),
        "stamp_sums",
        (pltpu.VMEM((16, LANES), F32), pltpu.VMEM(padded.shape, F32)),
        [info, blocks[-1], in_vmem(padded), wp, sp, mcol, in_vmem(state["q"][0])],
        12,
        10**9,
        [
            pltpu.VMEM((6, groups * PATCH_ROWS, LANES), F32),
            pltpu.VMEM((NB, depth, LANES), F32),
        ],
        aliases={2: 1},
        outside=(6,),
    )
    beside = [last_rows] + [more_columns(range(i, i + 2)) for i in range(nblk - 4, nblk, 2)]
    system = all_sum(system, n_epoch, beside)

    parts = 8
    detection, coefficients = pl.pallas_call(
        final_kernel,
        out_shape=(
            jax.ShapeDtypeStruct((rows, cols), F32),
            jax.ShapeDtypeStruct((NB,), F32),
        ),
        in_specs=[VMEM()] * 3,
        out_specs=(HBM(), HBM()),
        scratch_shapes=[
            pltpu.VMEM((16, LANES), F32),
            pltpu.VMEM((rows, cols), F32),
            pltpu.SMEM((NB,), F32),
            pltpu.SemaphoreType.DMA((parts + 1,)),
        ],
        compiler_params=pltpu.CompilerParams(vmem_limit_bytes=8 * 2**20),
        cost_estimate=pl.CostEstimate(flops=10**8, bytes_accessed=16 * 2**20, transcendentals=0),
        name="solve_subtract",
    )(system, d0, in_vmem(state["q"][0]))
    return (detection[None], coefficients)


def solution(mesh):
    return jax.shard_map(
        local,
        mesh=mesh,
        in_specs=(
            P(("patch", "tile"), "epoch"),
            P(("patch", "epoch"), "tile", None),
            P(("patch", "epoch"), "tile", None),
            P(("patch", "epoch"), "tile"),
            P(("patch", "epoch"), "tile"),
        ),
        out_specs=(P(("patch", "epoch"), "tile", None), P("patch")),
        check_vma=False,
    )
```

time: 47.5 us -> 44.4 us (0.935)
  waiting for transfers between devices: 1.28 us -> 11.3 us
  Pallas kernels: 25.8 us -> 17.2 us
  starting transfers between devices: 15.4 us -> 12.9 us
  other arithmetic: 2.36 us -> 0.97 us
  local copies, waits for them, and re-layouts: 1.61 us -> 0.93 us
    pallas_call x12, Pallas kernels: 22.3 us -> 15.2 us  [call(): pl.pallas_call(kernel, out_shape=out, in_specs=[spec(i, x) for i, x in en...]
    ppermute x4, starting transfers between devices: 8.06 us -> 1.19 us  [gather_ring(): fwd = lax.ppermute(fwd, 'epoch', ahead)]
    ppermute x3, starting transfers between devices: 0.45 us -> 6.25 us  [gather_ring(): bwd = lax.ppermute(bwd, 'epoch', back)]
    ppermute x3, waiting for transfers between devices: 0.03 us -> 4.17 us  [all_sum(): x = x + lax.ppermute(x, 'epoch', [(j, j ^ 1 << i) for j in range(count)])]
    ppermute x4, waiting for transfers between devices: 1.22 us -> 5.26 us  [gather_ring(): fwd = lax.ppermute(fwd, 'epoch', ahead)]
    pallas_call x1, Pallas kernels: 3.42 us -> 1.95 us  [local(): pl.pallas_call(final_kernel, out_shape=(jax.ShapeDtypeStruct((rows, cols)...]
    ppermute x3, waiting for transfers between devices: 0.03 us -> 1.44 us  [swap(): return lax.ppermute(x, 'tile', [(0, 1), (1, 0)])]
    ppermute x3, starting transfers between devices: 6.15 us -> 4.85 us  [all_sum(): x = x + lax.ppermute(x, 'epoch', [(j, j ^ 1 << i) for j in range(count)])]
  transfers between devices with their start and end apart: 13 -> 13, of which waited for: 3 -> 10; matrix products, arithmetic and copies ran while one was open for 7% -> 4% of each run, Pallas kernels for 42% -> 29%
where the time goes in v3:
time: 44.4 us; the launch traced here: 44.2 us
  Pallas kernels  17.2 us (39%)
  starting transfers between devices  12.9 us (29%)
  waiting for transfers between devices  11.3 us (25%)
  other arithmetic  0.97 us (2%)
  between operations  0.94 us (2%)
  local copies, waits for them, and re-layouts  0.93 us (2%)
    pallas_call x12, Pallas kernels, call(): pl.pallas_call(kernel, out_shape=out, in_specs=[spec(i, x) for i, x in en...  15.2 us
    ppermute x3, starting transfers between devices, gather_ring(): bwd = lax.ppermute(bwd, 'epoch', back)  6.25 us
    ppermute x4, waiting for transfers between devices, gather_ring(): fwd = lax.ppermute(fwd, 'epoch', ahead)  5.26 us
    ppermute x3, starting transfers between devices, all_sum(): x = x + lax.ppermute(x, 'epoch', [(j, j ^ 1 << i) for j in range(count)])  4.85 us
    ppermute x3, waiting for transfers between devices, all_sum(): x = x + lax.ppermute(x, 'epoch', [(j, j ^ 1 << i) for j in range(count)])  4.17 us
    pallas_call x1, Pallas kernels, local(): pl.pallas_call(final_kernel, out_shape=(jax.ShapeDtypeStruct((rows, cols)...  1.95 us
    ppermute x3, waiting for transfers between devices, swap(): return lax.ppermute(x, 'tile', [(0, 1), (1, 0)])  1.44 us
    ppermute x4, starting transfers between devices, gather_ring(): fwd = lax.ppermute(fwd, 'epoch', ahead)  1.19 us
  transfers between devices with their start and end apart: 13, of which 10 were waited for; matrix products, arithmetic and copies ran while one was open for 4% of the time, Pallas kernels for 29%

profile of v3, /device:TPU:0, one launch (start us, length us, event | category | flops | bytes accessed | tf_op | source)
XLA Modules:
  0.0 44.2 jit_solution(17346892388998658092)
XLA Ops:
  1.1 0.9 %pad.4 = f32[272,128]{1,0:T(8,128)S(1)} pad(f32[256,128]{1,0:T(8,128)} %param.10, f32[]{:T(128)} %constant.7.clone.1), padding=0_16x0_0 | pad | bytes 270340 | tf_op jit(solution)/shard_map/jit(_pad)/pad | solution.py:544
  2.3 2.9 %collective-permute-start.5 = (f32[272,128]{1,0:T(8,128)S(1)}, f32[272,128]{1,0:T(8,128)S(1)}, u32[]{:S(2)}, u32[]{:S(2)}) collective-permute-start(f32[272,128]{1,0:T(8,128)S(1)} %fusion.refs_0_), channel_id=1, source_target_pairs={{4,0},{8,4},{12,8},{14,12},{10,14},{6,10},{2,6},{0,2},{5,1},{9,5},... | collective-permute-start | bytes 417800 | tf_op jit(solution)/shard_map/ppermute | solution.py:474
  5.3 0.9 %slice_select_fusion = f32[16,1024]{1,0:T(8,128)S(1)} fusion(f32[256,1024]{1,0:T(8,128)} %bitcast.5, pred[]{:T(512)S(6)} %eq.4), kind=kLoop, calls=%fused_computation | loop fusion | flops 16384 | bytes 196609 | tf_op jit(solution)/shard_map/jit(_where)/select_n | solution.py:541
  6.3 2.5 %load.1 = (f32[8,256,128]{2,1,0:T(8,128)S(1)}, s32[8,256,128]{2,1,0:T(8,128)S(1)}, bf16[2,768,480]{2,1,0:T(8,128)(2,1)S(1)}, bf16[3,128,480]{2,1,0:T(8,128)(2,1)S(1)}, bf16[3,2,256,128]{3,2,1,0:T(8,128)(2,1)S(1)}) custom-call(f32[272,128]{1,0:T(8,128)S(1)} %fusion.refs_0_, f32[256,1024]{1,0:T(8,128)} %bitcast.6, s32[256,1024]{1,0:T(8,128)} %bitcast.7, ...), custom_call_target="tpu_custom_call" | custom-call | flops 2000000000 | bytes 1048576 | tf_op jit(solution)/shard_map/load/pallas_call | solution.py:513
  9.3 1.7 %collective-permute-start.6 = (f32[272,128]{1,0:T(8,128)S(1)}, f32[272,128]{1,0:T(8,128)S(1)}, u32[]{:S(2)}, u32[]{:S(2)}) collective-permute-start(f32[272,128]{1,0:T(8,128)S(1)} %collective-permute-done.5.refs_1_), channel_id=1, source_target_pairs={{4,0},{8,4},{12,8},{14,12},{10,14},{6,10},{2,6},{0,2},{5,1},{9,5},... | collective-permute-start | bytes 417800 | tf_op jit(solution)/shard_map/ppermute | solution.py:474
  11.3 2.1 %science_filter.1 = (f32[256,1024]{1,0:T(8,128)S(1)}, bf16[3,3,2,256,256]{4,3,2,1,0:T(8,128)(2,1)S(1)}, bf16[2,256,768]{2,1,0:T(8,128)(2,1)S(1)}) custom-call(f32[8,256,128]{2,1,0:T(8,128)S(1)} %get-tuple-element.45.sb.sci, f32[16,1024]{1,0:T(8,128)S(1)} %collective-permute-done.8.edge, bf16[3,128,480]{2,1,0:T(8,128)(2,1)S(1)} %get-tuple-element.50.lrow, ...), custom_call_target="tpu_custom_call" | custom-call | flops 2000000000 | bytes 1048576 | tf_op jit(solution)/shard_map/science_filter/pallas_call | solution.py:513
  13.9 2.7 %collective-permute-done.2.refs_0_.after = f32[272,128]{1,0:T(8,128)S(1)} collective-permute-done((f32[272,128]{1,0:T(8,128)S(1)}, f32[272,128]{1,0:T(8,128)S(1)}, u32[]{:S(2)}, u32[]{:S(2)}) %collective-permute-start.2) | collective-permute-done | bytes 139296 | tf_op jit(solution)/shard_map/ppermute | solution.py:475
  17.8 1.7 %collective-permute-start.7 = (f32[272,128]{1,0:T(8,128)S(1)}, f32[272,128]{1,0:T(8,128)S(1)}, u32[]{:S(2)}, u32[]{:S(2)}) collective-permute-start(f32[272,128]{1,0:T(8,128)S(1)} %collective-permute-done.6.refs_1_), channel_id=1, source_target_pairs={{4,0},{8,4},{12,8},{14,12},{10,14},{6,10},{2,6},{0,2},{5,1},{9,5},... | collective-permute-start | bytes 417800 | tf_op jit(solution)/shard_map/ppermute | solution.py:474
  19.5 0.9 %stamp_pixels.1 = (f32[128,128]{1,0:T(8,128)S(1)}, f32[128,128]{1,0:T(8,128)S(1)}) custom-call(s32[32]{0:T(128)S(1)} %pad_add_fusion.info, f32[8,256,128]{2,1,0:T(8,128)S(1)} %get-tuple-element.45.sb.sci, s32[8,256,128]{2,1,0:T(8,128)S(1)} %get-tuple-element.46.fb, f32[272,128]{1,0:T(8,128)S(1)} %collective-permute-done.2.refs_0_.after), custom_call_target="tpu_custom_call" | custom-call | flops 1000000000 | bytes 1048576 | tf_op jit(solution)/shard_map/stamp_pixels/pallas_call | solution.py:513
  20.4 1.4 %collective-permute-done.3.refs_0_ = f32[272,128]{1,0:T(8,128)S(1)} collective-permute-done((f32[272,128]{1,0:T(8,128)S(1)}, f32[272,128]{1,0:T(8,128)S(1)}, u32[]{:S(2)}, u32[]{:S(2)}) %collective-permute-start.3) | collective-permute-done | bytes 139296 | tf_op jit(solution)/shard_map/ppermute | solution.py:475
  22.9 0.7 %template_rows.8 = (bf16[8,6,256,128]{3,2,1,0:T(8,128)(2,1)S(1)}, bf16[8,6,256,128]{3,2,1,0:T(8,128)(2,1)S(1)}, f32[10,288,128]{2,1,0:T(8,128)S(1)}) custom-call(bf16[2,768,480]{2,1,0:T(8,128)(2,1)S(1)} %get-tuple-element.34.lrow, f32[272,128]{1,0:T(8,128)S(1)} %collective-permute-done.1.after.refs_0_, ...), custom_call_target="tpu_custom_call", output_to_operand_aliasing={{0}: (4, {}), {1}: (5, {}), {2}: (6, {})} | custom-call | flops 1000000000 | bytes 1048576 | tf_op jit(solution)/shard_map/template_rows/pallas_call | solution.py:513
  23.6 2.1 %template_columns.3.after.refs_0_ = f32[8,12,256,128]{3,2,1,0:T(8,128)S(1)} custom-call(bf16[8,6,256,128]{3,2,1,0:T(8,128)(2,1)S(1)} %get-tuple-element.53.rhi.refs_1_, bf16[8,6,256,128]{3,2,1,0:T(8,128)(2,1)S(1)} %get-tuple-element.54.rlo.refs_2_, bf16[3,3,2,256,256]{4,3,2,1,0:T(8,128)(2,1)S(1)} %get-tuple-element.55.wcol, ...), custom_call_target="tpu_custom_call" | custom-call | flops 200000000 | bytes 1048576 | tf_op jit(solution)/shard_map/template_columns/pallas_call | solution.py:513
  25.7 1.1 %collective-permute-done.4.last.refs_0_ = f32[272,128]{1,0:T(8,128)S(1)} collective-permute-done((f32[272,128]{1,0:T(8,128)S(1)}, f32[272,128]{1,0:T(8,128)S(1)}, u32[]{:S(2)}, u32[]{:S(2)}) %collective-permute-start.4) | collective-permute-done | bytes 139296 | tf_op jit(solution)/shard_map/ppermute | solution.py:475
  26.8 2.2 %stamp_sums.1 = (f32[16,128]{1,0:T(8,128)S(1)}, f32[10,288,128]{2,1,0:T(8,128)S(1)}) custom-call(s32[32]{0:T(128)S(1)} %pad_add_fusion.info, f32[272,128]{1,0:T(8,128)S(1)} %collective-permute-done.4.last.refs_0_, f32[10,288,128]{2,1,0:T(8,128)S(1)} %get-tuple-element.44.t_in, f32[128,128]{1,0:T(8,128)S(1)} %get-tuple-element.47.wp, ...), custom_call_target="tpu_custom_call", output_to_operand_aliasing={{1}: (2, {})} | custom-call | flops 1000000000 | bytes 1048576 | tf_op jit(solution)/shard_map/stamp_sums/pallas_call | solution.py:513
  29.0 1.2 %collective-permute-done.9 = f32[16,128]{1,0:T(8,128)S(1)} collective-permute-done((f32[16,128]{1,0:T(8,128)S(1)}, f32[16,128]{1,0:T(8,128)S(1)}, u32[]{:S(2)}, u32[]{:S(2)}) %collective-permute-start.9) | collective-permute-done | bytes 8224 | tf_op jit(solution)/shard_map/ppermute | solution.py:463
  30.2 1.6 %collective-permute-start.10 = (f32[16,128]{1,0:T(8,128)S(1)}, f32[16,128]{1,0:T(8,128)S(1)}, u32[]{:S(2)}, u32[]{:S(2)}) collective-permute-start(f32[16,128]{1,0:T(8,128)S(1)} %add.14.after), channel_id=1, source_target_pairs={{0,2},{2,0},{4,6},{6,4},{8,10},{10,8},{12,14},{14,12},{1,3},{3,1},... | collective-permute-start | bytes 24584 | tf_op jit(solution)/shard_map/ppermute | solution.py:491
  32.4 1.5 %collective-permute-done.10 = f32[16,128]{1,0:T(8,128)S(1)} collective-permute-done((f32[16,128]{1,0:T(8,128)S(1)}, f32[16,128]{1,0:T(8,128)S(1)}, u32[]{:S(2)}, u32[]{:S(2)}) %collective-permute-start.10) | collective-permute-done | bytes 8224 | tf_op jit(solution)/shard_map/ppermute | solution.py:491
  33.8 1.1 %collective-permute-start.11 = (f32[16,128]{1,0:T(8,128)S(1)}, f32[16,128]{1,0:T(8,128)S(1)}, u32[]{:S(2)}, u32[]{:S(2)}) collective-permute-start(f32[16,128]{1,0:T(8,128)S(1)} %add.15.after), channel_id=1, source_target_pairs={{0,4},{2,6},{4,0},{6,2},{8,12},{10,14},{12,8},{14,10},{1,5},{3,7},... | collective-permute-start | bytes 24584 | tf_op jit(solution)/shard_map/ppermute | solution.py:491
  35.0 1.1 %template_columns.4.refs_0_ = f32[8,12,256,128]{3,2,1,0:T(8,128)S(1)} custom-call(bf16[8,6,256,128]{3,2,1,0:T(8,128)(2,1)S(1)} %get-tuple-element.58.rhi, bf16[8,6,256,128]{3,2,1,0:T(8,128)(2,1)S(1)} %get-tuple-element.59.rlo, bf16[3,3,2,256,256]{4,3,2,1,0:T(8,128)(2,1)S(1)} %get-tuple-element.55.wcol, ...), custom_call_target="tpu_custom_call", output_to_operand_aliasing={{}: (4, {})} | custom-call | flops 100000000 | bytes 1048576 | tf_op jit(solution)/shard_map/template_columns/pallas_call | solution.py:513
  36.1 1.4 %collective-permute-done.11 = f32[16,128]{1,0:T(8,128)S(1)} collective-permute-done((f32[16,128]{1,0:T(8,128)S(1)}, f32[16,128]{1,0:T(8,128)S(1)}, u32[]{:S(2)}, u32[]{:S(2)}) %collective-permute-start.11) | collective-permute-done | bytes 8224 | tf_op jit(solution)/shard_map/ppermute | solution.py:491
  37.5 2.1 %collective-permute-start.12 = (f32[16,128]{1,0:T(8,128)S(1)}, f32[16,128]{1,0:T(8,128)S(1)}, u32[]{:S(2)}, u32[]{:S(2)}) collective-permute-start(f32[16,128]{1,0:T(8,128)S(1)} %add.16), channel_id=1, source_target_pairs={{0,8},{2,10},{4,12},{6,14},{8,0},{10,2},{12,4},{14,6},{1,9},{3,11}... | collective-permute-start | bytes 24584 | tf_op jit(solution)/shard_map/ppermute | solution.py:491
  39.6 1.1 %template_columns.5.images = f32[8,12,256,128]{3,2,1,0:T(8,128)S(1)} custom-call(bf16[8,6,256,128]{3,2,1,0:T(8,128)(2,1)S(1)} %get-tuple-element.58.rhi, bf16[8,6,256,128]{3,2,1,0:T(8,128)(2,1)S(1)} %get-tuple-element.59.rlo, bf16[3,3,2,256,256]{4,3,2,1,0:T(8,128)(2,1)S(1)} %get-tuple-element.55.wcol, ...), custom_call_target="tpu_custom_call", output_to_operand_aliasing={{}: (4, {})} | custom-call | flops 100000000 | bytes 1048576 | tf_op jit(solution)/shard_map/template_columns/pallas_call | solution.py:513
  40.8 1.3 %collective-permute-done.12 = f32[16,128]{1,0:T(8,128)S(1)} collective-permute-done((f32[16,128]{1,0:T(8,128)S(1)}, f32[16,128]{1,0:T(8,128)S(1)}, u32[]{:S(2)}, u32[]{:S(2)}) %collective-permute-start.12) | collective-permute-done | bytes 8224 | tf_op jit(solution)/shard_map/ppermute | solution.py:491
  42.0 1.9 %solve_subtract.1 = (f32[256,1024]{1,0:T(8,128)}, f32[12]{0:T(128)}) custom-call(f32[16,128]{1,0:T(8,128)S(1)} %add.17.system, f32[256,1024]{1,0:T(8,128)S(1)} %get-tuple-element.57.after.d0, f32[8,12,256,128]{3,2,1,0:T(8,128)S(1)} %template_columns.5.images), custom_call_target="tpu_custom_call" | custom-call | flops 100000000 | bytes 16777216 | tf_op jit(solution)/shard_map/solve_subtract/pallas_call | solution.py:665
  (27 shorter events, 5.1 us)
Async XLA Ops:
  0.6 1.7 %collective-permute-start = (f32[256,128]{1,0:T(8,128)}, f32[256,128]{1,0:T(8,128)S(1)}, u32[]{:S(2)}, u32[]{:S(2)}) collective-permute-start(f32[256,128]{1,0:T(8,128)} %param.10), channel_id=1, source_target_pairs={{0,1},{1,0},{2,3},{3,2},{4,5},{5,4},{6,7},{7,6},{8,9},{9,8},{10,11... | collective-permute-start | bytes 393224 | tf_op jit(solution)/shard_map/ppermute | solution.py:463
  2.3 6.9 %collective-permute-start.5 = (f32[272,128]{1,0:T(8,128)S(1)}, f32[272,128]{1,0:T(8,128)S(1)}, u32[]{:S(2)}, u32[]{:S(2)}) collective-permute-start(f32[272,128]{1,0:T(8,128)S(1)} %fusion.refs_0_), channel_id=1, source_target_pairs={{4,0},{8,4},{12,8},{14,12},{10,14},{6,10},{2,6},{0,2},{5,1},{9,5},... | collective-permute-start | bytes 417800 | tf_op jit(solution)/shard_map/ppermute | solution.py:474
  5.2 5.7 %collective-permute-start.1 = (f32[272,128]{1,0:T(8,128)S(1)}, f32[272,128]{1,0:T(8,128)S(1)}, u32[]{:S(2)}, u32[]{:S(2)}) collective-permute-start(f32[272,128]{1,0:T(8,128)S(1)} %fusion.refs_0_), channel_id=1, source_target_pairs={{0,4},{4,8},{8,12},{12,14},{14,10},{10,6},{6,2},{2,0},{1,5},{5,9},... | collective-permute-start | bytes 417800 | tf_op jit(solution)/shard_map/ppermute | solution.py:475
  6.2 5.1 %collective-permute-start.8 = (f32[16,1024]{1,0:T(8,128)S(1)}, f32[16,1024]{1,0:T(8,128)S(1)}, u32[]{:S(2)}, u32[]{:S(2)}) collective-permute-start(f32[16,1024]{1,0:T(8,128)S(1)} %slice_select_fusion), channel_id=1, source_target_pairs={{0,1},{1,0},{2,3},{3,2},{4,5},{5,4},{6,7},{7,6},{8,9},{9,8},{10,11... | collective-permute-start | bytes 196616 | tf_op jit(solution)/shard_map/ppermute | solution.py:463
  6.2 2.6 %copy-start = (s32[1,16]{1,0:T(1,128)S(1)}, s32[1,16]{1,0:T(1,128)}, u32[]{:S(2)}) copy-start(s32[1,16]{1,0:T(1,128)} %param.14) | copy-start | bytes 196
  6.3 2.6 %copy-start.1 = (s32[1,16]{1,0:T(1,128)S(1)}, s32[1,16]{1,0:T(1,128)}, u32[]{:S(2)}) copy-start(s32[1,16]{1,0:T(1,128)} %param.13) | copy-start | bytes 196
  9.3 8.5 %collective-permute-start.6 = (f32[272,128]{1,0:T(8,128)S(1)}, f32[272,128]{1,0:T(8,128)S(1)}, u32[]{:S(2)}, u32[]{:S(2)}) collective-permute-start(f32[272,128]{1,0:T(8,128)S(1)} %collective-permute-done.5.refs_1_), channel_id=1, source_target_pairs={{4,0},{8,4},{12,8},{14,12},{10,14},{6,10},{2,6},{0,2},{5,1},{9,5},... | collective-permute-start | bytes 417800 | tf_op jit(solution)/shard_map/ppermute | solution.py:474
  11.0 5.7 %collective-permute-start.2 = (f32[272,128]{1,0:T(8,128)S(1)}, f32[272,128]{1,0:T(8,128)S(1)}, u32[]{:S(2)}, u32[]{:S(2)}) collective-permute-start(f32[272,128]{1,0:T(8,128)S(1)} %collective-permute-done.1.after.refs_0_), channel_id=1, source_target_pairs={{0,4},{4,8},{8,12},{12,14},{14,10},{10,6},{6,2},{2,0},{1,5},{5,9},... | collective-permute-start | bytes 417800 | tf_op jit(solution)/shard_map/ppermute | solution.py:475
  16.7 5.1 %collective-permute-start.3 = (f32[272,128]{1,0:T(8,128)S(1)}, f32[272,128]{1,0:T(8,128)S(1)}, u32[]{:S(2)}, u32[]{:S(2)}) collective-permute-start(f32[272,128]{1,0:T(8,128)S(1)} %collective-permute-done.2.refs_0_.after), channel_id=1, source_target_pairs={{0,4},{4,8},{8,12},{12,14},{14,10},{10,6},{6,2},{2,0},{1,5},{5,9},... | collective-permute-start | bytes 417800 | tf_op jit(solution)/shard_map/ppermute | solution.py:475
  17.8 5.1 %collective-permute-start.7 = (f32[272,128]{1,0:T(8,128)S(1)}, f32[272,128]{1,0:T(8,128)S(1)}, u32[]{:S(2)}, u32[]{:S(2)}) collective-permute-start(f32[272,128]{1,0:T(8,128)S(1)} %collective-permute-done.6.refs_1_), channel_id=1, source_target_pairs={{4,0},{8,4},{12,8},{14,12},{10,14},{6,10},{2,6},{0,2},{5,1},{9,5},... | collective-permute-start | bytes 417800 | tf_op jit(solution)/shard_map/ppermute | solution.py:474
  21.7 5.1 %collective-permute-start.4 = (f32[272,128]{1,0:T(8,128)S(1)}, f32[272,128]{1,0:T(8,128)S(1)}, u32[]{:S(2)}, u32[]{:S(2)}) collective-permute-start(f32[272,128]{1,0:T(8,128)S(1)} %collective-permute-done.3.refs_0_), channel_id=1, source_target_pairs={{0,4},{4,8},{8,12},{12,14},{14,10},{10,6},{6,2},{2,0},{1,5},{5,9},... | collective-permute-start | bytes 417800 | tf_op jit(solution)/shard_map/ppermute | solution.py:475
  29.0 1.2 %collective-permute-start.9 = (f32[16,128]{1,0:T(8,128)S(1)}, f32[16,128]{1,0:T(8,128)S(1)}, u32[]{:S(2)}, u32[]{:S(2)}) collective-permute-start(f32[16,128]{1,0:T(8,128)S(1)} %get-tuple-element.56), channel_id=1, source_target_pairs={{0,1},{1,0},{2,3},{3,2},{4,5},{5,4},{6,7},{7,6},{8,9},{9,8},{10,11... | collective-permute-start | bytes 24584 | tf_op jit(solution)/shard_map/ppermute | solution.py:463
  30.2 3.7 %collective-permute-start.10 = (f32[16,128]{1,0:T(8,128)S(1)}, f32[16,128]{1,0:T(8,128)S(1)}, u32[]{:S(2)}, u32[]{:S(2)}) collective-permute-start(f32[16,128]{1,0:T(8,128)S(1)} %add.14.after), channel_id=1, source_target_pairs={{0,2},{2,0},{4,6},{6,4},{8,10},{10,8},{12,14},{14,12},{1,3},{3,1},... | collective-permute-start | bytes 24584 | tf_op jit(solution)/shard_map/ppermute | solution.py:491
  33.8 3.7 %collective-permute-start.11 = (f32[16,128]{1,0:T(8,128)S(1)}, f32[16,128]{1,0:T(8,128)S(1)}, u32[]{:S(2)}, u32[]{:S(2)}) collective-permute-start(f32[16,128]{1,0:T(8,128)S(1)} %add.15.after), channel_id=1, source_target_pairs={{0,4},{2,6},{4,0},{6,2},{8,12},{10,14},{12,8},{14,10},{1,5},{3,7},... | collective-permute-start | bytes 24584 | tf_op jit(solution)/shard_map/ppermute | solution.py:491
  37.5 4.5 %collective-permute-start.12 = (f32[16,128]{1,0:T(8,128)S(1)}, f32[16,128]{1,0:T(8,128)S(1)}, u32[]{:S(2)}, u32[]{:S(2)}) collective-permute-start(f32[16,128]{1,0:T(8,128)S(1)} %add.16), channel_id=1, source_target_pairs={{0,8},{2,10},{4,12},{6,14},{8,0},{10,2},{12,4},{14,6},{1,9},{3,11}... | collective-permute-start | bytes 24584 | tf_op jit(solution)/shard_map/ppermute | solution.py:491

commit v4 on v3

--- a/solution.py
+++ b/solution.py
@@ -247,9 +247,11 @@
         copy.wait()
 
 
-def cut_kernel(info, sb, fb, after, wp, sp):
+def cut_kernel(info, sb, fb, after, wp, sp, places):
     stamps = info.shape[0] // 2
     nblk = sb.shape[0]
+    for i in range(2 * stamps):
+        places[i] = info[i]
     lane = lane_index((STAMP, LANES))
     for g in range(stamps // 4):
         w = jnp.zeros((STAMP, LANES), F32)
@@ -480,15 +482,22 @@
 def all_sum(x, count, beside):
     beside[0](x)
     x = x + swap(x)
-    if count & (count - 1):
+    if count & (count - 1) or count < 4:
         for f in beside[1:]:
             f(x)
         return lax.psum(x, "epoch")
-    steps = count.bit_length() - 1
-    for i in range(steps):
-        for f in beside[1 + i :: steps]:
-            f(x)
-        x = x + lax.ppermute(x, "epoch", [(j, j ^ (1 << i)) for j in range(count)])
+
+    def other(bits):
+        return lax.ppermute(x, "epoch", [(j, j ^ bits) for j in range(count)])
+
+    beside[1](x)
+    x = (x + other(1)) + (other(2) + other(3))
+    bit = 4
+    for f in beside[2:]:
+        f(x)
+    while bit < count:
+        x = x + other(bit)
+        bit *= 2
     return x
 
 
@@ -514,7 +523,7 @@
         kernel,
         out_shape=out,
         in_specs=[spec(i, x) for i, x in enumerate(ins)],
-        out_specs=jax.tree.map(lambda _: VMEM(), out, is_leaf=lambda x: hasattr(x, "shape")),
+        out_specs=jax.tree.map(lambda x: SMEM() if len(x.shape) == 1 else VMEM(), out, is_leaf=lambda x: hasattr(x, "shape")),
         scratch_shapes=scratch,
         input_output_aliases=aliases or {},
         compiler_params=pltpu.CompilerParams(vmem_limit_bytes=limit * 2**20),
@@ -587,15 +596,17 @@
         outside=(4,),
         hbm=range(5, 5 + len(later_tables)),
     ))
-    wp, sp = map(in_vmem, call(
+    wp, sp, info = call(
         cut_kernel,
         "stamp_pixels",
-        (pltpu.VMEM((depth, LANES), F32),) * 2,
+        (pltpu.VMEM((depth, LANES), F32),) * 2 + (pltpu.SMEM(info.shape, info.dtype),),
         [info, sci, bad, blocks[3]],
         4,
         10**9,
         outside=(3,),
-    ))
+    )
+    wp, sp = in_vmem(wp), in_vmem(sp)
+    info = pltpu.with_memory_space_constraint(info, pltpu.SMEM)
 
     def row_filters(slots, r, store):
         ins = [lrow6, blocks[1] if store else d0] + [blocks[slot] for slot in slots]

time: 44.4 us -> 43.2 us (0.973)
  waiting for transfers between devices: 11.3 us -> 9.36 us
  starting transfers between devices: 12.9 us -> 14.1 us
  Pallas kernels: 17.2 us -> 16.7 us
    ppermute x3 -> x4, waiting for transfers between devices: 4.17 us -> 2.88 us  [other(): return lax.ppermute(x, 'epoch', [(j, j ^ bits) for j in range(count)])]
    ppermute x3 -> x4, starting transfers between devices: 4.85 us -> 6.08 us  [other(): return lax.ppermute(x, 'epoch', [(j, j ^ bits) for j in range(count)])]
    ppermute x3, waiting for transfers between devices: 1.44 us -> 0.85 us  [swap(): return lax.ppermute(x, 'tile', [(0, 1), (1, 0)])]
    pallas_call x12, Pallas kernels: 15.2 us -> 14.7 us  [call(): pl.pallas_call(kernel, out_shape=out, in_specs=[spec(i, x) for i, x in en...]
  transfers between devices with their start and end apart: 13 -> 14, of which waited for: 10 -> 10; matrix products, arithmetic and copies ran while one was open for 4% -> 4% of each run, Pallas kernels for 29% -> 30%
where the time goes in v4:
time: 43.2 us; the launch traced here: 43 us
  Pallas kernels  16.7 us (39%)
  starting transfers between devices  14.1 us (33%)
  waiting for transfers between devices  9.36 us (22%)
  other arithmetic  0.97 us (2%)
  between operations  0.95 us (2%)
  local copies, waits for them, and re-layouts  0.93 us (2%)
    pallas_call x12, Pallas kernels, call(): pl.pallas_call(kernel, out_shape=out, in_specs=[spec(i, x) for i, x in en...  14.7 us
    ppermute x3, starting transfers between devices, gather_ring(): bwd = lax.ppermute(bwd, 'epoch', back)  6.25 us
    ppermute x4, starting transfers between devices, other(): return lax.ppermute(x, 'epoch', [(j, j ^ bits) for j in range(count)])  6.08 us
    ppermute x4, waiting for transfers between devices, gather_ring(): fwd = lax.ppermute(fwd, 'epoch', ahead)  5.23 us
    ppermute x4, waiting for transfers between devices, other(): return lax.ppermute(x, 'epoch', [(j, j ^ bits) for j in range(count)])  2.88 us
    pallas_call x1, Pallas kernels, local(): pl.pallas_call(final_kernel, out_shape=(jax.ShapeDtypeStruct((rows, cols)...  1.95 us
    ppermute x4, starting transfers between devices, gather_ring(): fwd = lax.ppermute(fwd, 'epoch', ahead)  1.19 us
    pad x1, local copies, waits for them, and re-layouts, local(): tall = lax.optimization_barrier(jnp.pad(template, ((0, HALO), (0, 0))))  0.91 us
  transfers between devices with their start and end apart: 14, of which 10 were waited for; matrix products, arithmetic and copies ran while one was open for 4% of the time, Pallas kernels for 30%

profile of v4, /device:TPU:0, one launch (start us, length us, event | category | flops | bytes accessed | tf_op | source)
XLA Modules:
  0.0 43.0 jit_solution(17851865151849305172)
XLA Ops:
  1.1 0.9 %pad.4 = f32[272,128]{1,0:T(8,128)S(1)} pad(f32[256,128]{1,0:T(8,128)} %param.10, f32[]{:T(128)} %constant.7.clone.1), padding=0_16x0_0 | pad | bytes 270340 | tf_op jit(solution)/shard_map/jit(_pad)/pad | solution.py:553
  2.3 2.9 %collective-permute-start.5 = (f32[272,128]{1,0:T(8,128)S(1)}, f32[272,128]{1,0:T(8,128)S(1)}, u32[]{:S(2)}, u32[]{:S(2)}) collective-permute-start(f32[272,128]{1,0:T(8,128)S(1)} %fusion.refs_0_), channel_id=1, source_target_pairs={{4,0},{8,4},{12,8},{14,12},{10,14},{6,10},{2,6},{0,2},{5,1},{9,5},... | collective-permute-start | bytes 417800 | tf_op jit(solution)/shard_map/ppermute | solution.py:476
  5.3 0.9 %slice_select_fusion = f32[16,1024]{1,0:T(8,128)S(1)} fusion(f32[256,1024]{1,0:T(8,128)} %bitcast.5, pred[]{:T(512)S(6)} %eq.4), kind=kLoop, calls=%fused_computation | loop fusion | flops 16384 | bytes 196609 | tf_op jit(solution)/shard_map/jit(_where)/select_n | solution.py:550
  6.3 2.5 %load.1 = (f32[8,256,128]{2,1,0:T(8,128)S(1)}, s32[8,256,128]{2,1,0:T(8,128)S(1)}, bf16[2,768,480]{2,1,0:T(8,128)(2,1)S(1)}, bf16[3,128,480]{2,1,0:T(8,128)(2,1)S(1)}, bf16[3,2,256,128]{3,2,1,0:T(8,128)(2,1)S(1)}) custom-call(f32[272,128]{1,0:T(8,128)S(1)} %fusion.refs_0_, f32[256,1024]{1,0:T(8,128)} %bitcast.6, s32[256,1024]{1,0:T(8,128)} %bitcast.7, ...), custom_call_target="tpu_custom_call" | custom-call | flops 2000000000 | bytes 1048576 | tf_op jit(solution)/shard_map/load/pallas_call | solution.py:522
  9.3 1.7 %collective-permute-start.6 = (f32[272,128]{1,0:T(8,128)S(1)}, f32[272,128]{1,0:T(8,128)S(1)}, u32[]{:S(2)}, u32[]{:S(2)}) collective-permute-start(f32[272,128]{1,0:T(8,128)S(1)} %collective-permute-done.5.refs_1_), channel_id=1, source_target_pairs={{4,0},{8,4},{12,8},{14,12},{10,14},{6,10},{2,6},{0,2},{5,1},{9,5},... | collective-permute-start | bytes 417800 | tf_op jit(solution)/shard_map/ppermute | solution.py:476
  11.3 2.1 %science_filter.1 = (f32[256,1024]{1,0:T(8,128)S(1)}, bf16[3,3,2,256,256]{4,3,2,1,0:T(8,128)(2,1)S(1)}, bf16[2,256,768]{2,1,0:T(8,128)(2,1)S(1)}) custom-call(f32[8,256,128]{2,1,0:T(8,128)S(1)} %get-tuple-element.35.sb.sci, f32[16,1024]{1,0:T(8,128)S(1)} %collective-permute-done.8.edge, bf16[3,128,480]{2,1,0:T(8,128)(2,1)S(1)} %get-tuple-element.52.lrow, ...), custom_call_target="tpu_custom_call" | custom-call | flops 2000000000 | bytes 1048576 | tf_op jit(solution)/shard_map/science_filter/pallas_call | solution.py:522
  13.9 2.7 %collective-permute-done.2.after.refs_0_ = f32[272,128]{1,0:T(8,128)S(1)} collective-permute-done((f32[272,128]{1,0:T(8,128)S(1)}, f32[272,128]{1,0:T(8,128)S(1)}, u32[]{:S(2)}, u32[]{:S(2)}) %collective-permute-start.2) | collective-permute-done | bytes 139296 | tf_op jit(solution)/shard_map/ppermute | solution.py:477
  17.1 0.7 %template_rows.6 = (bf16[8,6,256,128]{3,2,1,0:T(8,128)(2,1)S(1)}, bf16[8,6,256,128]{3,2,1,0:T(8,128)(2,1)S(1)}, f32[10,288,128]{2,1,0:T(8,128)S(1)}) custom-call(bf16[2,768,480]{2,1,0:T(8,128)(2,1)S(1)} %get-tuple-element.38.lrow, f32[272,128]{1,0:T(8,128)S(1)} %collective-permute-done.1.after.refs_0_, ...), custom_call_target="tpu_custom_call", output_to_operand_aliasing={{0}: (4, {}), {1}: (5, {}), {2}: (6, {})} | custom-call | flops 1000000000 | bytes 1048576 | tf_op jit(solution)/shard_map/template_rows/pallas_call | solution.py:522
  17.8 1.7 %collective-permute-start.7 = (f32[272,128]{1,0:T(8,128)S(1)}, f32[272,128]{1,0:T(8,128)S(1)}, u32[]{:S(2)}, u32[]{:S(2)}) collective-permute-start(f32[272,128]{1,0:T(8,128)S(1)} %collective-permute-done.6.refs_1_), channel_id=1, source_target_pairs={{4,0},{8,4},{12,8},{14,12},{10,14},{6,10},{2,6},{0,2},{5,1},{9,5},... | collective-permute-start | bytes 417800 | tf_op jit(solution)/shard_map/ppermute | solution.py:476
  19.5 0.9 %stamp_pixels.1 = (f32[128,128]{1,0:T(8,128)S(1)}, f32[128,128]{1,0:T(8,128)S(1)}, s32[32]{0:T(128)S(4)}) custom-call(s32[32]{0:T(128)S(1)} %pad_add_fusion.info, f32[8,256,128]{2,1,0:T(8,128)S(1)} %get-tuple-element.35.sb.sci, s32[8,256,128]{2,1,0:T(8,128)S(1)} %get-tuple-element.36.fb, f32[272,128]{1,0:T(8,128)S(1)} %collective-permute-done.2.after.refs_0_), custom_call_target="tpu_custom_call" | custom-call | flops 1000000000 | bytes 1048576 | tf_op jit(solution)/shard_map/stamp_pixels/pallas_call | solution.py:522
  20.4 1.4 %collective-permute-done.3.refs_0_ = f32[272,128]{1,0:T(8,128)S(1)} collective-permute-done((f32[272,128]{1,0:T(8,128)S(1)}, f32[272,128]{1,0:T(8,128)S(1)}, u32[]{:S(2)}, u32[]{:S(2)}) %collective-permute-start.3) | collective-permute-done | bytes 139296 | tf_op jit(solution)/shard_map/ppermute | solution.py:477
  22.1 0.7 %template_rows.7 = (bf16[8,6,256,128]{3,2,1,0:T(8,128)(2,1)S(1)}, bf16[8,6,256,128]{3,2,1,0:T(8,128)(2,1)S(1)}, f32[10,288,128]{2,1,0:T(8,128)S(1)}) custom-call(bf16[2,768,480]{2,1,0:T(8,128)(2,1)S(1)} %get-tuple-element.38.lrow, f32[272,128]{1,0:T(8,128)S(1)} %collective-permute-done.1.after.refs_0_, ...), custom_call_target="tpu_custom_call", output_to_operand_aliasing={{0}: (4, {}), {1}: (5, {}), {2}: (6, {})} | custom-call | flops 1000000000 | bytes 1048576 | tf_op jit(solution)/shard_map/template_rows/pallas_call | solution.py:522
  22.9 0.7 %template_rows.8 = (bf16[8,6,256,128]{3,2,1,0:T(8,128)(2,1)S(1)}, bf16[8,6,256,128]{3,2,1,0:T(8,128)(2,1)S(1)}, f32[10,288,128]{2,1,0:T(8,128)S(1)}) custom-call(bf16[2,768,480]{2,1,0:T(8,128)(2,1)S(1)} %get-tuple-element.38.lrow, f32[272,128]{1,0:T(8,128)S(1)} %collective-permute-done.1.after.refs_0_, ...), custom_call_target="tpu_custom_call", output_to_operand_aliasing={{0}: (4, {}), {1}: (5, {}), {2}: (6, {})} | custom-call | flops 1000000000 | bytes 1048576 | tf_op jit(solution)/shard_map/template_rows/pallas_call | solution.py:522
  23.6 2.1 %template_columns.3.after.refs_0_ = f32[8,12,256,128]{3,2,1,0:T(8,128)S(1)} custom-call(bf16[8,6,256,128]{3,2,1,0:T(8,128)(2,1)S(1)} %get-tuple-element.55.rhi.refs_1_, bf16[8,6,256,128]{3,2,1,0:T(8,128)(2,1)S(1)} %get-tuple-element.56.rlo.refs_2_, bf16[3,3,2,256,256]{4,3,2,1,0:T(8,128)(2,1)S(1)} %get-tuple-element.57.wcol, ...), custom_call_target="tpu_custom_call" | custom-call | flops 200000000 | bytes 1048576 | tf_op jit(solution)/shard_map/template_columns/pallas_call | solution.py:522
  25.7 1.1 %collective-permute-done.4.last.refs_0_ = f32[272,128]{1,0:T(8,128)S(1)} collective-permute-done((f32[272,128]{1,0:T(8,128)S(1)}, f32[272,128]{1,0:T(8,128)S(1)}, u32[]{:S(2)}, u32[]{:S(2)}) %collective-permute-start.4) | collective-permute-done | bytes 139296 | tf_op jit(solution)/shard_map/ppermute | solution.py:477
  26.8 1.7 %stamp_sums.1 = (f32[16,128]{1,0:T(8,128)S(1)}, f32[10,288,128]{2,1,0:T(8,128)S(1)}) custom-call(s32[32]{0:T(128)S(4)} %get-tuple-element.37.info, f32[272,128]{1,0:T(8,128)S(1)} %collective-permute-done.4.last.refs_0_, f32[10,288,128]{2,1,0:T(8,128)S(1)} %get-tuple-element.48.t_in, ...), custom_call_target="tpu_custom_call", output_to_operand_aliasing={{1}: (2, {})} | custom-call | flops 1000000000 | bytes 1048576 | tf_op jit(solution)/shard_map/stamp_sums/pallas_call | solution.py:522
  28.5 0.6 %template_rows.9 = (bf16[8,6,256,128]{3,2,1,0:T(8,128)(2,1)S(1)}, bf16[8,6,256,128]{3,2,1,0:T(8,128)(2,1)S(1)}) custom-call(bf16[2,768,480]{2,1,0:T(8,128)(2,1)S(1)} %get-tuple-element.38.lrow, f32[256,1024]{1,0:T(8,128)S(1)} %get-tuple-element.59.after.d0, ...), custom_call_target="tpu_custom_call", output_to_operand_aliasing={{0}: (3, {}), {1}: (4, {})} | custom-call | flops 1000000000 | bytes 1048576 | tf_op jit(solution)/shard_map/template_rows/pallas_call | solution.py:522
  29.6 2.6 %collective-permute-start.12 = (f32[16,128]{1,0:T(8,128)S(1)}, f32[16,128]{1,0:T(8,128)S(1)}, u32[]{:S(2)}, u32[]{:S(2)}) collective-permute-start(f32[16,128]{1,0:T(8,128)S(1)} %add.17.after), channel_id=1, source_target_pairs={{0,6},{2,4},{4,2},{6,0},{8,14},{10,12},{12,10},{14,8},{1,7},{3,5},... | collective-permute-start | bytes 24584 | tf_op jit(solution)/shard_map/ppermute | solution.py:491
  33.1 1.1 %template_columns.4.refs_0_ = f32[8,12,256,128]{3,2,1,0:T(8,128)S(1)} custom-call(bf16[8,6,256,128]{3,2,1,0:T(8,128)(2,1)S(1)} %get-tuple-element.60.rhi, bf16[8,6,256,128]{3,2,1,0:T(8,128)(2,1)S(1)} %get-tuple-element.61.rlo, bf16[3,3,2,256,256]{4,3,2,1,0:T(8,128)(2,1)S(1)} %get-tuple-element.57.wcol, ...), custom_call_target="tpu_custom_call", output_to_operand_aliasing={{}: (4, {})} | custom-call | flops 100000000 | bytes 1048576 | tf_op jit(solution)/shard_map/template_columns/pallas_call | solution.py:522
  34.3 1.6 %collective-permute-done.11 = f32[16,128]{1,0:T(8,128)S(1)} collective-permute-done((f32[16,128]{1,0:T(8,128)S(1)}, f32[16,128]{1,0:T(8,128)S(1)}, u32[]{:S(2)}, u32[]{:S(2)}) %collective-permute-start.11) | collective-permute-done | bytes 8224 | tf_op jit(solution)/shard_map/ppermute | solution.py:491
  36.3 2.6 %collective-permute-start.13 = (f32[16,128]{1,0:T(8,128)S(1)}, f32[16,128]{1,0:T(8,128)S(1)}, u32[]{:S(2)}, u32[]{:S(2)}) collective-permute-start(f32[16,128]{1,0:T(8,128)S(1)} %add_add_fusion.after), channel_id=1, source_target_pairs={{0,8},{2,10},{4,12},{6,14},{8,0},{10,2},{12,4},{14,6},{1,9},{3,11}... | collective-permute-start | bytes 24584 | tf_op jit(solution)/shard_map/ppermute | solution.py:491
  38.9 1.1 %template_columns.5.images = f32[8,12,256,128]{3,2,1,0:T(8,128)S(1)} custom-call(bf16[8,6,256,128]{3,2,1,0:T(8,128)(2,1)S(1)} %get-tuple-element.60.rhi, bf16[8,6,256,128]{3,2,1,0:T(8,128)(2,1)S(1)} %get-tuple-element.61.rlo, bf16[3,3,2,256,256]{4,3,2,1,0:T(8,128)(2,1)S(1)} %get-tuple-element.57.wcol, ...), custom_call_target="tpu_custom_call", output_to_operand_aliasing={{}: (4, {})} | custom-call | flops 100000000 | bytes 1048576 | tf_op jit(solution)/shard_map/template_columns/pallas_call | solution.py:522
  40.1 0.8 %collective-permute-done.13 = f32[16,128]{1,0:T(8,128)S(1)} collective-permute-done((f32[16,128]{1,0:T(8,128)S(1)}, f32[16,128]{1,0:T(8,128)S(1)}, u32[]{:S(2)}, u32[]{:S(2)}) %collective-permute-start.13) | collective-permute-done | bytes 8224 | tf_op jit(solution)/shard_map/ppermute | solution.py:491
  40.9 1.9 %solve_subtract.1 = (f32[256,1024]{1,0:T(8,128)}, f32[12]{0:T(128)}) custom-call(f32[16,128]{1,0:T(8,128)S(1)} %add.21.system, f32[256,1024]{1,0:T(8,128)S(1)} %get-tuple-element.59.after.d0, f32[8,12,256,128]{3,2,1,0:T(8,128)S(1)} %template_columns.5.images), custom_call_target="tpu_custom_call" | custom-call | flops 100000000 | bytes 16777216 | tf_op jit(solution)/shard_map/solve_subtract/pallas_call | solution.py:676
  (28 shorter events, 5.1 us)
Async XLA Ops:
  0.6 1.7 %collective-permute-start = (f32[256,128]{1,0:T(8,128)}, f32[256,128]{1,0:T(8,128)S(1)}, u32[]{:S(2)}, u32[]{:S(2)}) collective-permute-start(f32[256,128]{1,0:T(8,128)} %param.10), channel_id=1, source_target_pairs={{0,1},{1,0},{2,3},{3,2},{4,5},{5,4},{6,7},{7,6},{8,9},{9,8},{10,11... | collective-permute-start | bytes 393224 | tf_op jit(solution)/shard_map/ppermute | solution.py:465
  2.3 6.9 %collective-permute-start.5 = (f32[272,128]{1,0:T(8,128)S(1)}, f32[272,128]{1,0:T(8,128)S(1)}, u32[]{:S(2)}, u32[]{:S(2)}) collective-permute-start(f32[272,128]{1,0:T(8,128)S(1)} %fusion.refs_0_), channel_id=1, source_target_pairs={{4,0},{8,4},{12,8},{14,12},{10,14},{6,10},{2,6},{0,2},{5,1},{9,5},... | collective-permute-start | bytes 417800 | tf_op jit(solution)/shard_map/ppermute | solution.py:476
  5.2 5.7 %collective-permute-start.1 = (f32[272,128]{1,0:T(8,128)S(1)}, f32[272,128]{1,0:T(8,128)S(1)}, u32[]{:S(2)}, u32[]{:S(2)}) collective-permute-start(f32[272,128]{1,0:T(8,128)S(1)} %fusion.refs_0_), channel_id=1, source_target_pairs={{0,4},{4,8},{8,12},{12,14},{14,10},{10,6},{6,2},{2,0},{1,5},{5,9},... | collective-permute-start | bytes 417800 | tf_op jit(solution)/shard_map/ppermute | solution.py:477
  6.2 5.1 %collective-permute-start.8 = (f32[16,1024]{1,0:T(8,128)S(1)}, f32[16,1024]{1,0:T(8,128)S(1)}, u32[]{:S(2)}, u32[]{:S(2)}) collective-permute-start(f32[16,1024]{1,0:T(8,128)S(1)} %slice_select_fusion), channel_id=1, source_target_pairs={{0,1},{1,0},{2,3},{3,2},{4,5},{5,4},{6,7},{7,6},{8,9},{9,8},{10,11... | collective-permute-start | bytes 196616 | tf_op jit(solution)/shard_map/ppermute | solution.py:465
  6.2 2.6 %copy-start = (s32[1,16]{1,0:T(1,128)S(1)}, s32[1,16]{1,0:T(1,128)}, u32[]{:S(2)}) copy-start(s32[1,16]{1,0:T(1,128)} %param.14) | copy-start | bytes 196
  6.3 2.6 %copy-start.1 = (s32[1,16]{1,0:T(1,128)S(1)}, s32[1,16]{1,0:T(1,128)}, u32[]{:S(2)}) copy-start(s32[1,16]{1,0:T(1,128)} %param.13) | copy-start | bytes 196
  9.3 8.5 %collective-permute-start.6 = (f32[272,128]{1,0:T(8,128)S(1)}, f32[272,128]{1,0:T(8,128)S(1)}, u32[]{:S(2)}, u32[]{:S(2)}) collective-permute-start(f32[272,128]{1,0:T(8,128)S(1)} %collective-permute-done.5.refs_1_), channel_id=1, source_target_pairs={{4,0},{8,4},{12,8},{14,12},{10,14},{6,10},{2,6},{0,2},{5,1},{9,5},... | collective-permute-start | bytes 417800 | tf_op jit(solution)/shard_map/ppermute | solution.py:476
  11.0 5.7 %collective-permute-start.2 = (f32[272,128]{1,0:T(8,128)S(1)}, f32[272,128]{1,0:T(8,128)S(1)}, u32[]{:S(2)}, u32[]{:S(2)}) collective-permute-start(f32[272,128]{1,0:T(8,128)S(1)} %collective-permute-done.1.after.refs_0_), channel_id=1, source_target_pairs={{0,4},{4,8},{8,12},{12,14},{14,10},{10,6},{6,2},{2,0},{1,5},{5,9},... | collective-permute-start | bytes 417800 | tf_op jit(solution)/shard_map/ppermute | solution.py:477
  16.7 5.1 %collective-permute-start.3 = (f32[272,128]{1,0:T(8,128)S(1)}, f32[272,128]{1,0:T(8,128)S(1)}, u32[]{:S(2)}, u32[]{:S(2)}) collective-permute-start(f32[272,128]{1,0:T(8,128)S(1)} %collective-permute-done.2.after.refs_0_), channel_id=1, source_target_pairs={{0,4},{4,8},{8,12},{12,14},{14,10},{10,6},{6,2},{2,0},{1,5},{5,9},... | collective-permute-start | bytes 417800 | tf_op jit(solution)/shard_map/ppermute | solution.py:477
  17.8 5.1 %collective-permute-start.7 = (f32[272,128]{1,0:T(8,128)S(1)}, f32[272,128]{1,0:T(8,128)S(1)}, u32[]{:S(2)}, u32[]{:S(2)}) collective-permute-start(f32[272,128]{1,0:T(8,128)S(1)} %collective-permute-done.6.refs_1_), channel_id=1, source_target_pairs={{4,0},{8,4},{12,8},{14,12},{10,14},{6,10},{2,6},{0,2},{5,1},{9,5},... | collective-permute-start | bytes 417800 | tf_op jit(solution)/shard_map/ppermute | solution.py:476
  21.7 5.1 %collective-permute-start.4 = (f32[272,128]{1,0:T(8,128)S(1)}, f32[272,128]{1,0:T(8,128)S(1)}, u32[]{:S(2)}, u32[]{:S(2)}) collective-permute-start(f32[272,128]{1,0:T(8,128)S(1)} %collective-permute-done.3.refs_0_), channel_id=1, source_target_pairs={{0,4},{4,8},{8,12},{12,14},{14,10},{10,6},{6,2},{2,0},{1,5},{5,9},... | collective-permute-start | bytes 417800 | tf_op jit(solution)/shard_map/ppermute | solution.py:477
  28.5 1.2 %collective-permute-start.9 = (f32[16,128]{1,0:T(8,128)S(1)}, f32[16,128]{1,0:T(8,128)S(1)}, u32[]{:S(2)}, u32[]{:S(2)}) collective-permute-start(f32[16,128]{1,0:T(8,128)S(1)} %get-tuple-element.58), channel_id=1, source_target_pairs={{0,1},{1,0},{2,3},{3,2},{4,5},{5,4},{6,7},{7,6},{8,9},{9,8},{10,11... | collective-permute-start | bytes 24584 | tf_op jit(solution)/shard_map/ppermute | solution.py:465
  29.6 4.6 %collective-permute-start.12 = (f32[16,128]{1,0:T(8,128)S(1)}, f32[16,128]{1,0:T(8,128)S(1)}, u32[]{:S(2)}, u32[]{:S(2)}) collective-permute-start(f32[16,128]{1,0:T(8,128)S(1)} %add.17.after), channel_id=1, source_target_pairs={{0,6},{2,4},{4,2},{6,0},{8,14},{10,12},{12,10},{14,8},{1,7},{3,5},... | collective-permute-start | bytes 24584 | tf_op jit(solution)/shard_map/ppermute | solution.py:491
  32.2 3.7 %collective-permute-start.11 = (f32[16,128]{1,0:T(8,128)S(1)}, f32[16,128]{1,0:T(8,128)S(1)}, u32[]{:S(2)}, u32[]{:S(2)}) collective-permute-start(f32[16,128]{1,0:T(8,128)S(1)} %add.17.after), channel_id=1, source_target_pairs={{0,4},{2,6},{4,0},{6,2},{8,12},{10,14},{12,8},{14,10},{1,5},{3,7},... | collective-permute-start | bytes 24584 | tf_op jit(solution)/shard_map/ppermute | solution.py:491
  32.7 3.7 %collective-permute-start.10 = (f32[16,128]{1,0:T(8,128)S(1)}, f32[16,128]{1,0:T(8,128)S(1)}, u32[]{:S(2)}, u32[]{:S(2)}) collective-permute-start(f32[16,128]{1,0:T(8,128)S(1)} %add.17.after), channel_id=1, source_target_pairs={{0,2},{2,0},{4,6},{6,4},{8,10},{10,8},{12,14},{14,12},{1,3},{3,1},... | collective-permute-start | bytes 24584 | tf_op jit(solution)/shard_map/ppermute | solution.py:491
  36.3 4.5 %collective-permute-start.13 = (f32[16,128]{1,0:T(8,128)S(1)}, f32[16,128]{1,0:T(8,128)S(1)}, u32[]{:S(2)}, u32[]{:S(2)}) collective-permute-start(f32[16,128]{1,0:T(8,128)S(1)} %add_add_fusion.after), channel_id=1, source_target_pairs={{0,8},{2,10},{4,12},{6,14},{8,0},{10,2},{12,4},{14,6},{1,9},{3,11}... | collective-permute-start | bytes 24584 | tf_op jit(solution)/shard_map/ppermute | solution.py:491

commit v5 on v4

--- a/solution.py
+++ b/solution.py
@@ -168,7 +168,7 @@
     if not ring:
         return jnp.int32(slot)
     step = (slot + 1) // 2
-    return ring_place(step if slot % 2 == 0 else -step, nblk)
+    return ring_place(-step if slot % 2 == 0 else step, nblk)
 
 
 def place_block(place, nblk, ring):
@@ -467,7 +467,7 @@
 
 def gather_ring(block, count):
     ring = ring_order(count)
-    ahead = [(ring[i], ring[(i + 1) % count]) for i in range(count)]
+    ahead = [(ring[i], ring[(i - 1) % count]) for i in range(count)]
     back = [(t, s) for s, t in ahead]
     out = [block]
     fwd = bwd = block

time: 43.2 us -> 42.2 us (0.977)
  waiting for transfers between devices: 9.36 us -> 8.45 us
    ppermute x4, waiting for transfers between devices: 2.88 us -> 1.79 us  [other(): return lax.ppermute(x, 'epoch', [(j, j ^ bits) for j in range(count)])]
  transfers between devices with their start and end apart: 14 -> 14, of which waited for: 10 -> 10; matrix products, arithmetic and copies ran while one was open for 4% -> 4% of each run, Pallas kernels for 30% -> 31%
where the time goes in v5:
time: 42.2 us; the launch traced here: 42 us
  Pallas kernels  16.7 us (40%)
  starting transfers between devices  14 us (33%)
  waiting for transfers between devices  8.45 us (20%)
  other arithmetic  0.97 us (2%)
  between operations  0.95 us (2%)
  local copies, waits for them, and re-layouts  0.93 us (2%)
    pallas_call x12, Pallas kernels, call(): pl.pallas_call(kernel, out_shape=out, in_specs=[spec(i, x) for i, x in en...  14.7 us
    ppermute x3, starting transfers between devices, gather_ring(): bwd = lax.ppermute(bwd, 'epoch', back)  6.52 us
    ppermute x4, starting transfers between devices, other(): return lax.ppermute(x, 'epoch', [(j, j ^ bits) for j in range(count)])  6.07 us
    ppermute x4, waiting for transfers between devices, gather_ring(): fwd = lax.ppermute(fwd, 'epoch', ahead)  5.45 us
    pallas_call x1, Pallas kernels, local(): pl.pallas_call(final_kernel, out_shape=(jax.ShapeDtypeStruct((rows, cols)...  1.95 us
    ppermute x4, waiting for transfers between devices, other(): return lax.ppermute(x, 'epoch', [(j, j ^ bits) for j in range(count)])  1.79 us
    pad x1, local copies, waits for them, and re-layouts, local(): tall = lax.optimization_barrier(jnp.pad(template, ((0, HALO), (0, 0))))  0.91 us
    select_n x1, other arithmetic, edge_of(): return jnp.where(tile == 0, x[-HALO:], x[:HALO])  0.88 us
  transfers between devices with their start and end apart: 14, of which 10 were waited for; matrix products, arithmetic and copies ran while one was open for 4% of the time, Pallas kernels for 31%

profile of v5, /device:TPU:0, one launch (start us, length us, event | category | flops | bytes accessed | tf_op | source)
XLA Modules:
  0.0 42.0 jit_solution(4793840262381881930)
XLA Ops:
  1.1 0.9 %pad.4 = f32[272,128]{1,0:T(8,128)S(1)} pad(f32[256,128]{1,0:T(8,128)} %param.10, f32[]{:T(128)} %constant.7.clone.1), padding=0_16x0_0 | pad | bytes 270340 | tf_op jit(solution)/shard_map/jit(_pad)/pad | solution.py:553
  2.3 2.9 %collective-permute-start.5 = (f32[272,128]{1,0:T(8,128)S(1)}, f32[272,128]{1,0:T(8,128)S(1)}, u32[]{:S(2)}, u32[]{:S(2)}) collective-permute-start(f32[272,128]{1,0:T(8,128)S(1)} %fusion.refs_0_), channel_id=1, source_target_pairs={{2,0},{0,4},{4,8},{8,12},{12,14},{14,10},{10,6},{6,2},{3,1},{1,5},... | collective-permute-start | bytes 417800 | tf_op jit(solution)/shard_map/ppermute | solution.py:476
  5.3 0.9 %slice_select_fusion = f32[16,1024]{1,0:T(8,128)S(1)} fusion(f32[256,1024]{1,0:T(8,128)} %bitcast.5, pred[]{:T(512)S(6)} %eq.4), kind=kLoop, calls=%fused_computation | loop fusion | flops 16384 | bytes 196609 | tf_op jit(solution)/shard_map/jit(_where)/select_n | solution.py:550
  6.3 2.5 %load.1 = (f32[8,256,128]{2,1,0:T(8,128)S(1)}, s32[8,256,128]{2,1,0:T(8,128)S(1)}, bf16[2,768,480]{2,1,0:T(8,128)(2,1)S(1)}, bf16[3,128,480]{2,1,0:T(8,128)(2,1)S(1)}, bf16[3,2,256,128]{3,2,1,0:T(8,128)(2,1)S(1)}) custom-call(f32[272,128]{1,0:T(8,128)S(1)} %fusion.refs_0_, f32[256,1024]{1,0:T(8,128)} %bitcast.6, s32[256,1024]{1,0:T(8,128)} %bitcast.7, ...), custom_call_target="tpu_custom_call" | custom-call | flops 2000000000 | bytes 1048576 | tf_op jit(solution)/shard_map/load/pallas_call | solution.py:522
  9.2 1.8 %collective-permute-start.6 = (f32[272,128]{1,0:T(8,128)S(1)}, f32[272,128]{1,0:T(8,128)S(1)}, u32[]{:S(2)}, u32[]{:S(2)}) collective-permute-start(f32[272,128]{1,0:T(8,128)S(1)} %collective-permute-done.5.refs_1_), channel_id=1, source_target_pairs={{2,0},{0,4},{4,8},{8,12},{12,14},{14,10},{10,6},{6,2},{3,1},{1,5},... | collective-permute-start | bytes 417800 | tf_op jit(solution)/shard_map/ppermute | solution.py:476
  11.2 2.1 %science_filter.1 = (f32[256,1024]{1,0:T(8,128)S(1)}, bf16[3,3,2,256,256]{4,3,2,1,0:T(8,128)(2,1)S(1)}, bf16[2,256,768]{2,1,0:T(8,128)(2,1)S(1)}) custom-call(f32[8,256,128]{2,1,0:T(8,128)S(1)} %get-tuple-element.35.sb.sci, f32[16,1024]{1,0:T(8,128)S(1)} %collective-permute-done.8.edge, bf16[3,128,480]{2,1,0:T(8,128)(2,1)S(1)} %get-tuple-element.52.lrow, ...), custom_call_target="tpu_custom_call" | custom-call | flops 2000000000 | bytes 1048576 | tf_op jit(solution)/shard_map/science_filter/pallas_call | solution.py:522
  13.9 2.9 %collective-permute-done.2.after.refs_0_ = f32[272,128]{1,0:T(8,128)S(1)} collective-permute-done((f32[272,128]{1,0:T(8,128)S(1)}, f32[272,128]{1,0:T(8,128)S(1)}, u32[]{:S(2)}, u32[]{:S(2)}) %collective-permute-start.2) | collective-permute-done | bytes 139296 | tf_op jit(solution)/shard_map/ppermute | solution.py:477
  17.0 0.7 %template_rows.6 = (bf16[8,6,256,128]{3,2,1,0:T(8,128)(2,1)S(1)}, bf16[8,6,256,128]{3,2,1,0:T(8,128)(2,1)S(1)}, f32[10,288,128]{2,1,0:T(8,128)S(1)}) custom-call(bf16[2,768,480]{2,1,0:T(8,128)(2,1)S(1)} %get-tuple-element.38.lrow, f32[272,128]{1,0:T(8,128)S(1)} %collective-permute-done.1.after.refs_0_, ...), custom_call_target="tpu_custom_call", output_to_operand_aliasing={{0}: (4, {}), {1}: (5, {}), {2}: (6, {})} | custom-call | flops 1000000000 | bytes 1048576 | tf_op jit(solution)/shard_map/template_rows/pallas_call | solution.py:522
  17.7 1.8 %collective-permute-start.7 = (f32[272,128]{1,0:T(8,128)S(1)}, f32[272,128]{1,0:T(8,128)S(1)}, u32[]{:S(2)}, u32[]{:S(2)}) collective-permute-start(f32[272,128]{1,0:T(8,128)S(1)} %collective-permute-done.6.refs_1_), channel_id=1, source_target_pairs={{2,0},{0,4},{4,8},{8,12},{12,14},{14,10},{10,6},{6,2},{3,1},{1,5},... | collective-permute-start | bytes 417800 | tf_op jit(solution)/shard_map/ppermute | solution.py:476
  19.5 0.9 %stamp_pixels.1 = (f32[128,128]{1,0:T(8,128)S(1)}, f32[128,128]{1,0:T(8,128)S(1)}, s32[32]{0:T(128)S(4)}) custom-call(s32[32]{0:T(128)S(1)} %pad_add_fusion.info, f32[8,256,128]{2,1,0:T(8,128)S(1)} %get-tuple-element.35.sb.sci, s32[8,256,128]{2,1,0:T(8,128)S(1)} %get-tuple-element.36.fb, f32[272,128]{1,0:T(8,128)S(1)} %collective-permute-done.2.after.refs_0_), custom_call_target="tpu_custom_call" | custom-call | flops 1000000000 | bytes 1048576 | tf_op jit(solution)/shard_map/stamp_pixels/pallas_call | solution.py:522
  20.4 1.4 %collective-permute-done.3.refs_0_ = f32[272,128]{1,0:T(8,128)S(1)} collective-permute-done((f32[272,128]{1,0:T(8,128)S(1)}, f32[272,128]{1,0:T(8,128)S(1)}, u32[]{:S(2)}, u32[]{:S(2)}) %collective-permute-start.3) | collective-permute-done | bytes 139296 | tf_op jit(solution)/shard_map/ppermute | solution.py:477
  22.1 0.7 %template_rows.7 = (bf16[8,6,256,128]{3,2,1,0:T(8,128)(2,1)S(1)}, bf16[8,6,256,128]{3,2,1,0:T(8,128)(2,1)S(1)}, f32[10,288,128]{2,1,0:T(8,128)S(1)}) custom-call(bf16[2,768,480]{2,1,0:T(8,128)(2,1)S(1)} %get-tuple-element.38.lrow, f32[272,128]{1,0:T(8,128)S(1)} %collective-permute-done.1.after.refs_0_, ...), custom_call_target="tpu_custom_call", output_to_operand_aliasing={{0}: (4, {}), {1}: (5, {}), {2}: (6, {})} | custom-call | flops 1000000000 | bytes 1048576 | tf_op jit(solution)/shard_map/template_rows/pallas_call | solution.py:522
  22.8 0.7 %template_rows.8 = (bf16[8,6,256,128]{3,2,1,0:T(8,128)(2,1)S(1)}, bf16[8,6,256,128]{3,2,1,0:T(8,128)(2,1)S(1)}, f32[10,288,128]{2,1,0:T(8,128)S(1)}) custom-call(bf16[2,768,480]{2,1,0:T(8,128)(2,1)S(1)} %get-tuple-element.38.lrow, f32[272,128]{1,0:T(8,128)S(1)} %collective-permute-done.1.after.refs_0_, ...), custom_call_target="tpu_custom_call", output_to_operand_aliasing={{0}: (4, {}), {1}: (5, {}), {2}: (6, {})} | custom-call | flops 1000000000 | bytes 1048576 | tf_op jit(solution)/shard_map/template_rows/pallas_call | solution.py:522
  23.5 2.1 %template_columns.3.after.refs_0_ = f32[8,12,256,128]{3,2,1,0:T(8,128)S(1)} custom-call(bf16[8,6,256,128]{3,2,1,0:T(8,128)(2,1)S(1)} %get-tuple-element.55.rhi.refs_1_, bf16[8,6,256,128]{3,2,1,0:T(8,128)(2,1)S(1)} %get-tuple-element.56.rlo.refs_2_, bf16[3,3,2,256,256]{4,3,2,1,0:T(8,128)(2,1)S(1)} %get-tuple-element.57.wcol, ...), custom_call_target="tpu_custom_call" | custom-call | flops 200000000 | bytes 1048576 | tf_op jit(solution)/shard_map/template_columns/pallas_call | solution.py:522
  25.7 1.2 %collective-permute-done.4.last.refs_0_ = f32[272,128]{1,0:T(8,128)S(1)} collective-permute-done((f32[272,128]{1,0:T(8,128)S(1)}, f32[272,128]{1,0:T(8,128)S(1)}, u32[]{:S(2)}, u32[]{:S(2)}) %collective-permute-start.4) | collective-permute-done | bytes 139296 | tf_op jit(solution)/shard_map/ppermute | solution.py:477
  26.9 1.7 %stamp_sums.1 = (f32[16,128]{1,0:T(8,128)S(1)}, f32[10,288,128]{2,1,0:T(8,128)S(1)}) custom-call(s32[32]{0:T(128)S(4)} %get-tuple-element.37.info, f32[272,128]{1,0:T(8,128)S(1)} %collective-permute-done.4.last.refs_0_, f32[10,288,128]{2,1,0:T(8,128)S(1)} %get-tuple-element.48.t_in, ...), custom_call_target="tpu_custom_call", output_to_operand_aliasing={{1}: (2, {})} | custom-call | flops 1000000000 | bytes 1048576 | tf_op jit(solution)/shard_map/stamp_sums/pallas_call | solution.py:522
  28.5 0.6 %template_rows.9 = (bf16[8,6,256,128]{3,2,1,0:T(8,128)(2,1)S(1)}, bf16[8,6,256,128]{3,2,1,0:T(8,128)(2,1)S(1)}) custom-call(bf16[2,768,480]{2,1,0:T(8,128)(2,1)S(1)} %get-tuple-element.38.lrow, f32[256,1024]{1,0:T(8,128)S(1)} %get-tuple-element.59.after.d0, ...), custom_call_target="tpu_custom_call", output_to_operand_aliasing={{0}: (3, {}), {1}: (4, {})} | custom-call | flops 1000000000 | bytes 1048576 | tf_op jit(solution)/shard_map/template_rows/pallas_call | solution.py:522
  29.7 1.5 %collective-permute-start.12 = (f32[16,128]{1,0:T(8,128)S(1)}, f32[16,128]{1,0:T(8,128)S(1)}, u32[]{:S(2)}, u32[]{:S(2)}) collective-permute-start(f32[16,128]{1,0:T(8,128)S(1)} %add.17.after), channel_id=1, source_target_pairs={{0,6},{2,4},{4,2},{6,0},{8,14},{10,12},{12,10},{14,8},{1,7},{3,5},... | collective-permute-start | bytes 24584 | tf_op jit(solution)/shard_map/ppermute | solution.py:491
  31.7 1.5 %collective-permute-start.10 = (f32[16,128]{1,0:T(8,128)S(1)}, f32[16,128]{1,0:T(8,128)S(1)}, u32[]{:S(2)}, u32[]{:S(2)}) collective-permute-start(f32[16,128]{1,0:T(8,128)S(1)} %add.17.after), channel_id=1, source_target_pairs={{0,2},{2,0},{4,6},{6,4},{8,10},{10,8},{12,14},{14,12},{1,3},{3,1},... | collective-permute-start | bytes 24584 | tf_op jit(solution)/shard_map/ppermute | solution.py:491
  33.2 1.1 %template_columns.4.refs_0_ = f32[8,12,256,128]{3,2,1,0:T(8,128)S(1)} custom-call(bf16[8,6,256,128]{3,2,1,0:T(8,128)(2,1)S(1)} %get-tuple-element.60.rhi, bf16[8,6,256,128]{3,2,1,0:T(8,128)(2,1)S(1)} %get-tuple-element.61.rlo, bf16[3,3,2,256,256]{4,3,2,1,0:T(8,128)(2,1)S(1)} %get-tuple-element.57.wcol, ...), custom_call_target="tpu_custom_call", output_to_operand_aliasing={{}: (4, {})} | custom-call | flops 100000000 | bytes 1048576 | tf_op jit(solution)/shard_map/template_columns/pallas_call | solution.py:522
  35.3 2.6 %collective-permute-start.13 = (f32[16,128]{1,0:T(8,128)S(1)}, f32[16,128]{1,0:T(8,128)S(1)}, u32[]{:S(2)}, u32[]{:S(2)}) collective-permute-start(f32[16,128]{1,0:T(8,128)S(1)} %add_add_fusion.after), channel_id=1, source_target_pairs={{0,8},{2,10},{4,12},{6,14},{8,0},{10,2},{12,4},{14,6},{1,9},{3,11}... | collective-permute-start | bytes 24584 | tf_op jit(solution)/shard_map/ppermute | solution.py:491
  37.9 1.1 %template_columns.5.images = f32[8,12,256,128]{3,2,1,0:T(8,128)S(1)} custom-call(bf16[8,6,256,128]{3,2,1,0:T(8,128)(2,1)S(1)} %get-tuple-element.60.rhi, bf16[8,6,256,128]{3,2,1,0:T(8,128)(2,1)S(1)} %get-tuple-element.61.rlo, bf16[3,3,2,256,256]{4,3,2,1,0:T(8,128)(2,1)S(1)} %get-tuple-element.57.wcol, ...), custom_call_target="tpu_custom_call", output_to_operand_aliasing={{}: (4, {})} | custom-call | flops 100000000 | bytes 1048576 | tf_op jit(solution)/shard_map/template_columns/pallas_call | solution.py:522
  39.0 0.8 %collective-permute-done.13 = f32[16,128]{1,0:T(8,128)S(1)} collective-permute-done((f32[16,128]{1,0:T(8,128)S(1)}, f32[16,128]{1,0:T(8,128)S(1)}, u32[]{:S(2)}, u32[]{:S(2)}) %collective-permute-start.13) | collective-permute-done | bytes 8224 | tf_op jit(solution)/shard_map/ppermute | solution.py:491
  39.9 1.9 %solve_subtract.1 = (f32[256,1024]{1,0:T(8,128)}, f32[12]{0:T(128)}) custom-call(f32[16,128]{1,0:T(8,128)S(1)} %add.21.system, f32[256,1024]{1,0:T(8,128)S(1)} %get-tuple-element.59.after.d0, f32[8,12,256,128]{3,2,1,0:T(8,128)S(1)} %template_columns.5.images), custom_call_target="tpu_custom_call" | custom-call | flops 100000000 | bytes 16777216 | tf_op jit(solution)/shard_map/solve_subtract/pallas_call | solution.py:676
  (28 shorter events, 4.7 us)
Async XLA Ops:
  0.6 1.7 %collective-permute-start = (f32[256,128]{1,0:T(8,128)}, f32[256,128]{1,0:T(8,128)S(1)}, u32[]{:S(2)}, u32[]{:S(2)}) collective-permute-start(f32[256,128]{1,0:T(8,128)} %param.10), channel_id=1, source_target_pairs={{0,1},{1,0},{2,3},{3,2},{4,5},{5,4},{6,7},{7,6},{8,9},{9,8},{10,11... | collective-permute-start | bytes 393224 | tf_op jit(solution)/shard_map/ppermute | solution.py:465
  2.3 6.9 %collective-permute-start.5 = (f32[272,128]{1,0:T(8,128)S(1)}, f32[272,128]{1,0:T(8,128)S(1)}, u32[]{:S(2)}, u32[]{:S(2)}) collective-permute-start(f32[272,128]{1,0:T(8,128)S(1)} %fusion.refs_0_), channel_id=1, source_target_pairs={{2,0},{0,4},{4,8},{8,12},{12,14},{14,10},{10,6},{6,2},{3,1},{1,5},... | collective-permute-start | bytes 417800 | tf_op jit(solution)/shard_map/ppermute | solution.py:476
  5.3 5.7 %collective-permute-start.1 = (f32[272,128]{1,0:T(8,128)S(1)}, f32[272,128]{1,0:T(8,128)S(1)}, u32[]{:S(2)}, u32[]{:S(2)}) collective-permute-start(f32[272,128]{1,0:T(8,128)S(1)} %fusion.refs_0_), channel_id=1, source_target_pairs={{0,2},{4,0},{8,4},{12,8},{14,12},{10,14},{6,10},{2,6},{1,3},{5,1},... | collective-permute-start | bytes 417800 | tf_op jit(solution)/shard_map/ppermute | solution.py:477
  6.2 5.1 %collective-permute-start.8 = (f32[16,1024]{1,0:T(8,128)S(1)}, f32[16,1024]{1,0:T(8,128)S(1)}, u32[]{:S(2)}, u32[]{:S(2)}) collective-permute-start(f32[16,1024]{1,0:T(8,128)S(1)} %slice_select_fusion), channel_id=1, source_target_pairs={{0,1},{1,0},{2,3},{3,2},{4,5},{5,4},{6,7},{7,6},{8,9},{9,8},{10,11... | collective-permute-start | bytes 196616 | tf_op jit(solution)/shard_map/ppermute | solution.py:465
  6.2 2.6 %copy-start = (s32[1,16]{1,0:T(1,128)S(1)}, s32[1,16]{1,0:T(1,128)}, u32[]{:S(2)}) copy-start(s32[1,16]{1,0:T(1,128)} %param.14) | copy-start | bytes 196
  6.3 2.6 %copy-start.1 = (s32[1,16]{1,0:T(1,128)S(1)}, s32[1,16]{1,0:T(1,128)}, u32[]{:S(2)}) copy-start(s32[1,16]{1,0:T(1,128)} %param.13) | copy-start | bytes 196
  9.2 8.5 %collective-permute-start.6 = (f32[272,128]{1,0:T(8,128)S(1)}, f32[272,128]{1,0:T(8,128)S(1)}, u32[]{:S(2)}, u32[]{:S(2)}) collective-permute-start(f32[272,128]{1,0:T(8,128)S(1)} %collective-permute-done.5.refs_1_), channel_id=1, source_target_pairs={{2,0},{0,4},{4,8},{8,12},{12,14},{14,10},{10,6},{6,2},{3,1},{1,5},... | collective-permute-start | bytes 417800 | tf_op jit(solution)/shard_map/ppermute | solution.py:476
  11.0 5.7 %collective-permute-start.2 = (f32[272,128]{1,0:T(8,128)S(1)}, f32[272,128]{1,0:T(8,128)S(1)}, u32[]{:S(2)}, u32[]{:S(2)}) collective-permute-start(f32[272,128]{1,0:T(8,128)S(1)} %collective-permute-done.1.after.refs_0_), channel_id=1, source_target_pairs={{0,2},{4,0},{8,4},{12,8},{14,12},{10,14},{6,10},{2,6},{1,3},{5,1},... | collective-permute-start | bytes 417800 | tf_op jit(solution)/shard_map/ppermute | solution.py:477
  16.7 5.1 %collective-permute-start.3 = (f32[272,128]{1,0:T(8,128)S(1)}, f32[272,128]{1,0:T(8,128)S(1)}, u32[]{:S(2)}, u32[]{:S(2)}) collective-permute-start(f32[272,128]{1,0:T(8,128)S(1)} %collective-permute-done.2.after.refs_0_), channel_id=1, source_target_pairs={{0,2},{4,0},{8,4},{12,8},{14,12},{10,14},{6,10},{2,6},{1,3},{5,1},... | collective-permute-start | bytes 417800 | tf_op jit(solution)/shard_map/ppermute | solution.py:477
  17.7 5.1 %collective-permute-start.7 = (f32[272,128]{1,0:T(8,128)S(1)}, f32[272,128]{1,0:T(8,128)S(1)}, u32[]{:S(2)}, u32[]{:S(2)}) collective-permute-start(f32[272,128]{1,0:T(8,128)S(1)} %collective-permute-done.6.refs_1_), channel_id=1, source_target_pairs={{2,0},{0,4},{4,8},{8,12},{12,14},{14,10},{10,6},{6,2},{3,1},{1,5},... | collective-permute-start | bytes 417800 | tf_op jit(solution)/shard_map/ppermute | solution.py:476
  21.8 5.1 %collective-permute-start.4 = (f32[272,128]{1,0:T(8,128)S(1)}, f32[272,128]{1,0:T(8,128)S(1)}, u32[]{:S(2)}, u32[]{:S(2)}) collective-permute-start(f32[272,128]{1,0:T(8,128)S(1)} %collective-permute-done.3.refs_0_), channel_id=1, source_target_pairs={{0,2},{4,0},{8,4},{12,8},{14,12},{10,14},{6,10},{2,6},{1,3},{5,1},... | collective-permute-start | bytes 417800 | tf_op jit(solution)/shard_map/ppermute | solution.py:477
  28.5 1.2 %collective-permute-start.9 = (f32[16,128]{1,0:T(8,128)S(1)}, f32[16,128]{1,0:T(8,128)S(1)}, u32[]{:S(2)}, u32[]{:S(2)}) collective-permute-start(f32[16,128]{1,0:T(8,128)S(1)} %get-tuple-element.58), channel_id=1, source_target_pairs={{0,1},{1,0},{2,3},{3,2},{4,5},{5,4},{6,7},{7,6},{8,9},{9,8},{10,11... | collective-permute-start | bytes 24584 | tf_op jit(solution)/shard_map/ppermute | solution.py:465
  29.7 4.6 %collective-permute-start.12 = (f32[16,128]{1,0:T(8,128)S(1)}, f32[16,128]{1,0:T(8,128)S(1)}, u32[]{:S(2)}, u32[]{:S(2)}) collective-permute-start(f32[16,128]{1,0:T(8,128)S(1)} %add.17.after), channel_id=1, source_target_pairs={{0,6},{2,4},{4,2},{6,0},{8,14},{10,12},{12,10},{14,8},{1,7},{3,5},... | collective-permute-start | bytes 24584 | tf_op jit(solution)/shard_map/ppermute | solution.py:491
  31.2 3.7 %collective-permute-start.11 = (f32[16,128]{1,0:T(8,128)S(1)}, f32[16,128]{1,0:T(8,128)S(1)}, u32[]{:S(2)}, u32[]{:S(2)}) collective-permute-start(f32[16,128]{1,0:T(8,128)S(1)} %add.17.after), channel_id=1, source_target_pairs={{0,4},{2,6},{4,0},{6,2},{8,12},{10,14},{12,8},{14,10},{1,5},{3,7},... | collective-permute-start | bytes 24584 | tf_op jit(solution)/shard_map/ppermute | solution.py:491
  31.7 3.7 %collective-permute-start.10 = (f32[16,128]{1,0:T(8,128)S(1)}, f32[16,128]{1,0:T(8,128)S(1)}, u32[]{:S(2)}, u32[]{:S(2)}) collective-permute-start(f32[16,128]{1,0:T(8,128)S(1)} %add.17.after), channel_id=1, source_target_pairs={{0,2},{2,0},{4,6},{6,4},{8,10},{10,8},{12,14},{14,12},{1,3},{3,1},... | collective-permute-start | bytes 24584 | tf_op jit(solution)/shard_map/ppermute | solution.py:491
  35.3 4.5 %collective-permute-start.13 = (f32[16,128]{1,0:T(8,128)S(1)}, f32[16,128]{1,0:T(8,128)S(1)}, u32[]{:S(2)}, u32[]{:S(2)}) collective-permute-start(f32[16,128]{1,0:T(8,128)S(1)} %add_add_fusion.after), channel_id=1, source_target_pairs={{0,8},{2,10},{4,12},{6,14},{8,0},{10,2},{12,4},{14,6},{1,9},{3,11}... | collective-permute-start | bytes 24584 | tf_op jit(solution)/shard_map/ppermute | solution.py:491

commit v6 on v5

--- a/solution.py
+++ b/solution.py
@@ -490,14 +490,15 @@
     def other(bits):
         return lax.ppermute(x, "epoch", [(j, j ^ bits) for j in range(count)])
 
-    beside[1](x)
-    x = (x + other(1)) + (other(2) + other(3))
+    for f in beside[1:2]:
+        f(x)
     bit = 4
-    for f in beside[2:]:
-        f(x)
     while bit < count:
         x = x + other(bit)
         bit *= 2
+    for f in beside[2:]:
+        f(x)
+    x = (x + other(1)) + (other(2) + other(3))
     return x
 
 

time: 42.2 us -> 42.2 us (level)
  no operation moved by 1% of the time
where the time goes in v6:
time: 42.2 us; the launch traced here: 42 us
  Pallas kernels  16.7 us (40%)
  starting transfers between devices  14 us (33%)
  waiting for transfers between devices  8.45 us (20%)
  other arithmetic  0.97 us (2%)
  between operations  0.95 us (2%)
  local copies, waits for them, and re-layouts  0.93 us (2%)
    pallas_call x12, Pallas kernels, call(): pl.pallas_call(kernel, out_shape=out, in_specs=[spec(i, x) for i, x in en...  14.7 us
    ppermute x3, starting transfers between devices, gather_ring(): bwd = lax.ppermute(bwd, 'epoch', back)  6.52 us
    ppermute x4, starting transfers between devices, other(): return lax.ppermute(x, 'epoch', [(j, j ^ bits) for j in range(count)])  6.08 us
    ppermute x4, waiting for transfers between devices, gather_ring(): fwd = lax.ppermute(fwd, 'epoch', ahead)  5.45 us
    pallas_call x1, Pallas kernels, local(): pl.pallas_call(final_kernel, out_shape=(jax.ShapeDtypeStruct((rows, cols)...  1.95 us
    ppermute x4, waiting for transfers between devices, other(): return lax.ppermute(x, 'epoch', [(j, j ^ bits) for j in range(count)])  1.79 us
    pad x1, local copies, waits for them, and re-layouts, local(): tall = lax.optimization_barrier(jnp.pad(template, ((0, HALO), (0, 0))))  0.91 us
    select_n x1, other arithmetic, edge_of(): return jnp.where(tile == 0, x[-HALO:], x[:HALO])  0.88 us
  transfers between devices with their start and end apart: 14, of which 10 were waited for; matrix products, arithmetic and copies ran while one was open for 4% of the time, Pallas kernels for 31%

profile of v6, /device:TPU:0, one launch (start us, length us, event | category | flops | bytes accessed | tf_op | source)
XLA Modules:
  0.0 42.0 jit_solution(203640838696981215)
XLA Ops:
  1.1 0.9 %pad.4 = f32[272,128]{1,0:T(8,128)S(1)} pad(f32[256,128]{1,0:T(8,128)} %param.10, f32[]{:T(128)} %constant.7.clone.1), padding=0_16x0_0 | pad | bytes 270340 | tf_op jit(solution)/shard_map/jit(_pad)/pad | solution.py:554
  2.3 2.9 %collective-permute-start.5 = (f32[272,128]{1,0:T(8,128)S(1)}, f32[272,128]{1,0:T(8,128)S(1)}, u32[]{:S(2)}, u32[]{:S(2)}) collective-permute-start(f32[272,128]{1,0:T(8,128)S(1)} %fusion.refs_0_), channel_id=1, source_target_pairs={{2,0},{0,4},{4,8},{8,12},{12,14},{14,10},{10,6},{6,2},{3,1},{1,5},... | collective-permute-start | bytes 417800 | tf_op jit(solution)/shard_map/ppermute | solution.py:476
  5.3 0.9 %slice_select_fusion = f32[16,1024]{1,0:T(8,128)S(1)} fusion(f32[256,1024]{1,0:T(8,128)} %bitcast.5, pred[]{:T(512)S(6)} %eq.4), kind=kLoop, calls=%fused_computation | loop fusion | flops 16384 | bytes 196609 | tf_op jit(solution)/shard_map/jit(_where)/select_n | solution.py:551
  6.3 2.5 %load.1 = (f32[8,256,128]{2,1,0:T(8,128)S(1)}, s32[8,256,128]{2,1,0:T(8,128)S(1)}, bf16[2,768,480]{2,1,0:T(8,128)(2,1)S(1)}, bf16[3,128,480]{2,1,0:T(8,128)(2,1)S(1)}, bf16[3,2,256,128]{3,2,1,0:T(8,128)(2,1)S(1)}) custom-call(f32[272,128]{1,0:T(8,128)S(1)} %fusion.refs_0_, f32[256,1024]{1,0:T(8,128)} %bitcast.6, s32[256,1024]{1,0:T(8,128)} %bitcast.7, ...), custom_call_target="tpu_custom_call" | custom-call | flops 2000000000 | bytes 1048576 | tf_op jit(solution)/shard_map/load/pallas_call | solution.py:523
  9.2 1.8 %collective-permute-start.6 = (f32[272,128]{1,0:T(8,128)S(1)}, f32[272,128]{1,0:T(8,128)S(1)}, u32[]{:S(2)}, u32[]{:S(2)}) collective-permute-start(f32[272,128]{1,0:T(8,128)S(1)} %collective-permute-done.5.refs_1_), channel_id=1, source_target_pairs={{2,0},{0,4},{4,8},{8,12},{12,14},{14,10},{10,6},{6,2},{3,1},{1,5},... | collective-permute-start | bytes 417800 | tf_op jit(solution)/shard_map/ppermute | solution.py:476
  11.2 2.1 %science_filter.1 = (f32[256,1024]{1,0:T(8,128)S(1)}, bf16[3,3,2,256,256]{4,3,2,1,0:T(8,128)(2,1)S(1)}, bf16[2,256,768]{2,1,0:T(8,128)(2,1)S(1)}) custom-call(f32[8,256,128]{2,1,0:T(8,128)S(1)} %get-tuple-element.35.sb.sci, f32[16,1024]{1,0:T(8,128)S(1)} %collective-permute-done.8.edge, bf16[3,128,480]{2,1,0:T(8,128)(2,1)S(1)} %get-tuple-element.52.lrow, ...), custom_call_target="tpu_custom_call" | custom-call | flops 2000000000 | bytes 1048576 | tf_op jit(solution)/shard_map/science_filter/pallas_call | solution.py:523
  13.9 2.9 %collective-permute-done.2.after.refs_0_ = f32[272,128]{1,0:T(8,128)S(1)} collective-permute-done((f32[272,128]{1,0:T(8,128)S(1)}, f32[272,128]{1,0:T(8,128)S(1)}, u32[]{:S(2)}, u32[]{:S(2)}) %collective-permute-start.2) | collective-permute-done | bytes 139296 | tf_op jit(solution)/shard_map/ppermute | solution.py:477
  17.0 0.7 %template_rows.6 = (bf16[8,6,256,128]{3,2,1,0:T(8,128)(2,1)S(1)}, bf16[8,6,256,128]{3,2,1,0:T(8,128)(2,1)S(1)}, f32[10,288,128]{2,1,0:T(8,128)S(1)}) custom-call(bf16[2,768,480]{2,1,0:T(8,128)(2,1)S(1)} %get-tuple-element.38.lrow, f32[272,128]{1,0:T(8,128)S(1)} %collective-permute-done.1.after.refs_0_, ...), custom_call_target="tpu_custom_call", output_to_operand_aliasing={{0}: (4, {}), {1}: (5, {}), {2}: (6, {})} | custom-call | flops 1000000000 | bytes 1048576 | tf_op jit(solution)/shard_map/template_rows/pallas_call | solution.py:523
  17.7 1.8 %collective-permute-start.7 = (f32[272,128]{1,0:T(8,128)S(1)}, f32[272,128]{1,0:T(8,128)S(1)}, u32[]{:S(2)}, u32[]{:S(2)}) collective-permute-start(f32[272,128]{1,0:T(8,128)S(1)} %collective-permute-done.6.refs_1_), channel_id=1, source_target_pairs={{2,0},{0,4},{4,8},{8,12},{12,14},{14,10},{10,6},{6,2},{3,1},{1,5},... | collective-permute-start | bytes 417800 | tf_op jit(solution)/shard_map/ppermute | solution.py:476
  19.5 0.9 %stamp_pixels.1 = (f32[128,128]{1,0:T(8,128)S(1)}, f32[128,128]{1,0:T(8,128)S(1)}, s32[32]{0:T(128)S(4)}) custom-call(s32[32]{0:T(128)S(1)} %pad_add_fusion.info, f32[8,256,128]{2,1,0:T(8,128)S(1)} %get-tuple-element.35.sb.sci, s32[8,256,128]{2,1,0:T(8,128)S(1)} %get-tuple-element.36.fb, f32[272,128]{1,0:T(8,128)S(1)} %collective-permute-done.2.after.refs_0_), custom_call_target="tpu_custom_call" | custom-call | flops 1000000000 | bytes 1048576 | tf_op jit(solution)/shard_map/stamp_pixels/pallas_call | solution.py:523
  20.4 1.4 %collective-permute-done.3.refs_0_ = f32[272,128]{1,0:T(8,128)S(1)} collective-permute-done((f32[272,128]{1,0:T(8,128)S(1)}, f32[272,128]{1,0:T(8,128)S(1)}, u32[]{:S(2)}, u32[]{:S(2)}) %collective-permute-start.3) | collective-permute-done | bytes 139296 | tf_op jit(solution)/shard_map/ppermute | solution.py:477
  22.1 0.7 %template_rows.7 = (bf16[8,6,256,128]{3,2,1,0:T(8,128)(2,1)S(1)}, bf16[8,6,256,128]{3,2,1,0:T(8,128)(2,1)S(1)}, f32[10,288,128]{2,1,0:T(8,128)S(1)}) custom-call(bf16[2,768,480]{2,1,0:T(8,128)(2,1)S(1)} %get-tuple-element.38.lrow, f32[272,128]{1,0:T(8,128)S(1)} %collective-permute-done.1.after.refs_0_, ...), custom_call_target="tpu_custom_call", output_to_operand_aliasing={{0}: (4, {}), {1}: (5, {}), {2}: (6, {})} | custom-call | flops 1000000000 | bytes 1048576 | tf_op jit(solution)/shard_map/template_rows/pallas_call | solution.py:523
  22.8 0.7 %template_rows.8 = (bf16[8,6,256,128]{3,2,1,0:T(8,128)(2,1)S(1)}, bf16[8,6,256,128]{3,2,1,0:T(8,128)(2,1)S(1)}, f32[10,288,128]{2,1,0:T(8,128)S(1)}) custom-call(bf16[2,768,480]{2,1,0:T(8,128)(2,1)S(1)} %get-tuple-element.38.lrow, f32[272,128]{1,0:T(8,128)S(1)} %collective-permute-done.1.after.refs_0_, ...), custom_call_target="tpu_custom_call", output_to_operand_aliasing={{0}: (4, {}), {1}: (5, {}), {2}: (6, {})} | custom-call | flops 1000000000 | bytes 1048576 | tf_op jit(solution)/shard_map/template_rows/pallas_call | solution.py:523
  23.5 2.1 %template_columns.3.after.refs_0_ = f32[8,12,256,128]{3,2,1,0:T(8,128)S(1)} custom-call(bf16[8,6,256,128]{3,2,1,0:T(8,128)(2,1)S(1)} %get-tuple-element.55.rhi.refs_1_, bf16[8,6,256,128]{3,2,1,0:T(8,128)(2,1)S(1)} %get-tuple-element.56.rlo.refs_2_, bf16[3,3,2,256,256]{4,3,2,1,0:T(8,128)(2,1)S(1)} %get-tuple-element.57.wcol, ...), custom_call_target="tpu_custom_call" | custom-call | flops 200000000 | bytes 1048576 | tf_op jit(solution)/shard_map/template_columns/pallas_call | solution.py:523
  25.7 1.2 %collective-permute-done.4.last.refs_0_ = f32[272,128]{1,0:T(8,128)S(1)} collective-permute-done((f32[272,128]{1,0:T(8,128)S(1)}, f32[272,128]{1,0:T(8,128)S(1)}, u32[]{:S(2)}, u32[]{:S(2)}) %collective-permute-start.4) | collective-permute-done | bytes 139296 | tf_op jit(solution)/shard_map/ppermute | solution.py:477
  26.9 1.7 %stamp_sums.1 = (f32[16,128]{1,0:T(8,128)S(1)}, f32[10,288,128]{2,1,0:T(8,128)S(1)}) custom-call(s32[32]{0:T(128)S(4)} %get-tuple-element.37.info, f32[272,128]{1,0:T(8,128)S(1)} %collective-permute-done.4.last.refs_0_, f32[10,288,128]{2,1,0:T(8,128)S(1)} %get-tuple-element.48.t_in, ...), custom_call_target="tpu_custom_call", output_to_operand_aliasing={{1}: (2, {})} | custom-call | flops 1000000000 | bytes 1048576 | tf_op jit(solution)/shard_map/stamp_sums/pallas_call | solution.py:523
  28.5 0.6 %template_rows.9 = (bf16[8,6,256,128]{3,2,1,0:T(8,128)(2,1)S(1)}, bf16[8,6,256,128]{3,2,1,0:T(8,128)(2,1)S(1)}) custom-call(bf16[2,768,480]{2,1,0:T(8,128)(2,1)S(1)} %get-tuple-element.38.lrow, f32[256,1024]{1,0:T(8,128)S(1)} %get-tuple-element.59.after.d0, ...), custom_call_target="tpu_custom_call", output_to_operand_aliasing={{0}: (3, {}), {1}: (4, {})} | custom-call | flops 1000000000 | bytes 1048576 | tf_op jit(solution)/shard_map/template_rows/pallas_call | solution.py:523
  29.7 2.6 %collective-permute-start.10 = (f32[16,128]{1,0:T(8,128)S(1)}, f32[16,128]{1,0:T(8,128)S(1)}, u32[]{:S(2)}, u32[]{:S(2)}) collective-permute-start(f32[16,128]{1,0:T(8,128)S(1)} %add.17.after), channel_id=1, source_target_pairs={{0,8},{2,10},{4,12},{6,14},{8,0},{10,2},{12,4},{14,6},{1,9},{3,11}... | collective-permute-start | bytes 24584 | tf_op jit(solution)/shard_map/ppermute | solution.py:491
  32.3 1.1 %template_columns.4.refs_0_ = f32[8,12,256,128]{3,2,1,0:T(8,128)S(1)} custom-call(bf16[8,6,256,128]{3,2,1,0:T(8,128)(2,1)S(1)} %get-tuple-element.60.rhi, bf16[8,6,256,128]{3,2,1,0:T(8,128)(2,1)S(1)} %get-tuple-element.61.rlo, bf16[3,3,2,256,256]{4,3,2,1,0:T(8,128)(2,1)S(1)} %get-tuple-element.57.wcol, ...), custom_call_target="tpu_custom_call", output_to_operand_aliasing={{}: (4, {})} | custom-call | flops 100000000 | bytes 1048576 | tf_op jit(solution)/shard_map/template_columns/pallas_call | solution.py:523
  33.4 0.8 %collective-permute-done.10 = f32[16,128]{1,0:T(8,128)S(1)} collective-permute-done((f32[16,128]{1,0:T(8,128)S(1)}, f32[16,128]{1,0:T(8,128)S(1)}, u32[]{:S(2)}, u32[]{:S(2)}) %collective-permute-start.10) | collective-permute-done | bytes 8224 | tf_op jit(solution)/shard_map/ppermute | solution.py:491
  34.3 1.5 %collective-permute-start.13 = (f32[16,128]{1,0:T(8,128)S(1)}, f32[16,128]{1,0:T(8,128)S(1)}, u32[]{:S(2)}, u32[]{:S(2)}) collective-permute-start(f32[16,128]{1,0:T(8,128)S(1)} %add.18.after), channel_id=1, source_target_pairs={{0,6},{2,4},{4,2},{6,0},{8,14},{10,12},{12,10},{14,8},{1,7},{3,5},... | collective-permute-start | bytes 24584 | tf_op jit(solution)/shard_map/ppermute | solution.py:491
  36.2 1.5 %collective-permute-start.11 = (f32[16,128]{1,0:T(8,128)S(1)}, f32[16,128]{1,0:T(8,128)S(1)}, u32[]{:S(2)}, u32[]{:S(2)}) collective-permute-start(f32[16,128]{1,0:T(8,128)S(1)} %add.18.after), channel_id=1, source_target_pairs={{0,2},{2,0},{4,6},{6,4},{8,10},{10,8},{12,14},{14,12},{1,3},{3,1},... | collective-permute-start | bytes 24584 | tf_op jit(solution)/shard_map/ppermute | solution.py:491
  37.7 1.1 %template_columns.5.images = f32[8,12,256,128]{3,2,1,0:T(8,128)S(1)} custom-call(bf16[8,6,256,128]{3,2,1,0:T(8,128)(2,1)S(1)} %get-tuple-element.60.rhi, bf16[8,6,256,128]{3,2,1,0:T(8,128)(2,1)S(1)} %get-tuple-element.61.rlo, bf16[3,3,2,256,256]{4,3,2,1,0:T(8,128)(2,1)S(1)} %get-tuple-element.57.wcol, ...), custom_call_target="tpu_custom_call", output_to_operand_aliasing={{}: (4, {})} | custom-call | flops 100000000 | bytes 1048576 | tf_op jit(solution)/shard_map/template_columns/pallas_call | solution.py:523
  39.9 1.9 %solve_subtract.1 = (f32[256,1024]{1,0:T(8,128)}, f32[12]{0:T(128)}) custom-call(f32[16,128]{1,0:T(8,128)S(1)} %add_add_fusion.system, f32[256,1024]{1,0:T(8,128)S(1)} %get-tuple-element.59.after.d0, f32[8,12,256,128]{3,2,1,0:T(8,128)S(1)} %template_columns.5.images), custom_call_target="tpu_custom_call" | custom-call | flops 100000000 | bytes 16777216 | tf_op jit(solution)/shard_map/solve_subtract/pallas_call | solution.py:677
  (28 shorter events, 4.7 us)
Async XLA Ops:
  0.6 1.7 %collective-permute-start = (f32[256,128]{1,0:T(8,128)}, f32[256,128]{1,0:T(8,128)S(1)}, u32[]{:S(2)}, u32[]{:S(2)}) collective-permute-start(f32[256,128]{1,0:T(8,128)} %param.10), channel_id=1, source_target_pairs={{0,1},{1,0},{2,3},{3,2},{4,5},{5,4},{6,7},{7,6},{8,9},{9,8},{10,11... | collective-permute-start | bytes 393224 | tf_op jit(solution)/shard_map/ppermute | solution.py:465
  2.3 6.9 %collective-permute-start.5 = (f32[272,128]{1,0:T(8,128)S(1)}, f32[272,128]{1,0:T(8,128)S(1)}, u32[]{:S(2)}, u32[]{:S(2)}) collective-permute-start(f32[272,128]{1,0:T(8,128)S(1)} %fusion.refs_0_), channel_id=1, source_target_pairs={{2,0},{0,4},{4,8},{8,12},{12,14},{14,10},{10,6},{6,2},{3,1},{1,5},... | collective-permute-start | bytes 417800 | tf_op jit(solution)/shard_map/ppermute | solution.py:476
  5.3 5.7 %collective-permute-start.1 = (f32[272,128]{1,0:T(8,128)S(1)}, f32[272,128]{1,0:T(8,128)S(1)}, u32[]{:S(2)}, u32[]{:S(2)}) collective-permute-start(f32[272,128]{1,0:T(8,128)S(1)} %fusion.refs_0_), channel_id=1, source_target_pairs={{0,2},{4,0},{8,4},{12,8},{14,12},{10,14},{6,10},{2,6},{1,3},{5,1},... | collective-permute-start | bytes 417800 | tf_op jit(solution)/shard_map/ppermute | solution.py:477
  6.2 5.1 %collective-permute-start.8 = (f32[16,1024]{1,0:T(8,128)S(1)}, f32[16,1024]{1,0:T(8,128)S(1)}, u32[]{:S(2)}, u32[]{:S(2)}) collective-permute-start(f32[16,1024]{1,0:T(8,128)S(1)} %slice_select_fusion), channel_id=1, source_target_pairs={{0,1},{1,0},{2,3},{3,2},{4,5},{5,4},{6,7},{7,6},{8,9},{9,8},{10,11... | collective-permute-start | bytes 196616 | tf_op jit(solution)/shard_map/ppermute | solution.py:465
  6.2 2.6 %copy-start = (s32[1,16]{1,0:T(1,128)S(1)}, s32[1,16]{1,0:T(1,128)}, u32[]{:S(2)}) copy-start(s32[1,16]{1,0:T(1,128)} %param.14) | copy-start | bytes 196
  6.3 2.6 %copy-start.1 = (s32[1,16]{1,0:T(1,128)S(1)}, s32[1,16]{1,0:T(1,128)}, u32[]{:S(2)}) copy-start(s32[1,16]{1,0:T(1,128)} %param.13) | copy-start | bytes 196
  9.2 8.5 %collective-permute-start.6 = (f32[272,128]{1,0:T(8,128)S(1)}, f32[272,128]{1,0:T(8,128)S(1)}, u32[]{:S(2)}, u32[]{:S(2)}) collective-permute-start(f32[272,128]{1,0:T(8,128)S(1)} %collective-permute-done.5.refs_1_), channel_id=1, source_target_pairs={{2,0},{0,4},{4,8},{8,12},{12,14},{14,10},{10,6},{6,2},{3,1},{1,5},... | collective-permute-start | bytes 417800 | tf_op jit(solution)/shard_map/ppermute | solution.py:476
  11.0 5.7 %collective-permute-start.2 = (f32[272,128]{1,0:T(8,128)S(1)}, f32[272,128]{1,0:T(8,128)S(1)}, u32[]{:S(2)}, u32[]{:S(2)}) collective-permute-start(f32[272,128]{1,0:T(8,128)S(1)} %collective-permute-done.1.after.refs_0_), channel_id=1, source_target_pairs={{0,2},{4,0},{8,4},{12,8},{14,12},{10,14},{6,10},{2,6},{1,3},{5,1},... | collective-permute-start | bytes 417800 | tf_op jit(solution)/shard_map/ppermute | solution.py:477
  16.7 5.1 %collective-permute-start.3 = (f32[272,128]{1,0:T(8,128)S(1)}, f32[272,128]{1,0:T(8,128)S(1)}, u32[]{:S(2)}, u32[]{:S(2)}) collective-permute-start(f32[272,128]{1,0:T(8,128)S(1)} %collective-permute-done.2.after.refs_0_), channel_id=1, source_target_pairs={{0,2},{4,0},{8,4},{12,8},{14,12},{10,14},{6,10},{2,6},{1,3},{5,1},... | collective-permute-start | bytes 417800 | tf_op jit(solution)/shard_map/ppermute | solution.py:477
  17.7 5.1 %collective-permute-start.7 = (f32[272,128]{1,0:T(8,128)S(1)}, f32[272,128]{1,0:T(8,128)S(1)}, u32[]{:S(2)}, u32[]{:S(2)}) collective-permute-start(f32[272,128]{1,0:T(8,128)S(1)} %collective-permute-done.6.refs_1_), channel_id=1, source_target_pairs={{2,0},{0,4},{4,8},{8,12},{12,14},{14,10},{10,6},{6,2},{3,1},{1,5},... | collective-permute-start | bytes 417800 | tf_op jit(solution)/shard_map/ppermute | solution.py:476
  21.8 5.1 %collective-permute-start.4 = (f32[272,128]{1,0:T(8,128)S(1)}, f32[272,128]{1,0:T(8,128)S(1)}, u32[]{:S(2)}, u32[]{:S(2)}) collective-permute-start(f32[272,128]{1,0:T(8,128)S(1)} %collective-permute-done.3.refs_0_), channel_id=1, source_target_pairs={{0,2},{4,0},{8,4},{12,8},{14,12},{10,14},{6,10},{2,6},{1,3},{5,1},... | collective-permute-start | bytes 417800 | tf_op jit(solution)/shard_map/ppermute | solution.py:477
  28.5 1.2 %collective-permute-start.9 = (f32[16,128]{1,0:T(8,128)S(1)}, f32[16,128]{1,0:T(8,128)S(1)}, u32[]{:S(2)}, u32[]{:S(2)}) collective-permute-start(f32[16,128]{1,0:T(8,128)S(1)} %get-tuple-element.58), channel_id=1, source_target_pairs={{0,1},{1,0},{2,3},{3,2},{4,5},{5,4},{6,7},{7,6},{8,9},{9,8},{10,11... | collective-permute-start | bytes 24584 | tf_op jit(solution)/shard_map/ppermute | solution.py:465
  29.7 4.5 %collective-permute-start.10 = (f32[16,128]{1,0:T(8,128)S(1)}, f32[16,128]{1,0:T(8,128)S(1)}, u32[]{:S(2)}, u32[]{:S(2)}) collective-permute-start(f32[16,128]{1,0:T(8,128)S(1)} %add.17.after), channel_id=1, source_target_pairs={{0,8},{2,10},{4,12},{6,14},{8,0},{10,2},{12,4},{14,6},{1,9},{3,11}... | collective-permute-start | bytes 24584 | tf_op jit(solution)/shard_map/ppermute | solution.py:491
  34.3 4.6 %collective-permute-start.13 = (f32[16,128]{1,0:T(8,128)S(1)}, f32[16,128]{1,0:T(8,128)S(1)}, u32[]{:S(2)}, u32[]{:S(2)}) collective-permute-start(f32[16,128]{1,0:T(8,128)S(1)} %add.18.after), channel_id=1, source_target_pairs={{0,6},{2,4},{4,2},{6,0},{8,14},{10,12},{12,10},{14,8},{1,7},{3,5},... | collective-permute-start | bytes 24584 | tf_op jit(solution)/shard_map/ppermute | solution.py:491
  35.8 3.7 %collective-permute-start.12 = (f32[16,128]{1,0:T(8,128)S(1)}, f32[16,128]{1,0:T(8,128)S(1)}, u32[]{:S(2)}, u32[]{:S(2)}) collective-permute-start(f32[16,128]{1,0:T(8,128)S(1)} %add.18.after), channel_id=1, source_target_pairs={{0,4},{2,6},{4,0},{6,2},{8,12},{10,14},{12,8},{14,10},{1,5},{3,7},... | collective-permute-start | bytes 24584 | tf_op jit(solution)/shard_map/ppermute | solution.py:491
  36.2 3.7 %collective-permute-start.11 = (f32[16,128]{1,0:T(8,128)S(1)}, f32[16,128]{1,0:T(8,128)S(1)}, u32[]{:S(2)}, u32[]{:S(2)}) collective-permute-start(f32[16,128]{1,0:T(8,128)S(1)} %add.18.after), channel_id=1, source_target_pairs={{0,2},{2,0},{4,6},{6,4},{8,10},{10,8},{12,14},{14,12},{1,3},{3,1},... | collective-permute-start | bytes 24584 | tf_op jit(solution)/shard_map/ppermute | solution.py:491
